TPU v7x, 32 devices: a whole 2x2x4 slice. The times are simulated.
32 devices in a mesh: dp: 8 (over z, y), space: 4 (over x, core).
Axes of the slice: x: 2, y: 2, z: 4, core: 2. Of those that a mesh axis runs over, the one named last changes fastest.
Arguments:
- activations: bfloat16 [8, 64, 32, 48, 128], P('dp', None, 'space'), may hold values from -6 to 6
- cotangent: bfloat16 [8, 64, 32, 48, 128], P('dp', None, 'space'), may hold values from -6 to 6
- mode_weights: bfloat16 [2048, 64, 128], P(('space', 'dp')), may hold values from -6 to 6
- pointwise: bfloat16 [64, 64], replicated, may hold values from -0.75 to 0.75
- offsets: float32 [64], replicated, may hold values from -3 to 3
Outputs:
- grad_in: bfloat16 [8, 64, 32, 48, 128], P('dp', None, 'space')
- grad_spectral: float32 [2048, 64, 128], P(('space', 'dp'))
All inputs are finite; a program needn't handle non-finite values.
Results may differ from a plain program's by a relative error of at most 0.02.
Values may be sent and summed in bfloat16 or wider, within the bound.
No kernel may reach another device: no remote copies, remote signals or barrier semaphores. Data moves between devices by JAX's collectives and lax.ppermute only.
A program may use at most 128 MiB of HBM per device.

v0:
```python
import functools
import math

import jax
import jax.numpy as jnp
import ml_dtypes
import numpy as np
from jax import lax
from jax.experimental import pallas as pl
from jax.experimental.pallas import tpu as pltpu
from jax.sharding import PartitionSpec as P

MX = 16
MY = 16
MZ = 8
NX = 32


def centered(count):
    index = jnp.arange(count, dtype=jnp.int32)
    return jnp.where(index < count // 2, index, index - count)


def plane_tables(rows_y, rows_z, modes_y, modes_z):
    along_y = jnp.arange(rows_y, dtype=jnp.int32)[:, None, None, None]
    along_z = jnp.arange(rows_z, dtype=jnp.int32)[None, :, None, None]
    freq_y = centered(modes_y)[None, None, :, None]
    freq_z = jnp.arange(modes_z, dtype=jnp.int32)[None, None, None, :]
    phase = jnp.mod(freq_y * along_y * rows_z + freq_z * along_z * rows_y, rows_y * rows_z)
    theta = phase.astype(jnp.float32) * (2.0 * math.pi / (rows_y * rows_z))
    cosine = jnp.cos(theta)
    sine = jnp.sin(theta)
    forward = jnp.stack([cosine, -sine], -1).reshape(rows_y * rows_z, modes_y * modes_z * 2)
    scaled = jnp.where(freq_z == 0, 1.0, 2.0).astype(jnp.float32) / (rows_y * rows_z)
    inverse = (
        jnp.stack([cosine * scaled, -sine * scaled], -1)
        .reshape(rows_y * rows_z, modes_y * modes_z * 2)
        .T
    )
    return (forward.astype(jnp.bfloat16), inverse.astype(jnp.bfloat16))


def line_tables(length, modes):
    along = jnp.arange(length, dtype=jnp.int32)[:, None]
    freq = centered(modes)[None, :]
    phase = jnp.mod(freq * along, length)
    theta = phase.astype(jnp.float32) * (2.0 * math.pi / length)
    cosine = jnp.cos(theta)
    sine = jnp.sin(theta)
    first = jnp.stack([cosine, -sine], -1)
    second = jnp.stack([sine, cosine], -1)
    forward = jnp.stack([first, second], 1).reshape(2 * length, 2 * modes)
    inv_first = jnp.stack([cosine.T, sine.T], -1) / length
    inv_second = jnp.stack([-sine.T, cosine.T], -1) / length
    inverse = jnp.stack([inv_first, inv_second], 1).reshape(2 * modes, 2 * length)
    return (forward.astype(jnp.bfloat16), inverse.astype(jnp.bfloat16))


def expand_weights(weights):
    half = weights.shape[1]
    real_part = weights[:, :, :half]
    imag_part = weights[:, :, half:]
    upper = jnp.concatenate([real_part, imag_part], axis=2)
    lower = jnp.concatenate([-imag_part, real_part], axis=2)
    return jnp.concatenate([upper, lower], axis=1)


def outer_sum(left, right):
    return jnp.einsum("mbi,mbo->mio", left, right, preferred_element_type=jnp.float32)


def weight_terms(spec_in, spec_grad):
    half = spec_in.shape[2] // 2
    in_real = spec_in[:, :, :half]
    in_imag = spec_in[:, :, half:]
    gr_real = spec_grad[:, :, :half]
    gr_imag = spec_grad[:, :, half:]
    real_term = outer_sum(in_real, gr_real) + outer_sum(in_imag, gr_imag)
    imag_term = outer_sum(in_real, gr_imag) - outer_sum(in_imag, gr_real)
    return jnp.concatenate([real_term, imag_term], axis=2)


def to_modes(slab, table, modes_x):
    samples, channels, width, pairs = slab.shape
    moved = lax.all_to_all(slab, "space", split_axis=3, concat_axis=2, tiled=True)
    length = moved.shape[2]
    local = moved.shape[3] // 2
    lines = moved.reshape(samples, channels, length, local, 2).transpose(0, 1, 3, 2, 4)
    lines = lines.reshape(samples, channels, local, 2 * length)
    spectra = jnp.dot(lines, table, preferred_element_type=jnp.float32).astype(jnp.bfloat16)
    spectra = spectra.reshape(samples, channels, local, modes_x, 2).transpose(2, 3, 0, 4, 1)
    return spectra.reshape(local * modes_x, samples, 2 * channels)


def to_slab(spectra, table, modes_x, channels):
    count, samples, doubled = spectra.shape
    local = count // modes_x
    lines = spectra.reshape(local, modes_x, samples, 2, channels).transpose(2, 4, 0, 1, 3)
    lines = lines.reshape(samples, channels, local, 2 * modes_x)
    lines = jnp.dot(lines, table, preferred_element_type=jnp.float32).astype(jnp.bfloat16)
    length = lines.shape[3] // 2
    lines = lines.reshape(samples, channels, local, length, 2).transpose(0, 1, 3, 2, 4)
    lines = lines.reshape(samples, channels, length, 2 * local)
    return lax.all_to_all(lines, "space", split_axis=2, concat_axis=3, tiled=True)


def to_owners(spectra):
    return lax.all_to_all(spectra, "dp", split_axis=0, concat_axis=1, tiled=True)


def from_owners(spectra):
    return lax.all_to_all(spectra, "dp", split_axis=1, concat_axis=0, tiled=True)


def gelu_slope(value):
    cdf = 0.5 * (1.0 + lax.erf(value * 0.7071067811865476))
    density = jnp.exp(-0.5 * value * value) * 0.3989422804014327
    return cdf + value * density


def general_body(activations, cotangent, mode_weights, pointwise, offsets):
    samples, channels, width, rows_y, rows_z = activations.shape
    plane_fwd, plane_inv = plane_tables(rows_y, rows_z, MY, MZ)
    line_fwd, line_inv = line_tables(NX, MX)
    flat = activations.reshape(samples, channels, width, rows_y * rows_z)
    planes = jnp.dot(flat, plane_fwd, preferred_element_type=jnp.float32).astype(jnp.bfloat16)
    spec_in = to_modes(planes, line_fwd, MX)
    blocks = expand_weights(mode_weights)
    held_in = to_owners(spec_in)
    held_out = jnp.einsum(
        "mbi,mio->mbo", held_in, blocks, preferred_element_type=jnp.float32
    ).astype(jnp.bfloat16)
    spec_out = from_owners(held_out)
    returned = to_slab(spec_out, line_inv, MX, channels)
    spectral = jnp.dot(returned, plane_inv, preferred_element_type=jnp.float32)
    local_part = jnp.einsum("io,bixn->boxn", pointwise, flat, preferred_element_type=jnp.float32)
    summed = spectral + local_part + offsets[None, :, None, None]
    upstream = cotangent.reshape(flat.shape).astype(jnp.float32)
    slope_grad = (upstream * gelu_slope(summed)).astype(jnp.bfloat16)
    back_plane = jnp.dot(slope_grad, plane_inv.T, preferred_element_type=jnp.float32).astype(
        jnp.bfloat16
    )
    spec_grad = to_modes(back_plane, line_inv.T, MX)
    held_grad = to_owners(spec_grad)
    held_dx = jnp.einsum(
        "mbo,mio->mbi", held_grad, blocks, preferred_element_type=jnp.float32
    ).astype(jnp.bfloat16)
    spec_dx = from_owners(held_dx)
    grad_spectral = weight_terms(held_in, held_grad)
    line_dx = to_slab(spec_dx, line_fwd.T, MX, channels)
    total = jnp.dot(line_dx, plane_fwd.T, preferred_element_type=jnp.float32)
    total = total + jnp.einsum(
        "io,boxn->bixn", pointwise, slope_grad, preferred_element_type=jnp.float32
    )
    grad_in = total.astype(jnp.bfloat16).reshape(activations.shape)
    return (grad_in, grad_spectral)


BF16 = jnp.bfloat16
F32 = jnp.float32
GROUP = 16
TILE = 8
SLOTS = 4
STEPS = GROUP // SLOTS
MIB = 1024 * 1024


def rounded(table):
    return np.asarray(table, np.float32).astype(ml_dtypes.bfloat16)


def angles(freq, points, length):
    phase = np.mod(np.outer(freq, points), length)
    return (phase * (2.0 * math.pi / length)).astype(np.float64)


def signed(count):
    index = np.arange(count)
    return np.where(index < count // 2, index, index - count)


def z_base(rows_z):
    theta = angles(np.arange(MZ), np.arange(rows_z), rows_z)
    pair = np.stack([np.cos(theta), -np.sin(theta)])
    table = np.repeat(pair.reshape(2 * MZ, rows_z), GROUP, axis=0).T
    return rounded(table).astype(np.float32)


def y_table(rows_y, width):
    theta = angles(signed(MY), np.arange(rows_y), rows_y)
    cosine, sine = np.cos(theta), np.sin(theta)
    turn = np.stack([np.stack([cosine, sine]), np.stack([-sine, cosine])])
    table = np.einsum("rsjy,xw->jxrswy", turn, np.eye(width))
    return rounded(table.reshape(MY * width * 2, 2 * width * rows_y))


def x_tables(samples, slabs, length):
    theta = angles(signed(MX), np.arange(length), length)
    cosine, sine = np.cos(theta), np.sin(theta)
    forward = np.stack([np.stack([cosine, sine]), np.stack([-sine, cosine])])
    inverse = np.stack([np.stack([cosine, sine]), np.stack([-sine, cosine])]) / length
    same = np.eye(samples)
    rows = MX * 2 * samples

    def lay(turn):
        turn = turn.reshape(2, 2, MX, slabs, length // slabs)
        table = np.einsum("arqsx,bd->qabdsxr", turn, same)
        return rounded(table.reshape(rows, samples * length * 2))

    return lay(forward), lay(inverse)


def dot(left, right):
    return jnp.dot(left, right, preferred_element_type=F32)


def doubled_slope(u):
    decay = jnp.exp(-(u * u)).astype(BF16)
    cdf = (1.0 + lax.erf(u)).astype(BF16)
    return cdf + u.astype(BF16) * jnp.asarray(2.0 / math.sqrt(math.pi), BF16) * decay


def over(index, size):
    return lax.shift_right_logical(index, jnp.int32(size.bit_length() - 1))


def within(index, size):
    return jnp.bitwise_and(index, jnp.int32(size - 1))


def fill_z(base, table):
    rows_z, lanes = base.shape
    owner = within(lax.broadcasted_iota(jnp.int32, (rows_z, lanes), 1), GROUP)
    values = base[...]
    for c in range(GROUP):
        table[c * rows_z : (c + 1) * rows_z] = jnp.where(owner == c, values, 0.0).astype(BF16)


def fill_z_back(base, table):
    lanes, rows_z = base.shape
    owner = within(lax.broadcasted_iota(jnp.int32, (lanes, rows_z), 0), GROUP)
    values = base[...]
    for c in range(GROUP):
        first = c % SLOTS * rows_z
        table[c // SLOTS, :, first : first + rows_z] = jnp.where(owner == c, values, 0.0).astype(BF16)


def grouped(lane, per, channels):
    c = within(lane, channels)
    return over(c, GROUP) * (MZ * GROUP) + over(lane, channels) * GROUP + within(c, GROUP)


def fill_order(per, channels, back, table):
    count = table.shape[0]
    row = lax.broadcasted_iota(jnp.int32, (count, count), 0)
    column = lax.broadcasted_iota(jnp.int32, (count, count), 1)
    if back:
        same = grouped(row[:, :1], per, channels) == column
    else:
        same = row == grouped(column[:1], per, channels)
    table[...] = jnp.where(same, 1.0, 0.0).astype(BF16)


def turned_index(index, slabs, devices):
    samples = devices // slabs
    return index % samples * slabs + index // samples


def deliver(spectra, ytab, order, scale, message, per, channels, slabs):
    groups = channels // GROUP
    rows = spectra.shape[0] // groups
    wide = spectra.shape[1] // 2
    halves = []
    for r in range(2):
        blocks = [spectra[g * rows : (g + 1) * rows, r * wide : (r + 1) * wide] for g in range(groups)]
        halves.append(jnp.concatenate(blocks, axis=1).astype(BF16))
    planes = dot(ytab[...], jnp.concatenate(halves, axis=0))
    if scale is not None:
        planes = planes * scale[...]
    ordered = dot(planes.astype(BF16), order[...]).astype(BF16)
    parts = MZ // per
    count = message.shape[1]
    lanes = per * channels
    for part in range(parts):
        block = ordered[:, part * lanes : (part + 1) * lanes]
        for j in range(MY):
            message[turned_index(j * parts + part, slabs, message.shape[0])] = block[j * count : (j + 1) * count]


def receive(message, order_back, ytab_back, scale, held, per, slabs):
    parts = MZ // per
    lanes = [
        jnp.concatenate(
            [message[turned_index(j * parts + part, slabs, message.shape[0])] for j in range(MY)], axis=0
        )
        for part in range(parts)
    ]
    ordered = dot(jnp.concatenate(lanes, axis=1), order_back[...]).astype(BF16)
    lines = dot(ytab_back[...], ordered)
    if scale is not None:
        lines = lines * scale[...]
    lines = lines.astype(BF16)
    rows = lines.shape[0] // 2
    wide = MZ * GROUP
    for group in range(held.shape[0] // rows):
        piece = lines[:, group * wide : (group + 1) * wide]
        held[group * rows : (group + 1) * rows] = jnp.concatenate([piece[:rows], piece[rows:]], axis=1)


class Move:
    def __init__(self, source, target, sems):
        self.source, self.target, self.sems = source, target, sems
        self.groups = target.shape[0] // GROUP

    def copy(self, step, g):
        run = pl.ds(g * GROUP + step * SLOTS, SLOTS)
        sem = self.sems.at[step * self.groups + g]
        return pltpu.make_async_copy(self.source.at[run], self.target.at[run], sem)

    def start(self, step):
        for g in range(self.groups):
            self.copy(step, g).start()

    def wait(self, step):
        for g in range(self.groups):
            self.copy(step, g).wait()


def start_all(moves, step):
    for each in moves:
        each.start(step)


def add_spectra(field, ztab, step, spectra):
    groups = field.shape[0] // GROUP
    rows_z = field.shape[-1]
    depth = SLOTS * rows_z
    table = ztab[pl.ds(pl.multiple_of(step * depth, depth), depth)]
    lanes = [
        jnp.concatenate(
            [field[g * GROUP + step * SLOTS + slot].reshape(-1, rows_z) for g in range(groups)], axis=0
        )
        for slot in range(SLOTS)
    ]
    spectra[...] += dot(jnp.concatenate(lanes, axis=1), table)


def plane_kernel(
    per, channels, slabs, field, base_far, ytab_far, message, ztab, order, spectra, buffer, base, ytab, sems, table_sems
):
    incoming = Move(field.at[0], buffer, sems)
    base_copy = pltpu.make_async_copy(base_far, base, table_sems.at[0])
    ytab_copy = pltpu.make_async_copy(ytab_far, ytab, table_sems.at[1])
    base_copy.start()
    incoming.start(0)
    fill_order(per, channels, False, order)
    spectra[...] = jnp.zeros_like(spectra)
    incoming.start(1)
    base_copy.wait()
    fill_z(base, ztab)
    incoming.start(2)
    ytab_copy.start()
    incoming.start(3)

    @pl.loop(0, STEPS)
    def _(step):
        incoming.wait(step)
        add_spectra(buffer, ztab, step, spectra)

    ytab_copy.wait()
    deliver(spectra, ytab, order, None, message, per, channels, slabs)


def slope_kernel(
    per, channels, slabs, arrived, local, cotangent, base, base_back, ytab, ytab_back, scale, scale_back,
    slope, message, ztab, ztab_back, order, held, spectra, local_in, cotangent_in, result, total,
    local_sems, cotangent_sems, result_sems,
):
    width, rows_y, rows_z = local.shape[1:]
    groups = channels // GROUP
    rows = width * rows_y
    wide = 2 * rows_y
    incoming = (Move(local, local_in, local_sems), Move(cotangent.at[0], cotangent_in, cotangent_sems))
    outgoing = Move(result, slope, result_sems)
    start_all(incoming, 0)
    fill_order(per, channels, True, order)
    receive(arrived, order, ytab_back, scale_back, held, per, slabs)
    start_all(incoming, 1)
    fill_z_back(base_back, ztab_back)
    fill_z(base, ztab)
    start_all(incoming, 2)
    fill_order(per, channels, False, order)
    spectra[...] = jnp.zeros_like(spectra)
    start_all(incoming, 3)

    @pl.loop(0, STEPS)
    def _(step):
        for each in incoming:
            each.wait(step)
        total[...] = dot(held[...], ztab_back[step])
        for g in range(groups):
            for slot in range(SLOTS):
                lanes = slice(slot * rows_z, (slot + 1) * rows_z)
                c = g * GROUP + step * SLOTS + slot
                for x in range(0, width, 2):
                    place = g * rows + x * rows_y
                    value = total[place : place + wide, lanes]
                    value = value + local_in[c, x : x + 2].reshape(wide, rows_z).astype(F32)
                    upstream = cotangent_in[c, x : x + 2].reshape(wide, rows_z)
                    answer = upstream * doubled_slope(value)
                    result[c, x : x + 2] = answer.reshape(2, rows_y, rows_z)
            outgoing.copy(step, g).start()
        add_spectra(result, ztab, step, spectra)

    deliver(spectra, ytab, order, scale, message, per, channels, slabs)
    for step in range(STEPS):
        outgoing.wait(step)


def field_kernel(
    per, channels, slabs, arrived, local, base_back, ytab_back, out, ztab_back, order, held, local_in, result,
    local_sems, result_sems,
):
    width, rows_y, rows_z = local.shape[1:]
    groups = channels // GROUP
    rows = width * rows_y
    incoming = Move(local, local_in, local_sems)
    outgoing = Move(result, out.at[0], result_sems)
    incoming.start(0)
    fill_order(per, channels, True, order)
    incoming.start(1)
    receive(arrived, order, ytab_back, None, held, per, slabs)
    incoming.start(2)
    fill_z_back(base_back, ztab_back)
    incoming.start(3)

    @pl.loop(0, STEPS)
    def _(step):
        incoming.wait(step)
        total = dot(held[...], ztab_back[step])
        for g in range(groups):
            for slot in range(SLOTS):
                lanes = slice(slot * rows_z, (slot + 1) * rows_z)
                c = g * GROUP + step * SLOTS + slot
                value = total[g * rows : (g + 1) * rows, lanes]
                value = value + local_in[c].reshape(rows, rows_z).astype(F32)
                result[c] = value.astype(BF16).reshape(width, rows_y, rows_z)
            outgoing.copy(step, g).start()

    for step in range(STEPS):
        outgoing.wait(step)


def pointwise_kernel(turned, field, mix, offsets, out, table, shift):
    channels = mix.shape[0]
    width, rows_y, rows_z = field.shape[1:]
    size = channels * TILE

    @pl.when(pl.program_id(0) == 0)
    def _():
        row = over(lax.broadcasted_iota(jnp.int32, (size, channels), 0), TILE)
        column = lax.broadcasted_iota(jnp.int32, (size, channels), 1)
        spread = jnp.where(row == column, 1.0, 0.0).astype(BF16)
        tall = lax.dot_general(
            spread, mix[...], (((1,), (1 if turned else 0,)), ((), ())), preferred_element_type=F32
        ).astype(BF16)
        whole = lax.dot_general(
            tall, spread, (((1,), (1,)), ((), ())), preferred_element_type=F32
        )
        place = within(lax.broadcasted_iota(jnp.int32, (size, size), 0), TILE)
        other = within(lax.broadcasted_iota(jnp.int32, (size, size), 1), TILE)
        table[...] = jnp.where(place == other, whole if turned else 0.5 * whole, 0.0).astype(BF16)
        if offsets is not None:
            for c in range(channels):
                shift[c] = jnp.full((1, rows_z), offsets[c], F32)

    for start in range(0, rows_y, 2 * TILE):
        pieces = [field[:, x, start : start + 2 * TILE, :].astype(F32) for x in range(width)]
        halves = []
        for row in range(0, 2 * TILE, TILE):
            rows = [piece[:, row : row + TILE].reshape(size, rows_z).astype(BF16) for piece in pieces]
            halves.append(dot(table[...], jnp.concatenate(rows, axis=1)))
        for x in range(width):
            values = [
                half[:, x * rows_z : (x + 1) * rows_z].reshape(channels, TILE, rows_z) for half in halves
            ]
            value = jnp.concatenate(values, axis=1)
            if offsets is not None:
                value = (value + shift[...]) * math.sqrt(0.5)
            out[:, x, start : start + 2 * TILE, :] = value.astype(BF16)


def spread_pair(first, second):
    nothing = jnp.zeros_like(first)
    upper = jnp.concatenate([first, nothing], axis=1)
    lower = jnp.concatenate([nothing, second], axis=1)
    return jnp.concatenate([upper, lower], axis=0)


def low_half(shape):
    return lax.broadcasted_iota(jnp.int32, shape, 1) < shape[1] // 2


def mix_kernel(per, samples, arrived, weights, line, line_back, spec_in, message, held):
    rows = 2 * samples
    lanes = 2 * weights.shape[1]
    low = low_half((samples, lanes))
    flat = arrived[...].reshape(-1, arrived.shape[2])
    spectra = dot(line[...], flat).astype(BF16)
    spec_in[...] = spectra
    for q in range(MX):
        for first in range(0, per, 2):
            block = spread_pair(weights[first * MX + q], weights[(first + 1) * MX + q])
            place = first // 2 * lanes
            terms = dot(spectra[q * rows : (q + 1) * rows, place : place + lanes], block)
            mixed = []
            for side in range(2):
                part = terms[:, side * lanes : (side + 1) * lanes]
                turned = pltpu.roll(part[samples:], lanes // 2, 1)
                mixed.append(part[:samples] + jnp.where(low, -turned, turned))
            real = jnp.where(low, mixed[0], pltpu.roll(mixed[1], lanes // 2, 1))
            imag = jnp.where(low, pltpu.roll(mixed[0], lanes // 2, 1), mixed[1])
            held[q * rows : (q + 1) * rows, place : place + lanes] = jnp.concatenate(
                [real, imag], axis=0
            ).astype(BF16)
    message[...] = dot(line_back[...], held[...]).astype(BF16).reshape(message.shape)


def mix_back_kernel(per, samples, arrived, weights, line, line_back, pairs, message, held):
    rows = 2 * samples
    lanes = 2 * weights.shape[1]
    low = low_half((samples, lanes))
    flat = arrived[...].reshape(-1, arrived.shape[2])
    spectra = dot(line[...], flat).astype(BF16).astype(F32)
    for q in range(MX):
        for first in range(0, per, 2):
            block = spread_pair(weights[first * MX + q], weights[(first + 1) * MX + q])
            place = first // 2 * lanes
            real = spectra[q * rows : q * rows + samples, place : place + lanes]
            imag = spectra[q * rows + samples : (q + 1) * rows, place : place + lanes]
            real_turned = pltpu.roll(real, lanes // 2, 1)
            imag_turned = pltpu.roll(imag, lanes // 2, 1)
            left = [jnp.where(low, real, imag_turned), jnp.where(low, imag, -real_turned)]
            right = [jnp.where(low, real_turned, imag), jnp.where(low, imag_turned, -real)]
            pair = jnp.concatenate(
                [jnp.concatenate(left, axis=0), jnp.concatenate(right, axis=0)], axis=1
            ).astype(BF16)
            pairs[q * rows : (q + 1) * rows, 2 * place : 2 * (place + lanes)] = pair
            held[q * rows : (q + 1) * rows, place : place + lanes] = lax.dot_general(
                pair, block, (((1,), (1,)), ((), ())), preferred_element_type=F32
            ).astype(BF16)
    message[...] = dot(line_back[...], held[...]).astype(BF16).reshape(message.shape)


def weight_kernel(per, samples, spec_in, pairs, out):
    rows = 2 * samples
    lanes = out.shape[2]
    half = lanes // 2
    for q in range(MX):
        for first in range(0, per, 2):
            place = first // 2 * lanes
            left = spec_in[q * rows : (q + 1) * rows, place : place + lanes]
            right = pairs[q * rows : (q + 1) * rows, 2 * place : 2 * (place + lanes)]
            outer = lax.dot_general(
                left, right, (((0,), (0,)), ((), ())), preferred_element_type=F32
            )
            out[first * MX + q] = outer[:half, :lanes]
            out[(first + 1) * MX + q] = outer[half:, lanes:]


def whole(array):
    return pl.BlockSpec(array.shape, lambda *step: (0,) * len(array.shape))


def shaped(shape, dtype):
    return jax.ShapeDtypeStruct(shape, dtype)


def params(mib):
    return pltpu.CompilerParams(vmem_limit_bytes=mib * MIB)


def cost(flops, moved, steep=0):
    return pl.CostEstimate(flops=flops, bytes_accessed=moved, transcendentals=steep)


def body(mesh_axes, devices, slabs, activations, cotangent, mode_weights, pointwise, offsets):
    _, channels, width, rows_y, rows_z = activations.shape
    samples = devices // slabs
    per = MY * MZ // devices
    groups = channels // GROUP
    field = activations.shape[1:]
    count = math.prod(field)
    base = z_base(rows_z)
    ytab = y_table(rows_y, width)
    line_fwd, line_inv = x_tables(samples, slabs, NX)
    weight = np.where(np.arange(MZ) == 0, 1.0, 2.0) / (rows_y * rows_z)
    scale = np.tile(np.repeat(weight, GROUP), groups)[None]
    scale, scale_t = (0.5 * scale).astype(np.float32), (math.sqrt(0.5) * scale).astype(np.float32)
    base_t, ytab_t = (np.ascontiguousarray(t.T) for t in (base, ytab))
    fwd_t, inv_t = (np.ascontiguousarray(t.T) for t in (line_fwd, line_inv))
    message = shaped((devices, 2 * width, per * channels), BF16)
    spectra = shaped((MX * 2 * samples, per * channels), BF16)
    ztab = pltpu.VMEM((GROUP * rows_z, 2 * MZ * GROUP), BF16)
    ztab_t = pltpu.VMEM((STEPS, 2 * MZ * GROUP, SLOTS * rows_z), BF16)
    order = pltpu.VMEM((MZ * channels, MZ * channels), BF16)
    rows = groups * width * rows_y
    held = pltpu.VMEM((rows, 2 * MZ * GROUP), BF16)
    sums = pltpu.VMEM((rows, 2 * MZ * GROUP), F32)
    slot_sums = pltpu.VMEM((rows, SLOTS * rows_z), F32)
    buffer = pltpu.VMEM(field, BF16)
    sems = pltpu.SemaphoreType.DMA((STEPS * groups,))
    far = pl.BlockSpec(memory_space=pltpu.HBM)
    far_field = pltpu.HBM(field, BF16)

    def kept_far(array):
        return pltpu.with_memory_space_constraint(array, pltpu.HBM)

    plane_flops = 2 * count * 2 * MZ * GROUP

    def exchange(array):
        return lax.all_to_all(array, mesh_axes, split_axis=0, concat_axis=0, tiled=True)

    def mix_points(values, turned, shifts):
        step = 2
        block = pl.BlockSpec((channels, step, rows_y, rows_z), lambda x: (0, x, 0, 0))
        kernel = functools.partial(pointwise_kernel, turned)
        specs = [block, whole(pointwise)]
        operands = [values, pointwise]
        if shifts is None:
            run = lambda a, b, *rest: kernel(a, b, None, *rest)
        else:
            run = kernel
            specs.append(pl.BlockSpec(memory_space=pltpu.SMEM))
            operands.append(shifts)
        return pl.pallas_call(
            run,
            grid=(width // step,),
            in_specs=specs,
            out_specs=block,
            out_shape=far_field,
            scratch_shapes=[
                pltpu.VMEM((channels * TILE, channels * TILE), BF16),
                pltpu.VMEM((channels, 1, rows_z), F32),
            ],
            compiler_params=params(32),
            cost_estimate=cost(2 * count * channels * TILE, 4 * count),
        )(*operands)

    planes = pl.pallas_call(
        functools.partial(plane_kernel, per, channels, slabs),
        in_specs=[far, far, far],
        out_specs=whole(message),
        out_shape=message,
        scratch_shapes=[
            ztab,
            order,
            sums,
            buffer,
            pltpu.VMEM(base.shape, F32),
            pltpu.VMEM(ytab.shape, BF16),
            sems,
            pltpu.SemaphoreType.DMA((2,)),
        ],
        compiler_params=params(32),
        cost_estimate=cost(plane_flops, 2 * count),
    )(kept_far(activations), kept_far(base), kept_far(ytab))
    arrived = exchange(planes)
    local = mix_points(kept_far(activations.reshape(field)), True, offsets)
    arrived, local = lax.optimization_barrier((arrived, local))
    spec_in, mixed = pl.pallas_call(
        functools.partial(mix_kernel, per, samples),
        out_shape=(spectra, message),
        scratch_shapes=[pltpu.VMEM(spectra.shape, BF16)],
        compiler_params=params(16),
        cost_estimate=cost(10**8, 2 * mode_weights.size),
    )(arrived, mode_weights, line_fwd, inv_t)
    returned = exchange(mixed)
    slope, back_plane = pl.pallas_call(
        functools.partial(slope_kernel, per, channels, slabs),
        in_specs=[whole(message), far, far]
        + [whole(t) for t in (base, base_t, ytab, ytab_t, scale, scale_t)],
        out_specs=(far, whole(message)),
        out_shape=(far_field, message),
        scratch_shapes=[ztab, ztab_t, order, held, sums]
        + [buffer] * 3
        + [slot_sums]
        + [sems] * 3,
        compiler_params=params(40),
        cost_estimate=cost(2 * plane_flops, 6 * count, 2 * count),
    )(returned, kept_far(local), kept_far(cotangent), base, base_t, ytab, ytab_t, scale, scale_t)
    arrived_back = exchange(back_plane)
    local_back = mix_points(kept_far(slope), False, None)
    arrived_back, local_back = lax.optimization_barrier((arrived_back, local_back))
    pairs, mixed_back = pl.pallas_call(
        functools.partial(mix_back_kernel, per, samples),
        out_shape=(shaped((spectra.shape[0], 2 * spectra.shape[1]), BF16), message),
        scratch_shapes=[pltpu.VMEM(spectra.shape, BF16)],
        compiler_params=params(16),
        cost_estimate=cost(10**8, 2 * mode_weights.size),
    )(arrived_back, mode_weights, line_inv, fwd_t)
    returned_back = exchange(mixed_back)
    grad_spectral = pl.pallas_call(
        functools.partial(weight_kernel, per, samples),
        out_shape=shaped(mode_weights.shape, F32),
        compiler_params=params(16),
        cost_estimate=cost(10**8, 4 * mode_weights.size),
    )(spec_in, pairs)
    grad_in = pl.pallas_call(
        functools.partial(field_kernel, per, channels, slabs),
        in_specs=[whole(message), far, whole(base_t), whole(ytab_t)],
        out_specs=far,
        out_shape=shaped(activations.shape, BF16),
        scratch_shapes=[ztab_t, order, held, buffer, buffer, sems, sems],
        compiler_params=params(32),
        cost_estimate=cost(plane_flops, 4 * count),
    )(returned_back, kept_far(local_back), base_t, ytab_t)
    return (grad_in, grad_spectral)


def chosen_body(mesh_axes, devices, slabs, activations, cotangent, mode_weights, pointwise, offsets):
    samples, channels, width, rows_y, rows_z = activations.shape
    per = MY * MZ // devices
    fits = (
        samples == 1
        and MY * MZ % devices == 0
        and per in (2, 4, 8)
        and width % 8 == 0
        and channels == 64
        and rows_y % TILE == 0
        and rows_z == 128
    )
    plan = functools.partial(body, mesh_axes, devices, slabs) if fits else general_body
    return plan(activations, cotangent, mode_weights, pointwise, offsets)


def solution(mesh):
    slabs = mesh.shape["space"]
    devices = slabs * mesh.shape["dp"]
    return jax.shard_map(
        functools.partial(chosen_body, ("dp", "space"), devices, slabs),
        mesh=mesh,
        in_specs=(
            P("dp", None, "space", None, None),
            P("dp", None, "space", None, None),
            P(("space", "dp"), None, None),
            P(),
            P(),
        ),
        out_specs=(P("dp", None, "space", None, None), P(("space", "dp"), None, None)),
        check_vma=False,
    )
```

profile of v0, /device:TPU:0, one launch (start us, length us, event | category | flops | bytes accessed | tf_op | source)
XLA Modules:
  0.0 86.6 jit_solution(15694049508192743027)
XLA Ops:
  0.6 0.0 copy-start.9
  0.6 0.0 copy-start.12
  0.6 5.7 %shard_map.158 = bf16[32,16,256]{2,1,0:T(8,128)(2,1)} custom-call(bf16[1,64,8,48,128]{4,3,2,1,0:T(8,128)(2,1)} %field.1, f32[128,256]{1,0:T(8,128)} %constant.20.clone.base_far.base, bf16[256,768]{1,0:T(8,128)(2,1)} %constant.21.clone.ytab_far.ytab), custom_call_target="tpu_custom_call" | custom-call | flops 1610612736 | bytes 6291456 | tf_op jit(solution)/shard_map/pallas_call | solution.py:650
  6.4 7.3 %all-to-all-start = ((bf16[32,16,256]{2,1,0:T(8,128)(2,1)}), bf16[32,16,256]{2,1,0:T(8,128)(2,1)S(1)}, u32[]{:S(2)}, u32[]{:S(2)}) async-start(bf16[32,16,256]{2,1,0:T(8,128)(2,1)} %shard_map.158), calls=%async_computation | async-start | bytes 524288 | tf_op jit(solution)/shard_map/all_to_all | solution.py:622
  13.7 0.0 copy-done.9
  13.7 0.0 copy-start
  13.7 0.0 copy-start.7
  13.7 0.0 copy-start.8
  13.8 0.0 copy-start.1
  13.8 0.0 copy-start.2
  13.8 0.0 copy-start.3
  13.8 0.0 copy-start.4
  13.8 0.0 copy-start.10
  13.8 0.0 copy-start.11
  13.8 8.3 %shard_map.159.local = bf16[64,8,48,128]{3,2,1,0:T(8,128)(2,1)} custom-call(bf16[64,8,48,128]{3,2,1,0:T(8,128)(2,1)} %bitcast.1, bf16[64,64]{1,0:T(8,128)(2,1)S(1)} %copy-done.9, f32[64]{0:T(128)S(1)} %copy-done.12), custom_call_target="tpu_custom_call" | custom-call | flops 3221225472 | bytes 12582912 | tf_op jit(solution)/shard_map/pallas_call | solution.py:636
  22.1 2.2 %all-to-all-done.arrived = bf16[32,16,256]{2,1,0:T(8,128)(2,1)S(1)} async-done(((bf16[32,16,256]{2,1,0:T(8,128)(2,1)}), bf16[32,16,256]{2,1,0:T(8,128)(2,1)S(1)}, u32[]{:S(2)}, u32[]{:S(2)}) %all-to-all-start) | async-done | bytes 262176 | tf_op jit(solution)/shard_map/all_to_all | solution.py:622
  24.3 0.0 copy-done.7
  24.3 1.0 %shard_map.160 = (bf16[256,256]{1,0:T(8,128)(2,1)S(1)}, bf16[32,16,256]{2,1,0:T(8,128)(2,1)S(1)}) custom-call(bf16[32,16,256]{2,1,0:T(8,128)(2,1)S(1)} %all-to-all-done.arrived, bf16[64,64,128]{2,1,0:T(8,128)(2,1)S(1)} %copy-done, bf16[256,512]{1,0:T(8,128)(2,1)S(1)} %copy-done.8, bf16[512,256]{1,0:T(8,128)(2,1)S(1)} %copy-done.7), custom_call_target="tpu_custom_call" | custom-call | flops 100000000 | bytes 1048576 | tf_op jit(solution)/shard_map/pallas_call | solution.py:671
  25.3 14.1 %all_to_all.20.arrived = bf16[32,16,256]{2,1,0:T(8,128)(2,1)S(1)} all-to-all(bf16[32,16,256]{2,1,0:T(8,128)(2,1)S(1)} %get-tuple-element.13), channel_id=1, replica_groups=mesh['dp'=8,'space'=4] {'dp','space'}, dimensions={0} | all-to-all | bytes 524288 | tf_op jit(solution)/shard_map/all_to_all | solution.py:622
  39.4 0.0 copy-done.1
  39.4 12.4 %shard_map.161 = (bf16[64,8,48,128]{3,2,1,0:T(8,128)(2,1)}, bf16[32,16,256]{2,1,0:T(8,128)(2,1)}) custom-call(bf16[32,16,256]{2,1,0:T(8,128)(2,1)S(1)} %all_to_all.20.arrived, bf16[64,8,48,128]{3,2,1,0:T(8,128)(2,1)} %shard_map.159.local, bf16[1,64,8,48,128]{4,3,2,1,0:T(8,128)(2,1)} %cotangent.1, f32[128,256]{1,0:T(8,128)S(1)} %copy-done.4, ...), custom_call_target="tpu_custom_call" | custom-call | flops 3221225472 | bytes 18874368 | tf_op jit(solution)/shard_map/pallas_call | solution.py:679
  51.8 2.6 %all-to-all-start.2 = ((bf16[32,16,256]{2,1,0:T(8,128)(2,1)}), bf16[32,16,256]{2,1,0:T(8,128)(2,1)S(1)}, u32[]{:S(2)}, u32[]{:S(2)}) async-start(bf16[32,16,256]{2,1,0:T(8,128)(2,1)} %get-tuple-element.15), calls=%async_computation.2 | async-start | bytes 524288 | tf_op jit(solution)/shard_map/all_to_all | solution.py:622
  54.4 0.0 copy-start.5
  54.4 0.0 copy-start.6
  54.4 8.2 %shard_map.162.local = bf16[64,8,48,128]{3,2,1,0:T(8,128)(2,1)} custom-call(bf16[64,8,48,128]{3,2,1,0:T(8,128)(2,1)} %get-tuple-element.16.a, bf16[64,64]{1,0:T(8,128)(2,1)S(1)} %copy-done.9), custom_call_target="tpu_custom_call" | custom-call | flops 3221225472 | bytes 12582912 | tf_op jit(solution)/shard_map/pallas_call | solution.py:636
  62.6 2.4 %all-to-all-done.2.arrived = bf16[32,16,256]{2,1,0:T(8,128)(2,1)S(1)} async-done(((bf16[32,16,256]{2,1,0:T(8,128)(2,1)}), bf16[32,16,256]{2,1,0:T(8,128)(2,1)S(1)}, u32[]{:S(2)}, u32[]{:S(2)}) %all-to-all-start.2) | async-done | bytes 262176 | tf_op jit(solution)/shard_map/all_to_all | solution.py:622
  65.0 0.0 copy-done.5
  65.0 1.9 %shard_map.163 = (bf16[256,512]{1,0:T(8,128)(2,1)S(1)}, bf16[32,16,256]{2,1,0:T(8,128)(2,1)}) custom-call(bf16[32,16,256]{2,1,0:T(8,128)(2,1)S(1)} %all-to-all-done.2.arrived, bf16[64,64,128]{2,1,0:T(8,128)(2,1)S(1)} %copy-done, bf16[256,512]{1,0:T(8,128)(2,1)S(1)} %copy-done.6, bf16[512,256]{1,0:T(8,128)(2,1)S(1)} %copy-done.5), custom_call_target="tpu_custom_call" | custom-call | flops 100000000 | bytes 1048576 | tf_op jit(solution)/shard_map/pallas_call | solution.py:695
  66.9 3.4 %all-to-all-start.3 = ((bf16[32,16,256]{2,1,0:T(8,128)(2,1)}), bf16[32,16,256]{2,1,0:T(8,128)(2,1)S(1)}, u32[]{:S(2)}, u32[]{:S(2)}) async-start(bf16[32,16,256]{2,1,0:T(8,128)(2,1)} %get-tuple-element.18), calls=%async_computation.3 | async-start | bytes 524288 | tf_op jit(solution)/shard_map/all_to_all | solution.py:622
  70.3 2.1 %shard_map.165 = f32[64,64,128]{2,1,0:T(8,128)} custom-call(bf16[256,256]{1,0:T(8,128)(2,1)S(1)} %get-tuple-element.20.spec_in, bf16[256,512]{1,0:T(8,128)(2,1)S(1)} %get-tuple-element.21.pairs), custom_call_target="tpu_custom_call" | custom-call | flops 100000000 | bytes 2097152 | tf_op jit(solution)/shard_map/pallas_call | solution.py:703
  72.4 8.5 %all-to-all-done.3.arrived = bf16[32,16,256]{2,1,0:T(8,128)(2,1)S(1)} async-done(((bf16[32,16,256]{2,1,0:T(8,128)(2,1)}), bf16[32,16,256]{2,1,0:T(8,128)(2,1)S(1)}, u32[]{:S(2)}, u32[]{:S(2)}) %all-to-all-start.3) | async-done | bytes 262176 | tf_op jit(solution)/shard_map/all_to_all | solution.py:622
  80.9 5.7 %shard_map.164 = bf16[1,64,8,48,128]{4,3,2,1,0:T(8,128)(2,1)} custom-call(bf16[32,16,256]{2,1,0:T(8,128)(2,1)S(1)} %all-to-all-done.3.arrived, bf16[64,8,48,128]{3,2,1,0:T(8,128)(2,1)} %shard_map.162.local, f32[256,128]{1,0:T(8,128)S(1)} %copy-done.3, bf16[768,256]{1,0:T(8,128)(2,1)S(1)} %copy-done.1), custom_call_target="tpu_custom_call" | custom-call | flops 1610612736 | bytes 12582912 | tf_op jit(solution)/shard_map/pallas_call | solution.py:709
  (9 shorter events, 0.0 us)
Async XLA Ops:
  0.6 13.1 %copy-start.9 = (bf16[64,64]{1,0:T(8,128)(2,1)S(1)}, bf16[64,64]{1,0:T(8,128)(2,1)}, u32[]{:S(2)}) copy-start(bf16[64,64]{1,0:T(8,128)(2,1)} %b.1) | copy-start | bytes 24580
  0.6 13.1 %copy-start.12 = (f32[64]{0:T(128)S(1)}, f32[64]{0:T(128)}, u32[]{:S(2)}) copy-start(f32[64]{0:T(128)} %offsets.1) | copy-start | bytes 772
  6.4 17.9 %all-to-all-start = ((bf16[32,16,256]{2,1,0:T(8,128)(2,1)}), bf16[32,16,256]{2,1,0:T(8,128)(2,1)S(1)}, u32[]{:S(2)}, u32[]{:S(2)}) async-start(bf16[32,16,256]{2,1,0:T(8,128)(2,1)} %shard_map.158), calls=%async_computation | async-start | bytes 524288 | tf_op jit(solution)/shard_map/all_to_all | solution.py:622
  13.7 10.6 %copy-start = (bf16[64,64,128]{2,1,0:T(8,128)(2,1)S(1)}, bf16[64,64,128]{2,1,0:T(8,128)(2,1)}, u32[]{:S(2)}) copy-start(bf16[64,64,128]{2,1,0:T(8,128)(2,1)} %weights.3) | copy-start | bytes 3145732
  13.7 10.6 %copy-start.7 = (bf16[512,256]{1,0:T(8,128)(2,1)S(1)}, bf16[512,256]{1,0:T(8,128)(2,1)}, u32[]{:S(2)}) copy-start(bf16[512,256]{1,0:T(8,128)(2,1)} %constant.23.clone.line_back) | copy-start | bytes 786436
  13.7 10.6 %copy-start.8 = (bf16[256,512]{1,0:T(8,128)(2,1)S(1)}, bf16[256,512]{1,0:T(8,128)(2,1)}, u32[]{:S(2)}) copy-start(bf16[256,512]{1,0:T(8,128)(2,1)} %constant.22.clone.line) | copy-start | bytes 786436
  13.8 25.6 %copy-start.1 = (bf16[768,256]{1,0:T(8,128)(2,1)S(1)}, bf16[768,256]{1,0:T(8,128)(2,1)}, u32[]{:S(2)}) copy-start(bf16[768,256]{1,0:T(8,128)(2,1)} %constant.25.clone.ytab_back) | copy-start | bytes 1179652
  13.8 25.6 %copy-start.2 = (bf16[256,768]{1,0:T(8,128)(2,1)S(1)}, bf16[256,768]{1,0:T(8,128)(2,1)}, u32[]{:S(2)}) copy-start(bf16[256,768]{1,0:T(8,128)(2,1)} %constant.21.clone.ytab_far.ytab) | copy-start | bytes 1179652
  13.8 25.6 %copy-start.3 = (f32[256,128]{1,0:T(8,128)S(1)}, f32[256,128]{1,0:T(8,128)}, u32[]{:S(2)}) copy-start(f32[256,128]{1,0:T(8,128)} %constant.24.clone.base_back) | copy-start | bytes 393220
  13.8 25.6 %copy-start.4 = (f32[128,256]{1,0:T(8,128)S(1)}, f32[128,256]{1,0:T(8,128)}, u32[]{:S(2)}) copy-start(f32[128,256]{1,0:T(8,128)} %constant.20.clone.base_far.base) | copy-start | bytes 393220
  13.8 25.6 %copy-start.10 = (f32[1,512]{1,0:T(1,128)S(1)}, f32[1,512]{1,0:T(1,128)}, u32[]{:S(2)}) copy-start(f32[1,512]{1,0:T(1,128)} %constant.27.clone.scale_back) | copy-start | bytes 6148
  13.8 25.6 %copy-start.11 = (f32[1,512]{1,0:T(1,128)S(1)}, f32[1,512]{1,0:T(1,128)}, u32[]{:S(2)}) copy-start(f32[1,512]{1,0:T(1,128)} %constant.26.clone.scale) | copy-start | bytes 6148
  51.8 13.2 %all-to-all-start.2 = ((bf16[32,16,256]{2,1,0:T(8,128)(2,1)}), bf16[32,16,256]{2,1,0:T(8,128)(2,1)S(1)}, u32[]{:S(2)}, u32[]{:S(2)}) async-start(bf16[32,16,256]{2,1,0:T(8,128)(2,1)} %get-tuple-element.15), calls=%async_computation.2 | async-start | bytes 524288 | tf_op jit(solution)/shard_map/all_to_all | solution.py:622
  54.4 10.6 %copy-start.5 = (bf16[512,256]{1,0:T(8,128)(2,1)S(1)}, bf16[512,256]{1,0:T(8,128)(2,1)}, u32[]{:S(2)}) copy-start(bf16[512,256]{1,0:T(8,128)(2,1)} %constant.29.clone.line_back) | copy-start | bytes 786436
  54.4 10.6 %copy-start.6 = (bf16[256,512]{1,0:T(8,128)(2,1)S(1)}, bf16[256,512]{1,0:T(8,128)(2,1)}, u32[]{:S(2)}) copy-start(bf16[256,512]{1,0:T(8,128)(2,1)} %constant.28.clone.line) | copy-start | bytes 786436
  66.9 14.0 %all-to-all-start.3 = ((bf16[32,16,256]{2,1,0:T(8,128)(2,1)}), bf16[32,16,256]{2,1,0:T(8,128)(2,1)S(1)}, u32[]{:S(2)}, u32[]{:S(2)}) async-start(bf16[32,16,256]{2,1,0:T(8,128)(2,1)} %get-tuple-element.18), calls=%async_computation.3 | async-start | bytes 524288 | tf_op jit(solution)/shard_map/all_to_all | solution.py:622
where the time goes:
time: 87.1 us; the launch traced here: 86.6 us
  Pallas kernels  45.2 us (52%)
  blocking collectives  14.1 us (16%)
  starting transfers between devices  13.3 us (15%)
  waiting for transfers between devices  13.1 us (15%)
    pallas_call x2, Pallas kernels, mix_points(): pl.pallas_call(run, grid=(width // step,), in_specs=specs, out_specs=bloc...  16.4 us
    all_to_all x1, blocking collectives, exchange(): lax.all_to_all(array, mesh_axes, split_axis=0, concat_axis=0, tiled=True)  14.1 us
    all_to_all x3, starting transfers between devices, exchange(): lax.all_to_all(array, mesh_axes, split_axis=0, concat_axis=0, tiled=True)  13.3 us
    all_to_all x3, waiting for transfers between devices, exchange(): lax.all_to_all(array, mesh_axes, split_axis=0, concat_axis=0, tiled=True)  13.1 us
    pallas_call x1, Pallas kernels, body(): pl.pallas_call(functools.partial(slope_kernel, per, channels, slabs), in_...  12.4 us
    pallas_call x1, Pallas kernels, body(): pl.pallas_call(functools.partial(plane_kernel, per, channels, slabs), in_...  5.73 us
    pallas_call x1, Pallas kernels, body(): pl.pallas_call(functools.partial(field_kernel, per, channels, slabs), in_...  5.66 us
    pallas_call x1, Pallas kernels, body(): pl.pallas_call(functools.partial(weight_kernel, per, samples), out_shape=...  2.07 us
  transfers between devices with their start and end apart: 3, of which 3 were waited for; matrix products, arithmetic and copies ran while one was open for 0% of the time, Pallas kernels for 21%

commit v1 on v0

--- a/solution.py
+++ b/solution.py
@@ -215,7 +215,7 @@
 
 
 def doubled_slope(u):
-    decay = jnp.exp(-(u * u)).astype(BF16)
+    decay = jnp.exp2(u * u * -math.log2(math.e)).astype(BF16)
     cdf = (1.0 + lax.erf(u)).astype(BF16)
     return cdf + u.astype(BF16) * jnp.asarray(2.0 / math.sqrt(math.pi), BF16) * decay
 
@@ -308,14 +308,15 @@
 
 
 class Move:
-    def __init__(self, source, target, sems):
+    def __init__(self, source, target, sems, first=0):
         self.source, self.target, self.sems = source, target, sems
         self.groups = target.shape[0] // GROUP
+        self.rows = pl.ds(first, source.shape[1])
 
     def copy(self, step, g):
         run = pl.ds(g * GROUP + step * SLOTS, SLOTS)
         sem = self.sems.at[step * self.groups + g]
-        return pltpu.make_async_copy(self.source.at[run], self.target.at[run], sem)
+        return pltpu.make_async_copy(self.source.at[run], self.target.at[run, self.rows], sem)
 
     def start(self, step):
         for g in range(self.groups):
@@ -372,15 +373,19 @@
 
 
 def slope_kernel(
-    per, channels, slabs, arrived, local, cotangent, base, base_back, ytab, ytab_back, scale, scale_back,
+    per, channels, slabs, arrived, local_low, local_high, cotangent, base, base_back, ytab, ytab_back, scale, scale_back,
     slope, message, ztab, ztab_back, order, held, spectra, local_in, cotangent_in, result, total,
-    local_sems, cotangent_sems, result_sems,
+    low_sems, high_sems, cotangent_sems, result_sems,
 ):
-    width, rows_y, rows_z = local.shape[1:]
+    width, rows_y, rows_z = slope.shape[1:]
     groups = channels // GROUP
     rows = width * rows_y
     wide = 2 * rows_y
-    incoming = (Move(local, local_in, local_sems), Move(cotangent.at[0], cotangent_in, cotangent_sems))
+    incoming = (
+        Move(local_low, local_in, low_sems),
+        Move(local_high, local_in, high_sems, local_low.shape[1]),
+        Move(cotangent.at[0], cotangent_in, cotangent_sems),
+    )
     outgoing = Move(result, slope, result_sems)
     start_all(incoming, 0)
     fill_order(per, channels, True, order)
@@ -530,11 +535,14 @@
     rows = 2 * samples
     lanes = 2 * weights.shape[1]
     low = low_half((samples, lanes))
+    first_lanes = jnp.where(low_half((lanes, lanes)), 1.0, 0.0).astype(BF16)
+    second_lanes = jnp.where(low_half((lanes, lanes)), 0.0, 1.0).astype(BF16)
     flat = arrived[...].reshape(-1, arrived.shape[2])
     spectra = dot(line[...], flat).astype(BF16).astype(F32)
     for q in range(MX):
         for first in range(0, per, 2):
-            block = spread_pair(weights[first * MX + q], weights[(first + 1) * MX + q])
+            both = jnp.concatenate([weights[first * MX + q], weights[(first + 1) * MX + q]], axis=0).T
+            block = jnp.concatenate([both * first_lanes, both * second_lanes], axis=0)
             place = first // 2 * lanes
             real = spectra[q * rows : q * rows + samples, place : place + lanes]
             imag = spectra[q * rows + samples : (q + 1) * rows, place : place + lanes]
@@ -546,9 +554,7 @@
                 [jnp.concatenate(left, axis=0), jnp.concatenate(right, axis=0)], axis=1
             ).astype(BF16)
             pairs[q * rows : (q + 1) * rows, 2 * place : 2 * (place + lanes)] = pair
-            held[q * rows : (q + 1) * rows, place : place + lanes] = lax.dot_general(
-                pair, block, (((1,), (1,)), ((), ())), preferred_element_type=F32
-            ).astype(BF16)
+            held[q * rows : (q + 1) * rows, place : place + lanes] = dot(pair, block).astype(BF16)
     message[...] = dot(line_back[...], held[...]).astype(BF16).reshape(message.shape)
 
 
@@ -621,12 +627,13 @@
     def exchange(array):
         return lax.all_to_all(array, mesh_axes, split_axis=0, concat_axis=0, tiled=True)
 
-    def mix_points(values, turned, shifts):
+    def mix_points(values, mix, turned, shifts, first, rows_x):
         step = 2
         block = pl.BlockSpec((channels, step, rows_y, rows_z), lambda x: (0, x, 0, 0))
+        source = pl.BlockSpec((channels, step, rows_y, rows_z), lambda x: (0, x + first // step, 0, 0))
         kernel = functools.partial(pointwise_kernel, turned)
-        specs = [block, whole(pointwise)]
-        operands = [values, pointwise]
+        specs = [source, whole(pointwise)]
+        operands = [values, mix]
         if shifts is None:
             run = lambda a, b, *rest: kernel(a, b, None, *rest)
         else:
@@ -635,16 +642,16 @@
             operands.append(shifts)
         return pl.pallas_call(
             run,
-            grid=(width // step,),
+            grid=(rows_x // step,),
             in_specs=specs,
             out_specs=block,
-            out_shape=far_field,
+            out_shape=pltpu.HBM((channels, rows_x, rows_y, rows_z), BF16),
             scratch_shapes=[
                 pltpu.VMEM((channels * TILE, channels * TILE), BF16),
                 pltpu.VMEM((channels, 1, rows_z), F32),
             ],
             compiler_params=params(32),
-            cost_estimate=cost(2 * count * channels * TILE, 4 * count),
+            cost_estimate=cost(2 * count * channels * TILE * rows_x // width, 4 * count * rows_x // width),
         )(*operands)
 
     planes = pl.pallas_call(
@@ -665,9 +672,11 @@
         compiler_params=params(32),
         cost_estimate=cost(plane_flops, 2 * count),
     )(kept_far(activations), kept_far(base), kept_far(ytab))
+    planes, early_pointwise = lax.optimization_barrier((planes, pointwise))
     arrived = exchange(planes)
-    local = mix_points(kept_far(activations.reshape(field)), True, offsets)
-    arrived, local = lax.optimization_barrier((arrived, local))
+    half = width // 2
+    local_low = mix_points(kept_far(activations.reshape(field)), early_pointwise, True, offsets, 0, half)
+    arrived, local_low = lax.optimization_barrier((arrived, local_low))
     spec_in, mixed = pl.pallas_call(
         functools.partial(mix_kernel, per, samples),
         out_shape=(spectra, message),
@@ -675,22 +684,24 @@
         compiler_params=params(16),
         cost_estimate=cost(10**8, 2 * mode_weights.size),
     )(arrived, mode_weights, line_fwd, inv_t)
+    mixed, late_pointwise = lax.optimization_barrier((mixed, pointwise))
     returned = exchange(mixed)
+    local_high = mix_points(kept_far(activations.reshape(field)), late_pointwise, True, offsets, half, half)
     slope, back_plane = pl.pallas_call(
         functools.partial(slope_kernel, per, channels, slabs),
-        in_specs=[whole(message), far, far]
+        in_specs=[whole(message), far, far, far]
         + [whole(t) for t in (base, base_t, ytab, ytab_t, scale, scale_t)],
         out_specs=(far, whole(message)),
         out_shape=(far_field, message),
         scratch_shapes=[ztab, ztab_t, order, held, sums]
         + [buffer] * 3
         + [slot_sums]
-        + [sems] * 3,
+        + [sems] * 4,
         compiler_params=params(40),
         cost_estimate=cost(2 * plane_flops, 6 * count, 2 * count),
-    )(returned, kept_far(local), kept_far(cotangent), base, base_t, ytab, ytab_t, scale, scale_t)
+    )(returned, kept_far(local_low), kept_far(local_high), kept_far(cotangent), base, base_t, ytab, ytab_t, scale, scale_t)
     arrived_back = exchange(back_plane)
-    local_back = mix_points(kept_far(slope), False, None)
+    local_back = mix_points(kept_far(slope), pointwise, False, None, 0, width)
     arrived_back, local_back = lax.optimization_barrier((arrived_back, local_back))
     pairs, mixed_back = pl.pallas_call(
         functools.partial(mix_back_kernel, per, samples),

time: 87.1 us -> 87.5 us (level)
  blocking collectives: 14.1 us -> 0 us
  waiting for transfers between devices: 13.1 us -> 21.9 us
  Pallas kernels: 45.2 us -> 48.3 us
  starting transfers between devices: 13.3 us -> 15.9 us
    all_to_all x1 -> x0, blocking collectives: 14.1 us -> none  [exchange(): lax.all_to_all(array, mesh_axes, split_axis=0, concat_axis=0, tiled=True)]
    all_to_all x3 -> x4, waiting for transfers between devices: 13.1 us -> 21.9 us  [exchange(): lax.all_to_all(array, mesh_axes, split_axis=0, concat_axis=0, tiled=True)]
    all_to_all x3 -> x4, starting transfers between devices: 13.3 us -> 15.9 us  [exchange(): lax.all_to_all(array, mesh_axes, split_axis=0, concat_axis=0, tiled=True)]
    pallas_call x2 -> x3, Pallas kernels: 16.4 us -> 18.4 us  [mix_points(): pl.pallas_call(run, grid=(rows_x // step,), in_specs=specs, out_specs=blo...]
  transfers between devices with their start and end apart: 3 -> 4, of which waited for: 3 -> 4; matrix products, arithmetic and copies ran while one was open for 0% -> 0% of each run, Pallas kernels for 21% -> 24%
where the time goes in v1:
time: 87.5 us; the launch traced here: 87 us
  Pallas kernels  48.3 us (55%)
  waiting for transfers between devices  21.9 us (25%)
  starting transfers between devices  15.9 us (18%)
    all_to_all x4, waiting for transfers between devices, exchange(): lax.all_to_all(array, mesh_axes, split_axis=0, concat_axis=0, tiled=True)  21.9 us
    pallas_call x3, Pallas kernels, mix_points(): pl.pallas_call(run, grid=(rows_x // step,), in_specs=specs, out_specs=blo...  18.4 us
    all_to_all x4, starting transfers between devices, exchange(): lax.all_to_all(array, mesh_axes, split_axis=0, concat_axis=0, tiled=True)  15.9 us
    pallas_call x1, Pallas kernels, body(): pl.pallas_call(functools.partial(slope_kernel, per, channels, slabs), in_...  13.1 us
    pallas_call x1, Pallas kernels, body(): pl.pallas_call(functools.partial(plane_kernel, per, channels, slabs), in_...  5.73 us
    pallas_call x1, Pallas kernels, body(): pl.pallas_call(functools.partial(field_kernel, per, channels, slabs), in_...  5.66 us
    pallas_call x1, Pallas kernels, body(): pl.pallas_call(functools.partial(weight_kernel, per, samples), out_shape=...  2.07 us
  transfers between devices with their start and end apart: 4, of which 4 were waited for; matrix products, arithmetic and copies ran while one was open for 0% of the time, Pallas kernels for 24%

profile of v1, /device:TPU:0, one launch (start us, length us, event | category | flops | bytes accessed | tf_op | source)
XLA Modules:
  0.0 87.0 jit_solution(638949167058670439)
XLA Ops:
  0.6 0.0 copy-start.9
  0.6 0.0 copy-start.12
  0.6 5.7 %shard_map.158 = bf16[32,16,256]{2,1,0:T(8,128)(2,1)} custom-call(bf16[1,64,8,48,128]{4,3,2,1,0:T(8,128)(2,1)} %field.1, f32[128,256]{1,0:T(8,128)} %constant.20.clone.base_far.base, bf16[256,768]{1,0:T(8,128)(2,1)} %constant.21.clone.ytab_far.ytab), custom_call_target="tpu_custom_call" | custom-call | flops 1610612736 | bytes 6291456 | tf_op jit(solution)/shard_map/pallas_call | solution.py:657
  6.4 0.0 copy-start
  6.4 0.0 copy-start.7
  6.4 0.0 copy-start.8
  6.4 7.3 %all-to-all-start = ((bf16[32,16,256]{2,1,0:T(8,128)(2,1)}), bf16[32,16,256]{2,1,0:T(8,128)(2,1)S(1)}, u32[]{:S(2)}, u32[]{:S(2)}) async-start(bf16[32,16,256]{2,1,0:T(8,128)(2,1)} %shard_map.158), calls=%async_computation | async-start | bytes 524288 | tf_op jit(solution)/shard_map/all_to_all | solution.py:628
  13.7 0.0 copy-done.9
  13.7 0.0 copy-done.12
  13.8 5.1 %shard_map.159.local_low = bf16[64,4,48,128]{3,2,1,0:T(8,128)(2,1)} custom-call(bf16[64,8,48,128]{3,2,1,0:T(8,128)(2,1)} %bitcast.1, bf16[64,64]{1,0:T(8,128)(2,1)S(1)} %copy-done.9, f32[64]{0:T(128)S(1)} %copy-done.12), custom_call_target="tpu_custom_call" | custom-call | flops 1610612736 | bytes 6291456 | tf_op jit(solution)/shard_map/pallas_call | solution.py:643
  18.9 0.0 copy-start.4
  18.9 0.0 copy-start.10
  18.9 0.0 copy-start.11
  18.9 5.4 %all-to-all-done.arrived = bf16[32,16,256]{2,1,0:T(8,128)(2,1)S(1)} async-done(((bf16[32,16,256]{2,1,0:T(8,128)(2,1)}), bf16[32,16,256]{2,1,0:T(8,128)(2,1)S(1)}, u32[]{:S(2)}, u32[]{:S(2)}) %all-to-all-start) | async-done | bytes 262176 | tf_op jit(solution)/shard_map/all_to_all | solution.py:628
  24.3 0.0 copy-done
  24.3 0.0 copy-done.8
  24.3 1.7 %shard_map.160 = (bf16[256,256]{1,0:T(8,128)(2,1)S(1)}, bf16[32,16,256]{2,1,0:T(8,128)(2,1)}) custom-call(bf16[32,16,256]{2,1,0:T(8,128)(2,1)S(1)} %all-to-all-done.arrived, bf16[64,64,128]{2,1,0:T(8,128)(2,1)S(1)} %copy-done, bf16[256,512]{1,0:T(8,128)(2,1)S(1)} %copy-done.8, bf16[512,256]{1,0:T(8,128)(2,1)S(1)} %copy-done.7), custom_call_target="tpu_custom_call" | custom-call | flops 100000000 | bytes 1048576 | tf_op jit(solution)/shard_map/pallas_call | solution.py:680
  26.1 2.6 %all-to-all-start.1 = ((bf16[32,16,256]{2,1,0:T(8,128)(2,1)}), bf16[32,16,256]{2,1,0:T(8,128)(2,1)S(1)}, u32[]{:S(2)}, u32[]{:S(2)}) async-start(bf16[32,16,256]{2,1,0:T(8,128)(2,1)} %get-tuple-element.20), calls=%async_computation.1 | async-start | bytes 524288 | tf_op jit(solution)/shard_map/all_to_all | solution.py:628
  28.6 5.1 %shard_map.161.local_high = bf16[64,4,48,128]{3,2,1,0:T(8,128)(2,1)} custom-call(bf16[64,8,48,128]{3,2,1,0:T(8,128)(2,1)} %bitcast.2, bf16[64,64]{1,0:T(8,128)(2,1)S(1)} %copy-done.9, f32[64]{0:T(128)S(1)} %copy-done.12), custom_call_target="tpu_custom_call" | custom-call | flops 1610612736 | bytes 6291456 | tf_op jit(solution)/shard_map/pallas_call | solution.py:643
  33.7 5.5 %all-to-all-done.1.arrived = bf16[32,16,256]{2,1,0:T(8,128)(2,1)S(1)} async-done(((bf16[32,16,256]{2,1,0:T(8,128)(2,1)}), bf16[32,16,256]{2,1,0:T(8,128)(2,1)S(1)}, u32[]{:S(2)}, u32[]{:S(2)}) %all-to-all-start.1) | async-done | bytes 262176 | tf_op jit(solution)/shard_map/all_to_all | solution.py:628
  39.3 13.1 %shard_map.162 = (bf16[64,8,48,128]{3,2,1,0:T(8,128)(2,1)}, bf16[32,16,256]{2,1,0:T(8,128)(2,1)}) custom-call(bf16[32,16,256]{2,1,0:T(8,128)(2,1)S(1)} %all-to-all-done.1.arrived, bf16[64,4,48,128]{3,2,1,0:T(8,128)(2,1)} %shard_map.159.local_low, bf16[64,4,48,128]{3,2,1,0:T(8,128)(2,1)} %shard_map.161.local_high, bf16[1,64,8,48,128]{4,3,2,1,0:T(8,128)(2,1)} %cotangent.1, ...), custom_call_target="tpu_custom_call" | custom-call | flops 3221225472 | bytes 18874368 | tf_op jit(solution)/shard_map/pallas_call | solution.py:690
  52.4 2.6 %all-to-all-start.2 = ((bf16[32,16,256]{2,1,0:T(8,128)(2,1)}), bf16[32,16,256]{2,1,0:T(8,128)(2,1)S(1)}, u32[]{:S(2)}, u32[]{:S(2)}) async-start(bf16[32,16,256]{2,1,0:T(8,128)(2,1)} %get-tuple-element.23), calls=%async_computation.2 | async-start | bytes 524288 | tf_op jit(solution)/shard_map/all_to_all | solution.py:628
  55.0 0.0 copy-start.5
  55.0 0.0 copy-start.6
  55.0 8.2 %shard_map.163.local = bf16[64,8,48,128]{3,2,1,0:T(8,128)(2,1)} custom-call(bf16[64,8,48,128]{3,2,1,0:T(8,128)(2,1)} %get-tuple-element.24.a, bf16[64,64]{1,0:T(8,128)(2,1)S(1)} %copy-done.9), custom_call_target="tpu_custom_call" | custom-call | flops 3221225472 | bytes 12582912 | tf_op jit(solution)/shard_map/pallas_call | solution.py:643
  63.2 2.4 %all-to-all-done.2.arrived = bf16[32,16,256]{2,1,0:T(8,128)(2,1)S(1)} async-done(((bf16[32,16,256]{2,1,0:T(8,128)(2,1)}), bf16[32,16,256]{2,1,0:T(8,128)(2,1)S(1)}, u32[]{:S(2)}, u32[]{:S(2)}) %all-to-all-start.2) | async-done | bytes 262176 | tf_op jit(solution)/shard_map/all_to_all | solution.py:628
  65.6 0.0 copy-done.5
  65.6 1.7 %shard_map.164 = (bf16[256,512]{1,0:T(8,128)(2,1)S(1)}, bf16[32,16,256]{2,1,0:T(8,128)(2,1)}) custom-call(bf16[32,16,256]{2,1,0:T(8,128)(2,1)S(1)} %all-to-all-done.2.arrived, bf16[64,64,128]{2,1,0:T(8,128)(2,1)S(1)} %copy-done, bf16[256,512]{1,0:T(8,128)(2,1)S(1)} %copy-done.6, bf16[512,256]{1,0:T(8,128)(2,1)S(1)} %copy-done.5), custom_call_target="tpu_custom_call" | custom-call | flops 100000000 | bytes 1048576 | tf_op jit(solution)/shard_map/pallas_call | solution.py:706
  67.3 3.4 %all-to-all-start.3 = ((bf16[32,16,256]{2,1,0:T(8,128)(2,1)}), bf16[32,16,256]{2,1,0:T(8,128)(2,1)S(1)}, u32[]{:S(2)}, u32[]{:S(2)}) async-start(bf16[32,16,256]{2,1,0:T(8,128)(2,1)} %get-tuple-element.26), calls=%async_computation.3 | async-start | bytes 524288 | tf_op jit(solution)/shard_map/all_to_all | solution.py:628
  70.7 2.1 %shard_map.166 = f32[64,64,128]{2,1,0:T(8,128)} custom-call(bf16[256,256]{1,0:T(8,128)(2,1)S(1)} %get-tuple-element.28.spec_in, bf16[256,512]{1,0:T(8,128)(2,1)S(1)} %get-tuple-element.29.pairs), custom_call_target="tpu_custom_call" | custom-call | flops 100000000 | bytes 2097152 | tf_op jit(solution)/shard_map/pallas_call | solution.py:714
  72.8 8.5 %all-to-all-done.3.arrived = bf16[32,16,256]{2,1,0:T(8,128)(2,1)S(1)} async-done(((bf16[32,16,256]{2,1,0:T(8,128)(2,1)}), bf16[32,16,256]{2,1,0:T(8,128)(2,1)S(1)}, u32[]{:S(2)}, u32[]{:S(2)}) %all-to-all-start.3) | async-done | bytes 262176 | tf_op jit(solution)/shard_map/all_to_all | solution.py:628
  81.3 5.7 %shard_map.165 = bf16[1,64,8,48,128]{4,3,2,1,0:T(8,128)(2,1)} custom-call(bf16[32,16,256]{2,1,0:T(8,128)(2,1)S(1)} %all-to-all-done.3.arrived, bf16[64,8,48,128]{3,2,1,0:T(8,128)(2,1)} %shard_map.163.local, f32[256,128]{1,0:T(8,128)S(1)} %copy-done.3, bf16[768,256]{1,0:T(8,128)(2,1)S(1)} %copy-done.1), custom_call_target="tpu_custom_call" | custom-call | flops 1610612736 | bytes 12582912 | tf_op jit(solution)/shard_map/pallas_call | solution.py:720
  (11 shorter events, 0.0 us)
Async XLA Ops:
  0.6 13.1 %copy-start.9 = (bf16[64,64]{1,0:T(8,128)(2,1)S(1)}, bf16[64,64]{1,0:T(8,128)(2,1)}, u32[]{:S(2)}) copy-start(bf16[64,64]{1,0:T(8,128)(2,1)} %b.1) | copy-start | bytes 24580
  0.6 13.1 %copy-start.12 = (f32[64]{0:T(128)S(1)}, f32[64]{0:T(128)}, u32[]{:S(2)}) copy-start(f32[64]{0:T(128)} %offsets.3) | copy-start | bytes 772
  6.4 17.9 %copy-start = (bf16[64,64,128]{2,1,0:T(8,128)(2,1)S(1)}, bf16[64,64,128]{2,1,0:T(8,128)(2,1)}, u32[]{:S(2)}) copy-start(bf16[64,64,128]{2,1,0:T(8,128)(2,1)} %weights.3) | copy-start | bytes 3145732
  6.4 17.9 %copy-start.7 = (bf16[512,256]{1,0:T(8,128)(2,1)S(1)}, bf16[512,256]{1,0:T(8,128)(2,1)}, u32[]{:S(2)}) copy-start(bf16[512,256]{1,0:T(8,128)(2,1)} %constant.23.clone.line_back) | copy-start | bytes 786436
  6.4 17.9 %copy-start.8 = (bf16[256,512]{1,0:T(8,128)(2,1)S(1)}, bf16[256,512]{1,0:T(8,128)(2,1)}, u32[]{:S(2)}) copy-start(bf16[256,512]{1,0:T(8,128)(2,1)} %constant.22.clone.line) | copy-start | bytes 786436
  6.4 17.9 %all-to-all-start = ((bf16[32,16,256]{2,1,0:T(8,128)(2,1)}), bf16[32,16,256]{2,1,0:T(8,128)(2,1)S(1)}, u32[]{:S(2)}, u32[]{:S(2)}) async-start(bf16[32,16,256]{2,1,0:T(8,128)(2,1)} %shard_map.158), calls=%async_computation | async-start | bytes 524288 | tf_op jit(solution)/shard_map/all_to_all | solution.py:628
  18.9 20.4 %copy-start.1 = (bf16[768,256]{1,0:T(8,128)(2,1)S(1)}, bf16[768,256]{1,0:T(8,128)(2,1)}, u32[]{:S(2)}) copy-start(bf16[768,256]{1,0:T(8,128)(2,1)} %constant.25.clone.ytab_back) | copy-start | bytes 1179652
  18.9 20.4 %copy-start.2 = (bf16[256,768]{1,0:T(8,128)(2,1)S(1)}, bf16[256,768]{1,0:T(8,128)(2,1)}, u32[]{:S(2)}) copy-start(bf16[256,768]{1,0:T(8,128)(2,1)} %constant.21.clone.ytab_far.ytab) | copy-start | bytes 1179652
  18.9 20.4 %copy-start.3 = (f32[256,128]{1,0:T(8,128)S(1)}, f32[256,128]{1,0:T(8,128)}, u32[]{:S(2)}) copy-start(f32[256,128]{1,0:T(8,128)} %constant.24.clone.base_back) | copy-start | bytes 393220
  18.9 20.4 %copy-start.4 = (f32[128,256]{1,0:T(8,128)S(1)}, f32[128,256]{1,0:T(8,128)}, u32[]{:S(2)}) copy-start(f32[128,256]{1,0:T(8,128)} %constant.20.clone.base_far.base) | copy-start | bytes 393220
  18.9 20.4 %copy-start.10 = (f32[1,512]{1,0:T(1,128)S(1)}, f32[1,512]{1,0:T(1,128)}, u32[]{:S(2)}) copy-start(f32[1,512]{1,0:T(1,128)} %constant.27.clone.scale_back) | copy-start | bytes 6148
  18.9 20.4 %copy-start.11 = (f32[1,512]{1,0:T(1,128)S(1)}, f32[1,512]{1,0:T(1,128)}, u32[]{:S(2)}) copy-start(f32[1,512]{1,0:T(1,128)} %constant.26.clone.scale) | copy-start | bytes 6148
  26.1 13.2 %all-to-all-start.1 = ((bf16[32,16,256]{2,1,0:T(8,128)(2,1)}), bf16[32,16,256]{2,1,0:T(8,128)(2,1)S(1)}, u32[]{:S(2)}, u32[]{:S(2)}) async-start(bf16[32,16,256]{2,1,0:T(8,128)(2,1)} %get-tuple-element.20), calls=%async_computation.1 | async-start | bytes 524288 | tf_op jit(solution)/shard_map/all_to_all | solution.py:628
  52.4 13.2 %all-to-all-start.2 = ((bf16[32,16,256]{2,1,0:T(8,128)(2,1)}), bf16[32,16,256]{2,1,0:T(8,128)(2,1)S(1)}, u32[]{:S(2)}, u32[]{:S(2)}) async-start(bf16[32,16,256]{2,1,0:T(8,128)(2,1)} %get-tuple-element.23), calls=%async_computation.2 | async-start | bytes 524288 | tf_op jit(solution)/shard_map/all_to_all | solution.py:628
  55.0 10.6 %copy-start.5 = (bf16[512,256]{1,0:T(8,128)(2,1)S(1)}, bf16[512,256]{1,0:T(8,128)(2,1)}, u32[]{:S(2)}) copy-start(bf16[512,256]{1,0:T(8,128)(2,1)} %constant.29.clone.line_back) | copy-start | bytes 786436
  55.0 10.6 %copy-start.6 = (bf16[256,512]{1,0:T(8,128)(2,1)S(1)}, bf16[256,512]{1,0:T(8,128)(2,1)}, u32[]{:S(2)}) copy-start(bf16[256,512]{1,0:T(8,128)(2,1)} %constant.28.clone.line) | copy-start | bytes 786436
  67.3 14.0 %all-to-all-start.3 = ((bf16[32,16,256]{2,1,0:T(8,128)(2,1)}), bf16[32,16,256]{2,1,0:T(8,128)(2,1)S(1)}, u32[]{:S(2)}, u32[]{:S(2)}) async-start(bf16[32,16,256]{2,1,0:T(8,128)(2,1)} %get-tuple-element.26), calls=%async_computation.3 | async-start | bytes 524288 | tf_op jit(solution)/shard_map/all_to_all | solution.py:628

commit v2 on v0

--- a/solution.py
+++ b/solution.py
@@ -215,7 +215,7 @@
 
 
 def doubled_slope(u):
-    decay = jnp.exp(-(u * u)).astype(BF16)
+    decay = jnp.exp2(u * u * -math.log2(math.e)).astype(BF16)
     cdf = (1.0 + lax.erf(u)).astype(BF16)
     return cdf + u.astype(BF16) * jnp.asarray(2.0 / math.sqrt(math.pi), BF16) * decay
 
@@ -310,20 +310,16 @@
 class Move:
     def __init__(self, source, target, sems):
         self.source, self.target, self.sems = source, target, sems
-        self.groups = target.shape[0] // GROUP
-
-    def copy(self, step, g):
-        run = pl.ds(g * GROUP + step * SLOTS, SLOTS)
-        sem = self.sems.at[step * self.groups + g]
-        return pltpu.make_async_copy(self.source.at[run], self.target.at[run], sem)
+
+    def copy(self, step):
+        run = pl.ds(step * SLOTS, SLOTS)
+        return pltpu.make_async_copy(self.source.at[:, run], self.target.at[:, run], self.sems.at[step])
 
     def start(self, step):
-        for g in range(self.groups):
-            self.copy(step, g).start()
+        self.copy(step).start()
 
     def wait(self, step):
-        for g in range(self.groups):
-            self.copy(step, g).wait()
+        self.copy(step).wait()
 
 
 def start_all(moves, step):
@@ -332,13 +328,13 @@
 
 
 def add_spectra(field, ztab, step, spectra):
-    groups = field.shape[0] // GROUP
+    groups = field.shape[0]
     rows_z = field.shape[-1]
     depth = SLOTS * rows_z
     table = ztab[pl.ds(pl.multiple_of(step * depth, depth), depth)]
     lanes = [
         jnp.concatenate(
-            [field[g * GROUP + step * SLOTS + slot].reshape(-1, rows_z) for g in range(groups)], axis=0
+            [field[g, step * SLOTS + slot].reshape(-1, rows_z) for g in range(groups)], axis=0
         )
         for slot in range(SLOTS)
     ]
@@ -348,7 +344,7 @@
 def plane_kernel(
     per, channels, slabs, field, base_far, ytab_far, message, ztab, order, spectra, buffer, base, ytab, sems, table_sems
 ):
-    incoming = Move(field.at[0], buffer, sems)
+    incoming = Move(field, buffer, sems)
     base_copy = pltpu.make_async_copy(base_far, base, table_sems.at[0])
     ytab_copy = pltpu.make_async_copy(ytab_far, ytab, table_sems.at[1])
     base_copy.start()
@@ -376,11 +372,11 @@
     slope, message, ztab, ztab_back, order, held, spectra, local_in, cotangent_in, result, total,
     local_sems, cotangent_sems, result_sems,
 ):
-    width, rows_y, rows_z = local.shape[1:]
+    width, rows_y, rows_z = local.shape[2:]
     groups = channels // GROUP
     rows = width * rows_y
     wide = 2 * rows_y
-    incoming = (Move(local, local_in, local_sems), Move(cotangent.at[0], cotangent_in, cotangent_sems))
+    incoming = (Move(local, local_in, local_sems), Move(cotangent, cotangent_in, cotangent_sems))
     outgoing = Move(result, slope, result_sems)
     start_all(incoming, 0)
     fill_order(per, channels, True, order)
@@ -401,15 +397,15 @@
         for g in range(groups):
             for slot in range(SLOTS):
                 lanes = slice(slot * rows_z, (slot + 1) * rows_z)
-                c = g * GROUP + step * SLOTS + slot
+                c = step * SLOTS + slot
                 for x in range(0, width, 2):
                     place = g * rows + x * rows_y
                     value = total[place : place + wide, lanes]
-                    value = value + local_in[c, x : x + 2].reshape(wide, rows_z).astype(F32)
-                    upstream = cotangent_in[c, x : x + 2].reshape(wide, rows_z)
+                    value = value + local_in[g, c, x : x + 2].reshape(wide, rows_z).astype(F32)
+                    upstream = cotangent_in[g, c, x : x + 2].reshape(wide, rows_z)
                     answer = upstream * doubled_slope(value)
-                    result[c, x : x + 2] = answer.reshape(2, rows_y, rows_z)
-            outgoing.copy(step, g).start()
+                    result[g, c, x : x + 2] = answer.reshape(2, rows_y, rows_z)
+        outgoing.start(step)
         add_spectra(result, ztab, step, spectra)
 
     deliver(spectra, ytab, order, scale, message, per, channels, slabs)
@@ -421,11 +417,11 @@
     per, channels, slabs, arrived, local, base_back, ytab_back, out, ztab_back, order, held, local_in, result,
     local_sems, result_sems,
 ):
-    width, rows_y, rows_z = local.shape[1:]
+    width, rows_y, rows_z = local.shape[2:]
     groups = channels // GROUP
     rows = width * rows_y
     incoming = Move(local, local_in, local_sems)
-    outgoing = Move(result, out.at[0], result_sems)
+    outgoing = Move(result, out, result_sems)
     incoming.start(0)
     fill_order(per, channels, True, order)
     incoming.start(1)
@@ -441,11 +437,11 @@
         for g in range(groups):
             for slot in range(SLOTS):
                 lanes = slice(slot * rows_z, (slot + 1) * rows_z)
-                c = g * GROUP + step * SLOTS + slot
+                c = step * SLOTS + slot
                 value = total[g * rows : (g + 1) * rows, lanes]
-                value = value + local_in[c].reshape(rows, rows_z).astype(F32)
-                result[c] = value.astype(BF16).reshape(width, rows_y, rows_z)
-            outgoing.copy(step, g).start()
+                value = value + local_in[g, c].reshape(rows, rows_z).astype(F32)
+                result[g, c] = value.astype(BF16).reshape(width, rows_y, rows_z)
+        outgoing.start(step)
 
     for step in range(STEPS):
         outgoing.wait(step)
@@ -530,11 +526,14 @@
     rows = 2 * samples
     lanes = 2 * weights.shape[1]
     low = low_half((samples, lanes))
+    first_lanes = jnp.where(low_half((lanes, lanes)), 1.0, 0.0).astype(BF16)
+    second_lanes = jnp.where(low_half((lanes, lanes)), 0.0, 1.0).astype(BF16)
     flat = arrived[...].reshape(-1, arrived.shape[2])
     spectra = dot(line[...], flat).astype(BF16).astype(F32)
     for q in range(MX):
         for first in range(0, per, 2):
-            block = spread_pair(weights[first * MX + q], weights[(first + 1) * MX + q])
+            both = jnp.concatenate([weights[first * MX + q], weights[(first + 1) * MX + q]], axis=0).T
+            block = jnp.concatenate([both * first_lanes, both * second_lanes], axis=0)
             place = first // 2 * lanes
             real = spectra[q * rows : q * rows + samples, place : place + lanes]
             imag = spectra[q * rows + samples : (q + 1) * rows, place : place + lanes]
@@ -546,9 +545,7 @@
                 [jnp.concatenate(left, axis=0), jnp.concatenate(right, axis=0)], axis=1
             ).astype(BF16)
             pairs[q * rows : (q + 1) * rows, 2 * place : 2 * (place + lanes)] = pair
-            held[q * rows : (q + 1) * rows, place : place + lanes] = lax.dot_general(
-                pair, block, (((1,), (1,)), ((), ())), preferred_element_type=F32
-            ).astype(BF16)
+            held[q * rows : (q + 1) * rows, place : place + lanes] = dot(pair, block).astype(BF16)
     message[...] = dot(line_back[...], held[...]).astype(BF16).reshape(message.shape)
 
 
@@ -608,8 +605,9 @@
     held = pltpu.VMEM((rows, 2 * MZ * GROUP), BF16)
     sums = pltpu.VMEM((rows, 2 * MZ * GROUP), F32)
     slot_sums = pltpu.VMEM((rows, SLOTS * rows_z), F32)
-    buffer = pltpu.VMEM(field, BF16)
-    sems = pltpu.SemaphoreType.DMA((STEPS * groups,))
+    grouped_field = (groups, GROUP) + field[1:]
+    buffer = pltpu.VMEM(grouped_field, BF16)
+    sems = pltpu.SemaphoreType.DMA((STEPS,))
     far = pl.BlockSpec(memory_space=pltpu.HBM)
     far_field = pltpu.HBM(field, BF16)
 
@@ -664,7 +662,7 @@
         ],
         compiler_params=params(32),
         cost_estimate=cost(plane_flops, 2 * count),
-    )(kept_far(activations), kept_far(base), kept_far(ytab))
+    )(kept_far(activations.reshape(grouped_field)), kept_far(base), kept_far(ytab))
     arrived = exchange(planes)
     local = mix_points(kept_far(activations.reshape(field)), True, offsets)
     arrived, local = lax.optimization_barrier((arrived, local))
@@ -681,16 +679,16 @@
         in_specs=[whole(message), far, far]
         + [whole(t) for t in (base, base_t, ytab, ytab_t, scale, scale_t)],
         out_specs=(far, whole(message)),
-        out_shape=(far_field, message),
+        out_shape=(pltpu.HBM(grouped_field, BF16), message),
         scratch_shapes=[ztab, ztab_t, order, held, sums]
         + [buffer] * 3
         + [slot_sums]
         + [sems] * 3,
         compiler_params=params(40),
         cost_estimate=cost(2 * plane_flops, 6 * count, 2 * count),
-    )(returned, kept_far(local), kept_far(cotangent), base, base_t, ytab, ytab_t, scale, scale_t)
+    )(returned, kept_far(local.reshape(grouped_field)), kept_far(cotangent.reshape(grouped_field)), base, base_t, ytab, ytab_t, scale, scale_t)
     arrived_back = exchange(back_plane)
-    local_back = mix_points(kept_far(slope), False, None)
+    local_back = mix_points(kept_far(slope.reshape(field)), False, None)
     arrived_back, local_back = lax.optimization_barrier((arrived_back, local_back))
     pairs, mixed_back = pl.pallas_call(
         functools.partial(mix_back_kernel, per, samples),
@@ -710,12 +708,12 @@
         functools.partial(field_kernel, per, channels, slabs),
         in_specs=[whole(message), far, whole(base_t), whole(ytab_t)],
         out_specs=far,
-        out_shape=shaped(activations.shape, BF16),
+        out_shape=shaped(grouped_field, BF16),
         scratch_shapes=[ztab_t, order, held, buffer, buffer, sems, sems],
         compiler_params=params(32),
         cost_estimate=cost(plane_flops, 4 * count),
-    )(returned_back, kept_far(local_back), base_t, ytab_t)
-    return (grad_in, grad_spectral)
+    )(returned_back, kept_far(local_back.reshape(grouped_field)), base_t, ytab_t)
+    return (grad_in.reshape(activations.shape), grad_spectral)
 
 
 def chosen_body(mesh_axes, devices, slabs, activations, cotangent, mode_weights, pointwise, offsets):

time: 87.1 us -> 86.4 us (level)
  transfers between devices with their start and end apart: 3 -> 3, of which waited for: 3 -> 3; matrix products, arithmetic and copies ran while one was open for 0% -> 0% of each run, Pallas kernels for 21% -> 22%
where the time goes in v2:
time: 86.4 us; the launch traced here: 86 us
  Pallas kernels  44.6 us (52%)
  blocking collectives  14.1 us (16%)
  starting transfers between devices  13.3 us (15%)
  waiting for transfers between devices  13.1 us (15%)
    pallas_call x2, Pallas kernels, mix_points(): pl.pallas_call(run, grid=(width // step,), in_specs=specs, out_specs=bloc...  16.4 us
    all_to_all x1, blocking collectives, exchange(): lax.all_to_all(array, mesh_axes, split_axis=0, concat_axis=0, tiled=True)  14.1 us
    all_to_all x3, starting transfers between devices, exchange(): lax.all_to_all(array, mesh_axes, split_axis=0, concat_axis=0, tiled=True)  13.3 us
    all_to_all x3, waiting for transfers between devices, exchange(): lax.all_to_all(array, mesh_axes, split_axis=0, concat_axis=0, tiled=True)  13.1 us
    pallas_call x1, Pallas kernels, body(): pl.pallas_call(functools.partial(slope_kernel, per, channels, slabs), in_...  12.4 us
    pallas_call x1, Pallas kernels, body(): pl.pallas_call(functools.partial(field_kernel, per, channels, slabs), in_...  5.6 us
    pallas_call x1, Pallas kernels, body(): pl.pallas_call(functools.partial(plane_kernel, per, channels, slabs), in_...  5.43 us
    pallas_call x1, Pallas kernels, body(): pl.pallas_call(functools.partial(weight_kernel, per, samples), out_shape=...  2.07 us
  transfers between devices with their start and end apart: 3, of which 3 were waited for; matrix products, arithmetic and copies ran while one was open for 0% of the time, Pallas kernels for 22%

profile of v2, /device:TPU:0, one launch (start us, length us, event | category | flops | bytes accessed | tf_op | source)
XLA Modules:
  0.0 86.0 jit_solution(4772346999316722205)
XLA Ops:
  0.6 0.0 copy-start.9
  0.6 0.0 copy-start.12
  0.6 5.4 %shard_map.158 = bf16[32,16,256]{2,1,0:T(8,128)(2,1)} custom-call(bf16[4,16,8,48,128]{4,3,2,1,0:T(8,128)(2,1)} %bitcast.7, f32[128,256]{1,0:T(8,128)} %constant.20.clone.base_far.base, bf16[256,768]{1,0:T(8,128)(2,1)} %constant.21.clone.ytab_far.ytab), custom_call_target="tpu_custom_call" | custom-call | flops 1610612736 | bytes 6291456 | tf_op jit(solution)/shard_map/pallas_call | solution.py:648
  6.1 7.3 %all-to-all-start = ((bf16[32,16,256]{2,1,0:T(8,128)(2,1)}), bf16[32,16,256]{2,1,0:T(8,128)(2,1)S(1)}, u32[]{:S(2)}, u32[]{:S(2)}) async-start(bf16[32,16,256]{2,1,0:T(8,128)(2,1)} %shard_map.158), calls=%async_computation | async-start | bytes 524288 | tf_op jit(solution)/shard_map/all_to_all | solution.py:620
  13.4 0.0 copy-done.9
  13.4 0.0 copy-done.12
  13.4 0.0 copy-start
  13.4 0.0 copy-start.7
  13.4 0.0 copy-start.8
  13.4 0.0 copy-start.1
  13.5 0.0 copy-start.2
  13.5 0.0 copy-start.3
  13.5 0.0 copy-start.4
  13.5 0.0 copy-start.10
  13.5 0.0 copy-start.11
  13.5 8.3 %shard_map.159 = bf16[64,8,48,128]{3,2,1,0:T(8,128)(2,1)} custom-call(bf16[64,8,48,128]{3,2,1,0:T(8,128)(2,1)} %bitcast.8, bf16[64,64]{1,0:T(8,128)(2,1)S(1)} %copy-done.9, f32[64]{0:T(128)S(1)} %copy-done.12), custom_call_target="tpu_custom_call" | custom-call | flops 3221225472 | bytes 12582912 | tf_op jit(solution)/shard_map/pallas_call | solution.py:634
  21.8 2.2 %all-to-all-done.arrived = bf16[32,16,256]{2,1,0:T(8,128)(2,1)S(1)} async-done(((bf16[32,16,256]{2,1,0:T(8,128)(2,1)}), bf16[32,16,256]{2,1,0:T(8,128)(2,1)S(1)}, u32[]{:S(2)}, u32[]{:S(2)}) %all-to-all-start) | async-done | bytes 262176 | tf_op jit(solution)/shard_map/all_to_all | solution.py:620
  24.0 1.0 %shard_map.160 = (bf16[256,256]{1,0:T(8,128)(2,1)S(1)}, bf16[32,16,256]{2,1,0:T(8,128)(2,1)S(1)}) custom-call(bf16[32,16,256]{2,1,0:T(8,128)(2,1)S(1)} %all-to-all-done.arrived, bf16[64,64,128]{2,1,0:T(8,128)(2,1)S(1)} %copy-done, bf16[256,512]{1,0:T(8,128)(2,1)S(1)} %copy-done.8, bf16[512,256]{1,0:T(8,128)(2,1)S(1)} %copy-done.7), custom_call_target="tpu_custom_call" | custom-call | flops 100000000 | bytes 1048576 | tf_op jit(solution)/shard_map/pallas_call | solution.py:669
  25.0 14.1 %all_to_all.20.arrived = bf16[32,16,256]{2,1,0:T(8,128)(2,1)S(1)} all-to-all(bf16[32,16,256]{2,1,0:T(8,128)(2,1)S(1)} %get-tuple-element.13), channel_id=1, replica_groups=mesh['dp'=8,'space'=4] {'dp','space'}, dimensions={0} | all-to-all | bytes 524288 | tf_op jit(solution)/shard_map/all_to_all | solution.py:620
  39.1 0.0 copy-done.1
  39.1 12.4 %shard_map.161 = (bf16[4,16,8,48,128]{4,3,2,1,0:T(8,128)(2,1)}, bf16[32,16,256]{2,1,0:T(8,128)(2,1)}) custom-call(bf16[32,16,256]{2,1,0:T(8,128)(2,1)S(1)} %all_to_all.20.arrived, bf16[4,16,8,48,128]{4,3,2,1,0:T(8,128)(2,1)} %bitcast.10, bf16[4,16,8,48,128]{4,3,2,1,0:T(8,128)(2,1)} %bitcast.11, f32[128,256]{1,0:T(8,128)S(1)} %copy-done.4, ...), custom_call_target="tpu_custom_call" | custom-call | flops 3221225472 | bytes 18874368 | tf_op jit(solution)/shard_map/pallas_call | solution.py:677
  51.5 2.6 %all-to-all-start.2 = ((bf16[32,16,256]{2,1,0:T(8,128)(2,1)}), bf16[32,16,256]{2,1,0:T(8,128)(2,1)S(1)}, u32[]{:S(2)}, u32[]{:S(2)}) async-start(bf16[32,16,256]{2,1,0:T(8,128)(2,1)} %get-tuple-element.15), calls=%async_computation.2 | async-start | bytes 524288 | tf_op jit(solution)/shard_map/all_to_all | solution.py:620
  54.1 0.0 copy-start.5
  54.1 0.0 copy-start.6
  54.1 8.2 %shard_map.162 = bf16[64,8,48,128]{3,2,1,0:T(8,128)(2,1)} custom-call(bf16[64,8,48,128]{3,2,1,0:T(8,128)(2,1)} %bitcast.12, bf16[64,64]{1,0:T(8,128)(2,1)S(1)} %copy-done.9), custom_call_target="tpu_custom_call" | custom-call | flops 3221225472 | bytes 12582912 | tf_op jit(solution)/shard_map/pallas_call | solution.py:634
  62.3 2.4 %all-to-all-done.2.arrived = bf16[32,16,256]{2,1,0:T(8,128)(2,1)S(1)} async-done(((bf16[32,16,256]{2,1,0:T(8,128)(2,1)}), bf16[32,16,256]{2,1,0:T(8,128)(2,1)S(1)}, u32[]{:S(2)}, u32[]{:S(2)}) %all-to-all-start.2) | async-done | bytes 262176 | tf_op jit(solution)/shard_map/all_to_all | solution.py:620
  64.7 0.0 copy-done.5
  64.7 1.7 %shard_map.163 = (bf16[256,512]{1,0:T(8,128)(2,1)S(1)}, bf16[32,16,256]{2,1,0:T(8,128)(2,1)}) custom-call(bf16[32,16,256]{2,1,0:T(8,128)(2,1)S(1)} %all-to-all-done.2.arrived, bf16[64,64,128]{2,1,0:T(8,128)(2,1)S(1)} %copy-done, bf16[256,512]{1,0:T(8,128)(2,1)S(1)} %copy-done.6, bf16[512,256]{1,0:T(8,128)(2,1)S(1)} %copy-done.5), custom_call_target="tpu_custom_call" | custom-call | flops 100000000 | bytes 1048576 | tf_op jit(solution)/shard_map/pallas_call | solution.py:693
  66.4 3.4 %all-to-all-start.3 = ((bf16[32,16,256]{2,1,0:T(8,128)(2,1)}), bf16[32,16,256]{2,1,0:T(8,128)(2,1)S(1)}, u32[]{:S(2)}, u32[]{:S(2)}) async-start(bf16[32,16,256]{2,1,0:T(8,128)(2,1)} %get-tuple-element.18), calls=%async_computation.3 | async-start | bytes 524288 | tf_op jit(solution)/shard_map/all_to_all | solution.py:620
  69.8 2.1 %shard_map.165 = f32[64,64,128]{2,1,0:T(8,128)} custom-call(bf16[256,256]{1,0:T(8,128)(2,1)S(1)} %get-tuple-element.20.spec_in, bf16[256,512]{1,0:T(8,128)(2,1)S(1)} %get-tuple-element.21.pairs), custom_call_target="tpu_custom_call" | custom-call | flops 100000000 | bytes 2097152 | tf_op jit(solution)/shard_map/pallas_call | solution.py:701
  71.9 8.5 %all-to-all-done.3.arrived = bf16[32,16,256]{2,1,0:T(8,128)(2,1)S(1)} async-done(((bf16[32,16,256]{2,1,0:T(8,128)(2,1)}), bf16[32,16,256]{2,1,0:T(8,128)(2,1)S(1)}, u32[]{:S(2)}, u32[]{:S(2)}) %all-to-all-start.3) | async-done | bytes 262176 | tf_op jit(solution)/shard_map/all_to_all | solution.py:620
  80.4 5.6 %shard_map.164 = bf16[4,16,8,48,128]{4,3,2,1,0:T(8,128)(2,1)} custom-call(bf16[32,16,256]{2,1,0:T(8,128)(2,1)S(1)} %all-to-all-done.3.arrived, bf16[4,16,8,48,128]{4,3,2,1,0:T(8,128)(2,1)} %bitcast.9, f32[256,128]{1,0:T(8,128)S(1)} %copy-done.3, bf16[768,256]{1,0:T(8,128)(2,1)S(1)} %copy-done.1), custom_call_target="tpu_custom_call" | custom-call | flops 1610612736 | bytes 12582912 | tf_op jit(solution)/shard_map/pallas_call | solution.py:707
  (9 shorter events, 0.0 us)
Async XLA Ops:
  0.6 12.8 %copy-start.9 = (bf16[64,64]{1,0:T(8,128)(2,1)S(1)}, bf16[64,64]{1,0:T(8,128)(2,1)}, u32[]{:S(2)}) copy-start(bf16[64,64]{1,0:T(8,128)(2,1)} %b.1) | copy-start | bytes 24580
  0.6 12.8 %copy-start.12 = (f32[64]{0:T(128)S(1)}, f32[64]{0:T(128)}, u32[]{:S(2)}) copy-start(f32[64]{0:T(128)} %offsets.1) | copy-start | bytes 772
  6.1 17.9 %all-to-all-start = ((bf16[32,16,256]{2,1,0:T(8,128)(2,1)}), bf16[32,16,256]{2,1,0:T(8,128)(2,1)S(1)}, u32[]{:S(2)}, u32[]{:S(2)}) async-start(bf16[32,16,256]{2,1,0:T(8,128)(2,1)} %shard_map.158), calls=%async_computation | async-start | bytes 524288 | tf_op jit(solution)/shard_map/all_to_all | solution.py:620
  13.4 10.6 %copy-start = (bf16[64,64,128]{2,1,0:T(8,128)(2,1)S(1)}, bf16[64,64,128]{2,1,0:T(8,128)(2,1)}, u32[]{:S(2)}) copy-start(bf16[64,64,128]{2,1,0:T(8,128)(2,1)} %weights.3) | copy-start | bytes 3145732
  13.4 10.6 %copy-start.7 = (bf16[512,256]{1,0:T(8,128)(2,1)S(1)}, bf16[512,256]{1,0:T(8,128)(2,1)}, u32[]{:S(2)}) copy-start(bf16[512,256]{1,0:T(8,128)(2,1)} %constant.23.clone.line_back) | copy-start | bytes 786436
  13.4 10.6 %copy-start.8 = (bf16[256,512]{1,0:T(8,128)(2,1)S(1)}, bf16[256,512]{1,0:T(8,128)(2,1)}, u32[]{:S(2)}) copy-start(bf16[256,512]{1,0:T(8,128)(2,1)} %constant.22.clone.line) | copy-start | bytes 786436
  13.4 25.6 %copy-start.1 = (bf16[768,256]{1,0:T(8,128)(2,1)S(1)}, bf16[768,256]{1,0:T(8,128)(2,1)}, u32[]{:S(2)}) copy-start(bf16[768,256]{1,0:T(8,128)(2,1)} %constant.25.clone.ytab_back) | copy-start | bytes 1179652
  13.5 25.6 %copy-start.2 = (bf16[256,768]{1,0:T(8,128)(2,1)S(1)}, bf16[256,768]{1,0:T(8,128)(2,1)}, u32[]{:S(2)}) copy-start(bf16[256,768]{1,0:T(8,128)(2,1)} %constant.21.clone.ytab_far.ytab) | copy-start | bytes 1179652
  13.5 25.6 %copy-start.3 = (f32[256,128]{1,0:T(8,128)S(1)}, f32[256,128]{1,0:T(8,128)}, u32[]{:S(2)}) copy-start(f32[256,128]{1,0:T(8,128)} %constant.24.clone.base_back) | copy-start | bytes 393220
  13.5 25.6 %copy-start.4 = (f32[128,256]{1,0:T(8,128)S(1)}, f32[128,256]{1,0:T(8,128)}, u32[]{:S(2)}) copy-start(f32[128,256]{1,0:T(8,128)} %constant.20.clone.base_far.base) | copy-start | bytes 393220
  13.5 25.6 %copy-start.10 = (f32[1,512]{1,0:T(1,128)S(1)}, f32[1,512]{1,0:T(1,128)}, u32[]{:S(2)}) copy-start(f32[1,512]{1,0:T(1,128)} %constant.27.clone.scale_back) | copy-start | bytes 6148
  13.5 25.6 %copy-start.11 = (f32[1,512]{1,0:T(1,128)S(1)}, f32[1,512]{1,0:T(1,128)}, u32[]{:S(2)}) copy-start(f32[1,512]{1,0:T(1,128)} %constant.26.clone.scale) | copy-start | bytes 6148
  51.5 13.2 %all-to-all-start.2 = ((bf16[32,16,256]{2,1,0:T(8,128)(2,1)}), bf16[32,16,256]{2,1,0:T(8,128)(2,1)S(1)}, u32[]{:S(2)}, u32[]{:S(2)}) async-start(bf16[32,16,256]{2,1,0:T(8,128)(2,1)} %get-tuple-element.15), calls=%async_computation.2 | async-start | bytes 524288 | tf_op jit(solution)/shard_map/all_to_all | solution.py:620
  54.1 10.6 %copy-start.5 = (bf16[512,256]{1,0:T(8,128)(2,1)S(1)}, bf16[512,256]{1,0:T(8,128)(2,1)}, u32[]{:S(2)}) copy-start(bf16[512,256]{1,0:T(8,128)(2,1)} %constant.29.clone.line_back) | copy-start | bytes 786436
  54.1 10.6 %copy-start.6 = (bf16[256,512]{1,0:T(8,128)(2,1)S(1)}, bf16[256,512]{1,0:T(8,128)(2,1)}, u32[]{:S(2)}) copy-start(bf16[256,512]{1,0:T(8,128)(2,1)} %constant.28.clone.line) | copy-start | bytes 786436
  66.4 14.0 %all-to-all-start.3 = ((bf16[32,16,256]{2,1,0:T(8,128)(2,1)}), bf16[32,16,256]{2,1,0:T(8,128)(2,1)S(1)}, u32[]{:S(2)}, u32[]{:S(2)}) async-start(bf16[32,16,256]{2,1,0:T(8,128)(2,1)} %get-tuple-element.18), calls=%async_computation.3 | async-start | bytes 524288 | tf_op jit(solution)/shard_map/all_to_all | solution.py:620

commit v3 on v2

--- a/solution.py
+++ b/solution.py
@@ -322,6 +322,21 @@
         self.copy(step).wait()
 
 
+class GroupMove(Move):
+    def copy(self, step, g):
+        run = pl.ds(step * SLOTS, SLOTS)
+        sem = self.sems.at[step * self.target.shape[0] + g]
+        return pltpu.make_async_copy(self.source.at[g, run], self.target.at[g, run], sem)
+
+    def start(self, step):
+        for g in range(self.target.shape[0]):
+            self.copy(step, g).start()
+
+    def wait(self, step):
+        for g in range(self.target.shape[0]):
+            self.copy(step, g).wait()
+
+
 def start_all(moves, step):
     for each in moves:
         each.start(step)
@@ -376,8 +391,8 @@
     groups = channels // GROUP
     rows = width * rows_y
     wide = 2 * rows_y
-    incoming = (Move(local, local_in, local_sems), Move(cotangent, cotangent_in, cotangent_sems))
-    outgoing = Move(result, slope, result_sems)
+    incoming = (GroupMove(local, local_in, local_sems), GroupMove(cotangent, cotangent_in, cotangent_sems))
+    outgoing = GroupMove(result, slope, result_sems)
     start_all(incoming, 0)
     fill_order(per, channels, True, order)
     receive(arrived, order, ytab_back, scale_back, held, per, slabs)
@@ -405,7 +420,7 @@
                     upstream = cotangent_in[g, c, x : x + 2].reshape(wide, rows_z)
                     answer = upstream * doubled_slope(value)
                     result[g, c, x : x + 2] = answer.reshape(2, rows_y, rows_z)
-        outgoing.start(step)
+            outgoing.copy(step, g).start()
         add_spectra(result, ztab, step, spectra)
 
     deliver(spectra, ytab, order, scale, message, per, channels, slabs)
@@ -608,6 +623,7 @@
     grouped_field = (groups, GROUP) + field[1:]
     buffer = pltpu.VMEM(grouped_field, BF16)
     sems = pltpu.SemaphoreType.DMA((STEPS,))
+    group_sems = pltpu.SemaphoreType.DMA((STEPS * groups,))
     far = pl.BlockSpec(memory_space=pltpu.HBM)
     far_field = pltpu.HBM(field, BF16)
 
@@ -683,7 +699,7 @@
         scratch_shapes=[ztab, ztab_t, order, held, sums]
         + [buffer] * 3
         + [slot_sums]
-        + [sems] * 3,
+        + [group_sems] * 3,
         compiler_params=params(40),
         cost_estimate=cost(2 * plane_flops, 6 * count, 2 * count),
     )(returned, kept_far(local.reshape(grouped_field)), kept_far(cotangent.reshape(grouped_field)), base, base_t, ytab, ytab_t, scale, scale_t)

time: 86.4 us -> 86 us (level)
  no operation moved by 1% of the time
where the time goes in v3:
time: 86 us; the launch traced here: 85.6 us
  Pallas kernels  44.2 us (51%)
  blocking collectives  14.1 us (16%)
  starting transfers between devices  13.3 us (15%)
  waiting for transfers between devices  13.1 us (15%)
    pallas_call x2, Pallas kernels, mix_points(): pl.pallas_call(run, grid=(width // step,), in_specs=specs, out_specs=bloc...  16.4 us
    all_to_all x1, blocking collectives, exchange(): lax.all_to_all(array, mesh_axes, split_axis=0, concat_axis=0, tiled=True)  14.1 us
    all_to_all x3, starting transfers between devices, exchange(): lax.all_to_all(array, mesh_axes, split_axis=0, concat_axis=0, tiled=True)  13.3 us
    all_to_all x3, waiting for transfers between devices, exchange(): lax.all_to_all(array, mesh_axes, split_axis=0, concat_axis=0, tiled=True)  13.1 us
    pallas_call x1, Pallas kernels, body(): pl.pallas_call(functools.partial(slope_kernel, per, channels, slabs), in_...  11.9 us
    pallas_call x1, Pallas kernels, body(): pl.pallas_call(functools.partial(field_kernel, per, channels, slabs), in_...  5.6 us
    pallas_call x1, Pallas kernels, body(): pl.pallas_call(functools.partial(plane_kernel, per, channels, slabs), in_...  5.43 us
    pallas_call x1, Pallas kernels, body(): pl.pallas_call(functools.partial(weight_kernel, per, samples), out_shape=...  2.07 us
  transfers between devices with their start and end apart: 3, of which 3 were waited for; matrix products, arithmetic and copies ran while one was open for 0% of the time, Pallas kernels for 22%

profile of v3, /device:TPU:0, one launch (start us, length us, event | category | flops | bytes accessed | tf_op | source)
XLA Modules:
  0.0 85.6 jit_solution(3876809106250129047)
XLA Ops:
  0.6 0.0 copy-start.9
  0.6 0.0 copy-start.12
  0.6 5.4 %shard_map.158 = bf16[32,16,256]{2,1,0:T(8,128)(2,1)} custom-call(bf16[4,16,8,48,128]{4,3,2,1,0:T(8,128)(2,1)} %bitcast.7, f32[128,256]{1,0:T(8,128)} %constant.20.clone.base_far.base, bf16[256,768]{1,0:T(8,128)(2,1)} %constant.21.clone.ytab_far.ytab), custom_call_target="tpu_custom_call" | custom-call | flops 1610612736 | bytes 6291456 | tf_op jit(solution)/shard_map/pallas_call | solution.py:664
  6.1 7.3 %all-to-all-start = ((bf16[32,16,256]{2,1,0:T(8,128)(2,1)}), bf16[32,16,256]{2,1,0:T(8,128)(2,1)S(1)}, u32[]{:S(2)}, u32[]{:S(2)}) async-start(bf16[32,16,256]{2,1,0:T(8,128)(2,1)} %shard_map.158), calls=%async_computation | async-start | bytes 524288 | tf_op jit(solution)/shard_map/all_to_all | solution.py:636
  13.4 0.0 copy-done.9
  13.4 0.0 copy-done.12
  13.4 0.0 copy-start
  13.4 0.0 copy-start.7
  13.4 0.0 copy-start.8
  13.4 0.0 copy-start.1
  13.5 0.0 copy-start.2
  13.5 0.0 copy-start.3
  13.5 0.0 copy-start.4
  13.5 0.0 copy-start.10
  13.5 0.0 copy-start.11
  13.5 8.3 %shard_map.159 = bf16[64,8,48,128]{3,2,1,0:T(8,128)(2,1)} custom-call(bf16[64,8,48,128]{3,2,1,0:T(8,128)(2,1)} %bitcast.8, bf16[64,64]{1,0:T(8,128)(2,1)S(1)} %copy-done.9, f32[64]{0:T(128)S(1)} %copy-done.12), custom_call_target="tpu_custom_call" | custom-call | flops 3221225472 | bytes 12582912 | tf_op jit(solution)/shard_map/pallas_call | solution.py:650
  21.8 2.2 %all-to-all-done.arrived = bf16[32,16,256]{2,1,0:T(8,128)(2,1)S(1)} async-done(((bf16[32,16,256]{2,1,0:T(8,128)(2,1)}), bf16[32,16,256]{2,1,0:T(8,128)(2,1)S(1)}, u32[]{:S(2)}, u32[]{:S(2)}) %all-to-all-start) | async-done | bytes 262176 | tf_op jit(solution)/shard_map/all_to_all | solution.py:636
  24.0 1.0 %shard_map.160 = (bf16[256,256]{1,0:T(8,128)(2,1)S(1)}, bf16[32,16,256]{2,1,0:T(8,128)(2,1)S(1)}) custom-call(bf16[32,16,256]{2,1,0:T(8,128)(2,1)S(1)} %all-to-all-done.arrived, bf16[64,64,128]{2,1,0:T(8,128)(2,1)S(1)} %copy-done, bf16[256,512]{1,0:T(8,128)(2,1)S(1)} %copy-done.8, bf16[512,256]{1,0:T(8,128)(2,1)S(1)} %copy-done.7), custom_call_target="tpu_custom_call" | custom-call | flops 100000000 | bytes 1048576 | tf_op jit(solution)/shard_map/pallas_call | solution.py:685
  25.0 14.1 %all_to_all.20.arrived = bf16[32,16,256]{2,1,0:T(8,128)(2,1)S(1)} all-to-all(bf16[32,16,256]{2,1,0:T(8,128)(2,1)S(1)} %get-tuple-element.13), channel_id=1, replica_groups=mesh['dp'=8,'space'=4] {'dp','space'}, dimensions={0} | all-to-all | bytes 524288 | tf_op jit(solution)/shard_map/all_to_all | solution.py:636
  39.1 0.0 copy-done.1
  39.1 11.9 %shard_map.161 = (bf16[4,16,8,48,128]{4,3,2,1,0:T(8,128)(2,1)}, bf16[32,16,256]{2,1,0:T(8,128)(2,1)}) custom-call(bf16[32,16,256]{2,1,0:T(8,128)(2,1)S(1)} %all_to_all.20.arrived, bf16[4,16,8,48,128]{4,3,2,1,0:T(8,128)(2,1)} %bitcast.10, bf16[4,16,8,48,128]{4,3,2,1,0:T(8,128)(2,1)} %bitcast.11, f32[128,256]{1,0:T(8,128)S(1)} %copy-done.4, ...), custom_call_target="tpu_custom_call" | custom-call | flops 3221225472 | bytes 18874368 | tf_op jit(solution)/shard_map/pallas_call | solution.py:693
  51.1 2.6 %all-to-all-start.2 = ((bf16[32,16,256]{2,1,0:T(8,128)(2,1)}), bf16[32,16,256]{2,1,0:T(8,128)(2,1)S(1)}, u32[]{:S(2)}, u32[]{:S(2)}) async-start(bf16[32,16,256]{2,1,0:T(8,128)(2,1)} %get-tuple-element.15), calls=%async_computation.2 | async-start | bytes 524288 | tf_op jit(solution)/shard_map/all_to_all | solution.py:636
  53.7 0.0 copy-start.5
  53.7 0.0 copy-start.6
  53.7 8.2 %shard_map.162 = bf16[64,8,48,128]{3,2,1,0:T(8,128)(2,1)} custom-call(bf16[64,8,48,128]{3,2,1,0:T(8,128)(2,1)} %bitcast.12, bf16[64,64]{1,0:T(8,128)(2,1)S(1)} %copy-done.9), custom_call_target="tpu_custom_call" | custom-call | flops 3221225472 | bytes 12582912 | tf_op jit(solution)/shard_map/pallas_call | solution.py:650
  61.9 2.4 %all-to-all-done.2.arrived = bf16[32,16,256]{2,1,0:T(8,128)(2,1)S(1)} async-done(((bf16[32,16,256]{2,1,0:T(8,128)(2,1)}), bf16[32,16,256]{2,1,0:T(8,128)(2,1)S(1)}, u32[]{:S(2)}, u32[]{:S(2)}) %all-to-all-start.2) | async-done | bytes 262176 | tf_op jit(solution)/shard_map/all_to_all | solution.py:636
  64.3 0.0 copy-done.5
  64.3 1.7 %shard_map.163 = (bf16[256,512]{1,0:T(8,128)(2,1)S(1)}, bf16[32,16,256]{2,1,0:T(8,128)(2,1)}) custom-call(bf16[32,16,256]{2,1,0:T(8,128)(2,1)S(1)} %all-to-all-done.2.arrived, bf16[64,64,128]{2,1,0:T(8,128)(2,1)S(1)} %copy-done, bf16[256,512]{1,0:T(8,128)(2,1)S(1)} %copy-done.6, bf16[512,256]{1,0:T(8,128)(2,1)S(1)} %copy-done.5), custom_call_target="tpu_custom_call" | custom-call | flops 100000000 | bytes 1048576 | tf_op jit(solution)/shard_map/pallas_call | solution.py:709
  66.0 3.4 %all-to-all-start.3 = ((bf16[32,16,256]{2,1,0:T(8,128)(2,1)}), bf16[32,16,256]{2,1,0:T(8,128)(2,1)S(1)}, u32[]{:S(2)}, u32[]{:S(2)}) async-start(bf16[32,16,256]{2,1,0:T(8,128)(2,1)} %get-tuple-element.18), calls=%async_computation.3 | async-start | bytes 524288 | tf_op jit(solution)/shard_map/all_to_all | solution.py:636
  69.4 2.1 %shard_map.165 = f32[64,64,128]{2,1,0:T(8,128)} custom-call(bf16[256,256]{1,0:T(8,128)(2,1)S(1)} %get-tuple-element.20.spec_in, bf16[256,512]{1,0:T(8,128)(2,1)S(1)} %get-tuple-element.21.pairs), custom_call_target="tpu_custom_call" | custom-call | flops 100000000 | bytes 2097152 | tf_op jit(solution)/shard_map/pallas_call | solution.py:717
  71.5 8.5 %all-to-all-done.3.arrived = bf16[32,16,256]{2,1,0:T(8,128)(2,1)S(1)} async-done(((bf16[32,16,256]{2,1,0:T(8,128)(2,1)}), bf16[32,16,256]{2,1,0:T(8,128)(2,1)S(1)}, u32[]{:S(2)}, u32[]{:S(2)}) %all-to-all-start.3) | async-done | bytes 262176 | tf_op jit(solution)/shard_map/all_to_all | solution.py:636
  80.0 5.6 %shard_map.164 = bf16[4,16,8,48,128]{4,3,2,1,0:T(8,128)(2,1)} custom-call(bf16[32,16,256]{2,1,0:T(8,128)(2,1)S(1)} %all-to-all-done.3.arrived, bf16[4,16,8,48,128]{4,3,2,1,0:T(8,128)(2,1)} %bitcast.9, f32[256,128]{1,0:T(8,128)S(1)} %copy-done.3, bf16[768,256]{1,0:T(8,128)(2,1)S(1)} %copy-done.1), custom_call_target="tpu_custom_call" | custom-call | flops 1610612736 | bytes 12582912 | tf_op jit(solution)/shard_map/pallas_call | solution.py:723
  (9 shorter events, 0.0 us)
Async XLA Ops:
  0.6 12.8 %copy-start.9 = (bf16[64,64]{1,0:T(8,128)(2,1)S(1)}, bf16[64,64]{1,0:T(8,128)(2,1)}, u32[]{:S(2)}) copy-start(bf16[64,64]{1,0:T(8,128)(2,1)} %b.1) | copy-start | bytes 24580
  0.6 12.8 %copy-start.12 = (f32[64]{0:T(128)S(1)}, f32[64]{0:T(128)}, u32[]{:S(2)}) copy-start(f32[64]{0:T(128)} %offsets.1) | copy-start | bytes 772
  6.1 17.9 %all-to-all-start = ((bf16[32,16,256]{2,1,0:T(8,128)(2,1)}), bf16[32,16,256]{2,1,0:T(8,128)(2,1)S(1)}, u32[]{:S(2)}, u32[]{:S(2)}) async-start(bf16[32,16,256]{2,1,0:T(8,128)(2,1)} %shard_map.158), calls=%async_computation | async-start | bytes 524288 | tf_op jit(solution)/shard_map/all_to_all | solution.py:636
  13.4 10.6 %copy-start = (bf16[64,64,128]{2,1,0:T(8,128)(2,1)S(1)}, bf16[64,64,128]{2,1,0:T(8,128)(2,1)}, u32[]{:S(2)}) copy-start(bf16[64,64,128]{2,1,0:T(8,128)(2,1)} %weights.3) | copy-start | bytes 3145732
  13.4 10.6 %copy-start.7 = (bf16[512,256]{1,0:T(8,128)(2,1)S(1)}, bf16[512,256]{1,0:T(8,128)(2,1)}, u32[]{:S(2)}) copy-start(bf16[512,256]{1,0:T(8,128)(2,1)} %constant.23.clone.line_back) | copy-start | bytes 786436
  13.4 10.6 %copy-start.8 = (bf16[256,512]{1,0:T(8,128)(2,1)S(1)}, bf16[256,512]{1,0:T(8,128)(2,1)}, u32[]{:S(2)}) copy-start(bf16[256,512]{1,0:T(8,128)(2,1)} %constant.22.clone.line) | copy-start | bytes 786436
  13.4 25.6 %copy-start.1 = (bf16[768,256]{1,0:T(8,128)(2,1)S(1)}, bf16[768,256]{1,0:T(8,128)(2,1)}, u32[]{:S(2)}) copy-start(bf16[768,256]{1,0:T(8,128)(2,1)} %constant.25.clone.ytab_back) | copy-start | bytes 1179652
  13.5 25.6 %copy-start.2 = (bf16[256,768]{1,0:T(8,128)(2,1)S(1)}, bf16[256,768]{1,0:T(8,128)(2,1)}, u32[]{:S(2)}) copy-start(bf16[256,768]{1,0:T(8,128)(2,1)} %constant.21.clone.ytab_far.ytab) | copy-start | bytes 1179652
  13.5 25.6 %copy-start.3 = (f32[256,128]{1,0:T(8,128)S(1)}, f32[256,128]{1,0:T(8,128)}, u32[]{:S(2)}) copy-start(f32[256,128]{1,0:T(8,128)} %constant.24.clone.base_back) | copy-start | bytes 393220
  13.5 25.6 %copy-start.4 = (f32[128,256]{1,0:T(8,128)S(1)}, f32[128,256]{1,0:T(8,128)}, u32[]{:S(2)}) copy-start(f32[128,256]{1,0:T(8,128)} %constant.20.clone.base_far.base) | copy-start | bytes 393220
  13.5 25.6 %copy-start.10 = (f32[1,512]{1,0:T(1,128)S(1)}, f32[1,512]{1,0:T(1,128)}, u32[]{:S(2)}) copy-start(f32[1,512]{1,0:T(1,128)} %constant.27.clone.scale_back) | copy-start | bytes 6148
  13.5 25.6 %copy-start.11 = (f32[1,512]{1,0:T(1,128)S(1)}, f32[1,512]{1,0:T(1,128)}, u32[]{:S(2)}) copy-start(f32[1,512]{1,0:T(1,128)} %constant.26.clone.scale) | copy-start | bytes 6148
  51.1 13.2 %all-to-all-start.2 = ((bf16[32,16,256]{2,1,0:T(8,128)(2,1)}), bf16[32,16,256]{2,1,0:T(8,128)(2,1)S(1)}, u32[]{:S(2)}, u32[]{:S(2)}) async-start(bf16[32,16,256]{2,1,0:T(8,128)(2,1)} %get-tuple-element.15), calls=%async_computation.2 | async-start | bytes 524288 | tf_op jit(solution)/shard_map/all_to_all | solution.py:636
  53.7 10.6 %copy-start.5 = (bf16[512,256]{1,0:T(8,128)(2,1)S(1)}, bf16[512,256]{1,0:T(8,128)(2,1)}, u32[]{:S(2)}) copy-start(bf16[512,256]{1,0:T(8,128)(2,1)} %constant.29.clone.line_back) | copy-start | bytes 786436
  53.7 10.6 %copy-start.6 = (bf16[256,512]{1,0:T(8,128)(2,1)S(1)}, bf16[256,512]{1,0:T(8,128)(2,1)}, u32[]{:S(2)}) copy-start(bf16[256,512]{1,0:T(8,128)(2,1)} %constant.28.clone.line) | copy-start | bytes 786436
  66.0 14.0 %all-to-all-start.3 = ((bf16[32,16,256]{2,1,0:T(8,128)(2,1)}), bf16[32,16,256]{2,1,0:T(8,128)(2,1)S(1)}, u32[]{:S(2)}, u32[]{:S(2)}) async-start(bf16[32,16,256]{2,1,0:T(8,128)(2,1)} %get-tuple-element.18), calls=%async_computation.3 | async-start | bytes 524288 | tf_op jit(solution)/shard_map/all_to_all | solution.py:636

commit v4 on v3

--- a/solution.py
+++ b/solution.py
@@ -390,7 +390,6 @@
     width, rows_y, rows_z = local.shape[2:]
     groups = channels // GROUP
     rows = width * rows_y
-    wide = 2 * rows_y
     incoming = (GroupMove(local, local_in, local_sems), GroupMove(cotangent, cotangent_in, cotangent_sems))
     outgoing = GroupMove(result, slope, result_sems)
     start_all(incoming, 0)
@@ -413,13 +412,13 @@
             for slot in range(SLOTS):
                 lanes = slice(slot * rows_z, (slot + 1) * rows_z)
                 c = step * SLOTS + slot
-                for x in range(0, width, 2):
+                for x in range(width):
                     place = g * rows + x * rows_y
-                    value = total[place : place + wide, lanes]
-                    value = value + local_in[g, c, x : x + 2].reshape(wide, rows_z).astype(F32)
-                    upstream = cotangent_in[g, c, x : x + 2].reshape(wide, rows_z)
+                    value = total[place : place + rows_y, lanes]
+                    value = value + local_in[g, c, x].astype(F32)
+                    upstream = cotangent_in[g, c, x]
                     answer = upstream * doubled_slope(value)
-                    result[g, c, x : x + 2] = answer.reshape(2, rows_y, rows_z)
+                    result[g, c, x] = answer
             outgoing.copy(step, g).start()
         add_spectra(result, ztab, step, spectra)
 

time: 86 us -> 86 us (level)
  no operation moved by 1% of the time
where the time goes in v4:
time: 86 us; the launch traced here: 85.6 us
  Pallas kernels  44.2 us (51%)
  blocking collectives  14.1 us (16%)
  starting transfers between devices  13.3 us (15%)
  waiting for transfers between devices  13.1 us (15%)
    pallas_call x2, Pallas kernels, mix_points(): pl.pallas_call(run, grid=(width // step,), in_specs=specs, out_specs=bloc...  16.4 us
    all_to_all x1, blocking collectives, exchange(): lax.all_to_all(array, mesh_axes, split_axis=0, concat_axis=0, tiled=True)  14.1 us
    all_to_all x3, starting transfers between devices, exchange(): lax.all_to_all(array, mesh_axes, split_axis=0, concat_axis=0, tiled=True)  13.3 us
    all_to_all x3, waiting for transfers between devices, exchange(): lax.all_to_all(array, mesh_axes, split_axis=0, concat_axis=0, tiled=True)  13.1 us
    pallas_call x1, Pallas kernels, body(): pl.pallas_call(functools.partial(slope_kernel, per, channels, slabs), in_...  11.9 us
    pallas_call x1, Pallas kernels, body(): pl.pallas_call(functools.partial(field_kernel, per, channels, slabs), in_...  5.6 us
    pallas_call x1, Pallas kernels, body(): pl.pallas_call(functools.partial(plane_kernel, per, channels, slabs), in_...  5.43 us
    pallas_call x1, Pallas kernels, body(): pl.pallas_call(functools.partial(weight_kernel, per, samples), out_shape=...  2.07 us
  transfers between devices with their start and end apart: 3, of which 3 were waited for; matrix products, arithmetic and copies ran while one was open for 0% of the time, Pallas kernels for 22%

profile of v4, /device:TPU:0, one launch (start us, length us, event | category | flops | bytes accessed | tf_op | source)
XLA Modules:
  0.0 85.6 jit_solution(3876809106250129047)
XLA Ops:
  0.6 0.0 copy-start.9
  0.6 0.0 copy-start.12
  0.6 5.4 %shard_map.158 = bf16[32,16,256]{2,1,0:T(8,128)(2,1)} custom-call(bf16[4,16,8,48,128]{4,3,2,1,0:T(8,128)(2,1)} %bitcast.7, f32[128,256]{1,0:T(8,128)} %constant.20.clone.base_far.base, bf16[256,768]{1,0:T(8,128)(2,1)} %constant.21.clone.ytab_far.ytab), custom_call_target="tpu_custom_call" | custom-call | flops 1610612736 | bytes 6291456 | tf_op jit(solution)/shard_map/pallas_call | solution.py:663
  6.1 7.3 %all-to-all-start = ((bf16[32,16,256]{2,1,0:T(8,128)(2,1)}), bf16[32,16,256]{2,1,0:T(8,128)(2,1)S(1)}, u32[]{:S(2)}, u32[]{:S(2)}) async-start(bf16[32,16,256]{2,1,0:T(8,128)(2,1)} %shard_map.158), calls=%async_computation | async-start | bytes 524288 | tf_op jit(solution)/shard_map/all_to_all | solution.py:635
  13.4 0.0 copy-done.9
  13.4 0.0 copy-done.12
  13.4 0.0 copy-start
  13.4 0.0 copy-start.7
  13.4 0.0 copy-start.8
  13.4 0.0 copy-start.1
  13.5 0.0 copy-start.2
  13.5 0.0 copy-start.3
  13.5 0.0 copy-start.4
  13.5 0.0 copy-start.10
  13.5 0.0 copy-start.11
  13.5 8.3 %shard_map.159 = bf16[64,8,48,128]{3,2,1,0:T(8,128)(2,1)} custom-call(bf16[64,8,48,128]{3,2,1,0:T(8,128)(2,1)} %bitcast.8, bf16[64,64]{1,0:T(8,128)(2,1)S(1)} %copy-done.9, f32[64]{0:T(128)S(1)} %copy-done.12), custom_call_target="tpu_custom_call" | custom-call | flops 3221225472 | bytes 12582912 | tf_op jit(solution)/shard_map/pallas_call | solution.py:649
  21.8 2.2 %all-to-all-done.arrived = bf16[32,16,256]{2,1,0:T(8,128)(2,1)S(1)} async-done(((bf16[32,16,256]{2,1,0:T(8,128)(2,1)}), bf16[32,16,256]{2,1,0:T(8,128)(2,1)S(1)}, u32[]{:S(2)}, u32[]{:S(2)}) %all-to-all-start) | async-done | bytes 262176 | tf_op jit(solution)/shard_map/all_to_all | solution.py:635
  24.0 1.0 %shard_map.160 = (bf16[256,256]{1,0:T(8,128)(2,1)S(1)}, bf16[32,16,256]{2,1,0:T(8,128)(2,1)S(1)}) custom-call(bf16[32,16,256]{2,1,0:T(8,128)(2,1)S(1)} %all-to-all-done.arrived, bf16[64,64,128]{2,1,0:T(8,128)(2,1)S(1)} %copy-done, bf16[256,512]{1,0:T(8,128)(2,1)S(1)} %copy-done.8, bf16[512,256]{1,0:T(8,128)(2,1)S(1)} %copy-done.7), custom_call_target="tpu_custom_call" | custom-call | flops 100000000 | bytes 1048576 | tf_op jit(solution)/shard_map/pallas_call | solution.py:684
  25.0 14.1 %all_to_all.20.arrived = bf16[32,16,256]{2,1,0:T(8,128)(2,1)S(1)} all-to-all(bf16[32,16,256]{2,1,0:T(8,128)(2,1)S(1)} %get-tuple-element.13), channel_id=1, replica_groups=mesh['dp'=8,'space'=4] {'dp','space'}, dimensions={0} | all-to-all | bytes 524288 | tf_op jit(solution)/shard_map/all_to_all | solution.py:635
  39.1 0.0 copy-done.1
  39.1 11.9 %shard_map.161 = (bf16[4,16,8,48,128]{4,3,2,1,0:T(8,128)(2,1)}, bf16[32,16,256]{2,1,0:T(8,128)(2,1)}) custom-call(bf16[32,16,256]{2,1,0:T(8,128)(2,1)S(1)} %all_to_all.20.arrived, bf16[4,16,8,48,128]{4,3,2,1,0:T(8,128)(2,1)} %bitcast.10, bf16[4,16,8,48,128]{4,3,2,1,0:T(8,128)(2,1)} %bitcast.11, f32[128,256]{1,0:T(8,128)S(1)} %copy-done.4, ...), custom_call_target="tpu_custom_call" | custom-call | flops 3221225472 | bytes 18874368 | tf_op jit(solution)/shard_map/pallas_call | solution.py:692
  51.1 2.6 %all-to-all-start.2 = ((bf16[32,16,256]{2,1,0:T(8,128)(2,1)}), bf16[32,16,256]{2,1,0:T(8,128)(2,1)S(1)}, u32[]{:S(2)}, u32[]{:S(2)}) async-start(bf16[32,16,256]{2,1,0:T(8,128)(2,1)} %get-tuple-element.15), calls=%async_computation.2 | async-start | bytes 524288 | tf_op jit(solution)/shard_map/all_to_all | solution.py:635
  53.7 0.0 copy-start.5
  53.7 0.0 copy-start.6
  53.7 8.2 %shard_map.162 = bf16[64,8,48,128]{3,2,1,0:T(8,128)(2,1)} custom-call(bf16[64,8,48,128]{3,2,1,0:T(8,128)(2,1)} %bitcast.12, bf16[64,64]{1,0:T(8,128)(2,1)S(1)} %copy-done.9), custom_call_target="tpu_custom_call" | custom-call | flops 3221225472 | bytes 12582912 | tf_op jit(solution)/shard_map/pallas_call | solution.py:649
  61.9 2.4 %all-to-all-done.2.arrived = bf16[32,16,256]{2,1,0:T(8,128)(2,1)S(1)} async-done(((bf16[32,16,256]{2,1,0:T(8,128)(2,1)}), bf16[32,16,256]{2,1,0:T(8,128)(2,1)S(1)}, u32[]{:S(2)}, u32[]{:S(2)}) %all-to-all-start.2) | async-done | bytes 262176 | tf_op jit(solution)/shard_map/all_to_all | solution.py:635
  64.3 0.0 copy-done.5
  64.3 1.7 %shard_map.163 = (bf16[256,512]{1,0:T(8,128)(2,1)S(1)}, bf16[32,16,256]{2,1,0:T(8,128)(2,1)}) custom-call(bf16[32,16,256]{2,1,0:T(8,128)(2,1)S(1)} %all-to-all-done.2.arrived, bf16[64,64,128]{2,1,0:T(8,128)(2,1)S(1)} %copy-done, bf16[256,512]{1,0:T(8,128)(2,1)S(1)} %copy-done.6, bf16[512,256]{1,0:T(8,128)(2,1)S(1)} %copy-done.5), custom_call_target="tpu_custom_call" | custom-call | flops 100000000 | bytes 1048576 | tf_op jit(solution)/shard_map/pallas_call | solution.py:708
  66.0 3.4 %all-to-all-start.3 = ((bf16[32,16,256]{2,1,0:T(8,128)(2,1)}), bf16[32,16,256]{2,1,0:T(8,128)(2,1)S(1)}, u32[]{:S(2)}, u32[]{:S(2)}) async-start(bf16[32,16,256]{2,1,0:T(8,128)(2,1)} %get-tuple-element.18), calls=%async_computation.3 | async-start | bytes 524288 | tf_op jit(solution)/shard_map/all_to_all | solution.py:635
  69.4 2.1 %shard_map.165 = f32[64,64,128]{2,1,0:T(8,128)} custom-call(bf16[256,256]{1,0:T(8,128)(2,1)S(1)} %get-tuple-element.20.spec_in, bf16[256,512]{1,0:T(8,128)(2,1)S(1)} %get-tuple-element.21.pairs), custom_call_target="tpu_custom_call" | custom-call | flops 100000000 | bytes 2097152 | tf_op jit(solution)/shard_map/pallas_call | solution.py:716
  71.5 8.5 %all-to-all-done.3.arrived = bf16[32,16,256]{2,1,0:T(8,128)(2,1)S(1)} async-done(((bf16[32,16,256]{2,1,0:T(8,128)(2,1)}), bf16[32,16,256]{2,1,0:T(8,128)(2,1)S(1)}, u32[]{:S(2)}, u32[]{:S(2)}) %all-to-all-start.3) | async-done | bytes 262176 | tf_op jit(solution)/shard_map/all_to_all | solution.py:635
  80.0 5.6 %shard_map.164 = bf16[4,16,8,48,128]{4,3,2,1,0:T(8,128)(2,1)} custom-call(bf16[32,16,256]{2,1,0:T(8,128)(2,1)S(1)} %all-to-all-done.3.arrived, bf16[4,16,8,48,128]{4,3,2,1,0:T(8,128)(2,1)} %bitcast.9, f32[256,128]{1,0:T(8,128)S(1)} %copy-done.3, bf16[768,256]{1,0:T(8,128)(2,1)S(1)} %copy-done.1), custom_call_target="tpu_custom_call" | custom-call | flops 1610612736 | bytes 12582912 | tf_op jit(solution)/shard_map/pallas_call | solution.py:722
  (9 shorter events, 0.0 us)
Async XLA Ops:
  0.6 12.8 %copy-start.9 = (bf16[64,64]{1,0:T(8,128)(2,1)S(1)}, bf16[64,64]{1,0:T(8,128)(2,1)}, u32[]{:S(2)}) copy-start(bf16[64,64]{1,0:T(8,128)(2,1)} %b.1) | copy-start | bytes 24580
  0.6 12.8 %copy-start.12 = (f32[64]{0:T(128)S(1)}, f32[64]{0:T(128)}, u32[]{:S(2)}) copy-start(f32[64]{0:T(128)} %offsets.1) | copy-start | bytes 772
  6.1 17.9 %all-to-all-start = ((bf16[32,16,256]{2,1,0:T(8,128)(2,1)}), bf16[32,16,256]{2,1,0:T(8,128)(2,1)S(1)}, u32[]{:S(2)}, u32[]{:S(2)}) async-start(bf16[32,16,256]{2,1,0:T(8,128)(2,1)} %shard_map.158), calls=%async_computation | async-start | bytes 524288 | tf_op jit(solution)/shard_map/all_to_all | solution.py:635
  13.4 10.6 %copy-start = (bf16[64,64,128]{2,1,0:T(8,128)(2,1)S(1)}, bf16[64,64,128]{2,1,0:T(8,128)(2,1)}, u32[]{:S(2)}) copy-start(bf16[64,64,128]{2,1,0:T(8,128)(2,1)} %weights.3) | copy-start | bytes 3145732
  13.4 10.6 %copy-start.7 = (bf16[512,256]{1,0:T(8,128)(2,1)S(1)}, bf16[512,256]{1,0:T(8,128)(2,1)}, u32[]{:S(2)}) copy-start(bf16[512,256]{1,0:T(8,128)(2,1)} %constant.23.clone.line_back) | copy-start | bytes 786436
  13.4 10.6 %copy-start.8 = (bf16[256,512]{1,0:T(8,128)(2,1)S(1)}, bf16[256,512]{1,0:T(8,128)(2,1)}, u32[]{:S(2)}) copy-start(bf16[256,512]{1,0:T(8,128)(2,1)} %constant.22.clone.line) | copy-start | bytes 786436
  13.4 25.6 %copy-start.1 = (bf16[768,256]{1,0:T(8,128)(2,1)S(1)}, bf16[768,256]{1,0:T(8,128)(2,1)}, u32[]{:S(2)}) copy-start(bf16[768,256]{1,0:T(8,128)(2,1)} %constant.25.clone.ytab_back) | copy-start | bytes 1179652
  13.5 25.6 %copy-start.2 = (bf16[256,768]{1,0:T(8,128)(2,1)S(1)}, bf16[256,768]{1,0:T(8,128)(2,1)}, u32[]{:S(2)}) copy-start(bf16[256,768]{1,0:T(8,128)(2,1)} %constant.21.clone.ytab_far.ytab) | copy-start | bytes 1179652
  13.5 25.6 %copy-start.3 = (f32[256,128]{1,0:T(8,128)S(1)}, f32[256,128]{1,0:T(8,128)}, u32[]{:S(2)}) copy-start(f32[256,128]{1,0:T(8,128)} %constant.24.clone.base_back) | copy-start | bytes 393220
  13.5 25.6 %copy-start.4 = (f32[128,256]{1,0:T(8,128)S(1)}, f32[128,256]{1,0:T(8,128)}, u32[]{:S(2)}) copy-start(f32[128,256]{1,0:T(8,128)} %constant.20.clone.base_far.base) | copy-start | bytes 393220
  13.5 25.6 %copy-start.10 = (f32[1,512]{1,0:T(1,128)S(1)}, f32[1,512]{1,0:T(1,128)}, u32[]{:S(2)}) copy-start(f32[1,512]{1,0:T(1,128)} %constant.27.clone.scale_back) | copy-start | bytes 6148
  13.5 25.6 %copy-start.11 = (f32[1,512]{1,0:T(1,128)S(1)}, f32[1,512]{1,0:T(1,128)}, u32[]{:S(2)}) copy-start(f32[1,512]{1,0:T(1,128)} %constant.26.clone.scale) | copy-start | bytes 6148
  51.1 13.2 %all-to-all-start.2 = ((bf16[32,16,256]{2,1,0:T(8,128)(2,1)}), bf16[32,16,256]{2,1,0:T(8,128)(2,1)S(1)}, u32[]{:S(2)}, u32[]{:S(2)}) async-start(bf16[32,16,256]{2,1,0:T(8,128)(2,1)} %get-tuple-element.15), calls=%async_computation.2 | async-start | bytes 524288 | tf_op jit(solution)/shard_map/all_to_all | solution.py:635
  53.7 10.6 %copy-start.5 = (bf16[512,256]{1,0:T(8,128)(2,1)S(1)}, bf16[512,256]{1,0:T(8,128)(2,1)}, u32[]{:S(2)}) copy-start(bf16[512,256]{1,0:T(8,128)(2,1)} %constant.29.clone.line_back) | copy-start | bytes 786436
  53.7 10.6 %copy-start.6 = (bf16[256,512]{1,0:T(8,128)(2,1)S(1)}, bf16[256,512]{1,0:T(8,128)(2,1)}, u32[]{:S(2)}) copy-start(bf16[256,512]{1,0:T(8,128)(2,1)} %constant.28.clone.line) | copy-start | bytes 786436
  66.0 14.0 %all-to-all-start.3 = ((bf16[32,16,256]{2,1,0:T(8,128)(2,1)}), bf16[32,16,256]{2,1,0:T(8,128)(2,1)S(1)}, u32[]{:S(2)}, u32[]{:S(2)}) async-start(bf16[32,16,256]{2,1,0:T(8,128)(2,1)} %get-tuple-element.18), calls=%async_computation.3 | async-start | bytes 524288 | tf_op jit(solution)/shard_map/all_to_all | solution.py:635

commit v5 on v4

--- a/solution.py
+++ b/solution.py
@@ -162,6 +162,8 @@
 TILE = 8
 SLOTS = 4
 STEPS = GROUP // SLOTS
+SMALL_SLOTS = 2
+SMALL_STEPS = GROUP // SMALL_SLOTS
 MIB = 1024 * 1024
 
 
@@ -241,8 +243,9 @@
     owner = within(lax.broadcasted_iota(jnp.int32, (lanes, rows_z), 0), GROUP)
     values = base[...]
     for c in range(GROUP):
-        first = c % SLOTS * rows_z
-        table[c // SLOTS, :, first : first + rows_z] = jnp.where(owner == c, values, 0.0).astype(BF16)
+        slots = GROUP // table.shape[0]
+        first = c % slots * rows_z
+        table[c // slots, :, first : first + rows_z] = jnp.where(owner == c, values, 0.0).astype(BF16)
 
 
 def grouped(lane, per, channels):
@@ -310,9 +313,10 @@
 class Move:
     def __init__(self, source, target, sems):
         self.source, self.target, self.sems = source, target, sems
+        self.slots = GROUP // sems.shape[0]
 
     def copy(self, step):
-        run = pl.ds(step * SLOTS, SLOTS)
+        run = pl.ds(step * self.slots, self.slots)
         return pltpu.make_async_copy(self.source.at[:, run], self.target.at[:, run], self.sems.at[step])
 
     def start(self, step):
@@ -342,16 +346,16 @@
         each.start(step)
 
 
-def add_spectra(field, ztab, step, spectra):
+def add_spectra(field, ztab, step, slots, spectra):
     groups = field.shape[0]
     rows_z = field.shape[-1]
-    depth = SLOTS * rows_z
+    depth = slots * rows_z
     table = ztab[pl.ds(pl.multiple_of(step * depth, depth), depth)]
     lanes = [
         jnp.concatenate(
-            [field[g, step * SLOTS + slot].reshape(-1, rows_z) for g in range(groups)], axis=0
+            [field[g, step * slots + slot].reshape(-1, rows_z) for g in range(groups)], axis=0
         )
-        for slot in range(SLOTS)
+        for slot in range(slots)
     ]
     spectra[...] += dot(jnp.concatenate(lanes, axis=1), table)
 
@@ -364,19 +368,21 @@
     ytab_copy = pltpu.make_async_copy(ytab_far, ytab, table_sems.at[1])
     base_copy.start()
     incoming.start(0)
+    incoming.start(1)
     fill_order(per, channels, False, order)
+    incoming.start(2)
     spectra[...] = jnp.zeros_like(spectra)
-    incoming.start(1)
+    incoming.start(3)
     base_copy.wait()
     fill_z(base, ztab)
-    incoming.start(2)
+    for step in range(4, SMALL_STEPS):
+        incoming.start(step)
     ytab_copy.start()
-    incoming.start(3)
-
-    @pl.loop(0, STEPS)
+
+    @pl.loop(0, SMALL_STEPS)
     def _(step):
         incoming.wait(step)
-        add_spectra(buffer, ztab, step, spectra)
+        add_spectra(buffer, ztab, step, SMALL_SLOTS, spectra)
 
     ytab_copy.wait()
     deliver(spectra, ytab, order, None, message, per, channels, slabs)
@@ -420,7 +426,7 @@
                     answer = upstream * doubled_slope(value)
                     result[g, c, x] = answer
             outgoing.copy(step, g).start()
-        add_spectra(result, ztab, step, spectra)
+        add_spectra(result, ztab, step, SLOTS, spectra)
 
     deliver(spectra, ytab, order, scale, message, per, channels, slabs)
     for step in range(STEPS):
@@ -437,27 +443,31 @@
     incoming = Move(local, local_in, local_sems)
     outgoing = Move(result, out, result_sems)
     incoming.start(0)
+    incoming.start(1)
     fill_order(per, channels, True, order)
-    incoming.start(1)
+    incoming.start(2)
+    incoming.start(3)
     receive(arrived, order, ytab_back, None, held, per, slabs)
-    incoming.start(2)
+    incoming.start(4)
+    incoming.start(5)
     fill_z_back(base_back, ztab_back)
-    incoming.start(3)
-
-    @pl.loop(0, STEPS)
+    incoming.start(6)
+    incoming.start(7)
+
+    @pl.loop(0, SMALL_STEPS)
     def _(step):
         incoming.wait(step)
         total = dot(held[...], ztab_back[step])
         for g in range(groups):
-            for slot in range(SLOTS):
+            for slot in range(SMALL_SLOTS):
                 lanes = slice(slot * rows_z, (slot + 1) * rows_z)
-                c = step * SLOTS + slot
+                c = step * SMALL_SLOTS + slot
                 value = total[g * rows : (g + 1) * rows, lanes]
                 value = value + local_in[g, c].reshape(rows, rows_z).astype(F32)
                 result[g, c] = value.astype(BF16).reshape(width, rows_y, rows_z)
         outgoing.start(step)
 
-    for step in range(STEPS):
+    for step in range(SMALL_STEPS):
         outgoing.wait(step)
 
 
@@ -614,6 +624,7 @@
     spectra = shaped((MX * 2 * samples, per * channels), BF16)
     ztab = pltpu.VMEM((GROUP * rows_z, 2 * MZ * GROUP), BF16)
     ztab_t = pltpu.VMEM((STEPS, 2 * MZ * GROUP, SLOTS * rows_z), BF16)
+    small_ztab_t = pltpu.VMEM((SMALL_STEPS, 2 * MZ * GROUP, SMALL_SLOTS * rows_z), BF16)
     order = pltpu.VMEM((MZ * channels, MZ * channels), BF16)
     rows = groups * width * rows_y
     held = pltpu.VMEM((rows, 2 * MZ * GROUP), BF16)
@@ -621,7 +632,7 @@
     slot_sums = pltpu.VMEM((rows, SLOTS * rows_z), F32)
     grouped_field = (groups, GROUP) + field[1:]
     buffer = pltpu.VMEM(grouped_field, BF16)
-    sems = pltpu.SemaphoreType.DMA((STEPS,))
+    sems = pltpu.SemaphoreType.DMA((SMALL_STEPS,))
     group_sems = pltpu.SemaphoreType.DMA((STEPS * groups,))
     far = pl.BlockSpec(memory_space=pltpu.HBM)
     far_field = pltpu.HBM(field, BF16)
@@ -724,7 +735,7 @@
         in_specs=[whole(message), far, whole(base_t), whole(ytab_t)],
         out_specs=far,
         out_shape=shaped(grouped_field, BF16),
-        scratch_shapes=[ztab_t, order, held, buffer, buffer, sems, sems],
+        scratch_shapes=[small_ztab_t, order, held, buffer, buffer, sems, sems],
         compiler_params=params(32),
         cost_estimate=cost(plane_flops, 4 * count),
     )(returned_back, kept_far(local_back.reshape(grouped_field)), base_t, ytab_t)

time: 86 us -> 86.8 us (level)
  transfers between devices with their start and end apart: 3 -> 3, of which waited for: 3 -> 3; matrix products, arithmetic and copies ran while one was open for 0% -> 0% of each run, Pallas kernels for 22% -> 21%
where the time goes in v5:
time: 86.8 us; the launch traced here: 86.4 us
  Pallas kernels  44.9 us (52%)
  blocking collectives  14.1 us (16%)
  starting transfers between devices  13.3 us (15%)
  waiting for transfers between devices  13.1 us (15%)
    pallas_call x2, Pallas kernels, mix_points(): pl.pallas_call(run, grid=(width // step,), in_specs=specs, out_specs=bloc...  16.4 us
    all_to_all x1, blocking collectives, exchange(): lax.all_to_all(array, mesh_axes, split_axis=0, concat_axis=0, tiled=True)  14.1 us
    all_to_all x3, starting transfers between devices, exchange(): lax.all_to_all(array, mesh_axes, split_axis=0, concat_axis=0, tiled=True)  13.3 us
    all_to_all x3, waiting for transfers between devices, exchange(): lax.all_to_all(array, mesh_axes, split_axis=0, concat_axis=0, tiled=True)  13.1 us
    pallas_call x1, Pallas kernels, body(): pl.pallas_call(functools.partial(slope_kernel, per, channels, slabs), in_...  11.9 us
    pallas_call x1, Pallas kernels, body(): pl.pallas_call(functools.partial(plane_kernel, per, channels, slabs), in_...  6.05 us
    pallas_call x1, Pallas kernels, body(): pl.pallas_call(functools.partial(field_kernel, per, channels, slabs), in_...  5.75 us
    pallas_call x1, Pallas kernels, body(): pl.pallas_call(functools.partial(weight_kernel, per, samples), out_shape=...  2.07 us
  transfers between devices with their start and end apart: 3, of which 3 were waited for; matrix products, arithmetic and copies ran while one was open for 0% of the time, Pallas kernels for 21%

profile of v5, /device:TPU:0, one launch (start us, length us, event | category | flops | bytes accessed | tf_op | source)
XLA Modules:
  0.0 86.4 jit_solution(15574484855760045891)
XLA Ops:
  0.6 0.0 copy-start.9
  0.6 0.0 copy-start.12
  0.6 6.0 %shard_map.158 = bf16[32,16,256]{2,1,0:T(8,128)(2,1)} custom-call(bf16[4,16,8,48,128]{4,3,2,1,0:T(8,128)(2,1)} %bitcast.7, f32[128,256]{1,0:T(8,128)} %constant.20.clone.base_far.base, bf16[256,768]{1,0:T(8,128)(2,1)} %constant.21.clone.ytab_far.ytab), custom_call_target="tpu_custom_call" | custom-call | flops 1610612736 | bytes 6291456 | tf_op jit(solution)/shard_map/pallas_call | solution.py:674
  6.7 7.3 %all-to-all-start = ((bf16[32,16,256]{2,1,0:T(8,128)(2,1)}), bf16[32,16,256]{2,1,0:T(8,128)(2,1)S(1)}, u32[]{:S(2)}, u32[]{:S(2)}) async-start(bf16[32,16,256]{2,1,0:T(8,128)(2,1)} %shard_map.158), calls=%async_computation | async-start | bytes 524288 | tf_op jit(solution)/shard_map/all_to_all | solution.py:646
  14.0 0.0 copy-done.9
  14.0 0.0 copy-start
  14.0 0.0 copy-start.7
  14.1 0.0 copy-start.8
  14.1 0.0 copy-start.1
  14.1 0.0 copy-start.2
  14.1 0.0 copy-start.3
  14.1 0.0 copy-start.4
  14.1 0.0 copy-start.10
  14.1 0.0 copy-start.11
  14.1 8.3 %shard_map.159 = bf16[64,8,48,128]{3,2,1,0:T(8,128)(2,1)} custom-call(bf16[64,8,48,128]{3,2,1,0:T(8,128)(2,1)} %bitcast.8, bf16[64,64]{1,0:T(8,128)(2,1)S(1)} %copy-done.9, f32[64]{0:T(128)S(1)} %copy-done.12), custom_call_target="tpu_custom_call" | custom-call | flops 3221225472 | bytes 12582912 | tf_op jit(solution)/shard_map/pallas_call | solution.py:660
  22.4 2.2 %all-to-all-done.arrived = bf16[32,16,256]{2,1,0:T(8,128)(2,1)S(1)} async-done(((bf16[32,16,256]{2,1,0:T(8,128)(2,1)}), bf16[32,16,256]{2,1,0:T(8,128)(2,1)S(1)}, u32[]{:S(2)}, u32[]{:S(2)}) %all-to-all-start) | async-done | bytes 262176 | tf_op jit(solution)/shard_map/all_to_all | solution.py:646
  24.6 0.0 copy-done.7
  24.6 1.0 %shard_map.160 = (bf16[256,256]{1,0:T(8,128)(2,1)S(1)}, bf16[32,16,256]{2,1,0:T(8,128)(2,1)S(1)}) custom-call(bf16[32,16,256]{2,1,0:T(8,128)(2,1)S(1)} %all-to-all-done.arrived, bf16[64,64,128]{2,1,0:T(8,128)(2,1)S(1)} %copy-done, bf16[256,512]{1,0:T(8,128)(2,1)S(1)} %copy-done.8, bf16[512,256]{1,0:T(8,128)(2,1)S(1)} %copy-done.7), custom_call_target="tpu_custom_call" | custom-call | flops 100000000 | bytes 1048576 | tf_op jit(solution)/shard_map/pallas_call | solution.py:695
  25.6 14.1 %all_to_all.20.arrived = bf16[32,16,256]{2,1,0:T(8,128)(2,1)S(1)} all-to-all(bf16[32,16,256]{2,1,0:T(8,128)(2,1)S(1)} %get-tuple-element.13), channel_id=1, replica_groups=mesh['dp'=8,'space'=4] {'dp','space'}, dimensions={0} | all-to-all | bytes 524288 | tf_op jit(solution)/shard_map/all_to_all | solution.py:646
  39.7 0.0 copy-done.1
  39.8 11.9 %shard_map.161 = (bf16[4,16,8,48,128]{4,3,2,1,0:T(8,128)(2,1)}, bf16[32,16,256]{2,1,0:T(8,128)(2,1)}) custom-call(bf16[32,16,256]{2,1,0:T(8,128)(2,1)S(1)} %all_to_all.20.arrived, bf16[4,16,8,48,128]{4,3,2,1,0:T(8,128)(2,1)} %bitcast.10, bf16[4,16,8,48,128]{4,3,2,1,0:T(8,128)(2,1)} %bitcast.11, f32[128,256]{1,0:T(8,128)S(1)} %copy-done.4, ...), custom_call_target="tpu_custom_call" | custom-call | flops 3221225472 | bytes 18874368 | tf_op jit(solution)/shard_map/pallas_call | solution.py:703
  51.7 2.6 %all-to-all-start.2 = ((bf16[32,16,256]{2,1,0:T(8,128)(2,1)}), bf16[32,16,256]{2,1,0:T(8,128)(2,1)S(1)}, u32[]{:S(2)}, u32[]{:S(2)}) async-start(bf16[32,16,256]{2,1,0:T(8,128)(2,1)} %get-tuple-element.15), calls=%async_computation.2 | async-start | bytes 524288 | tf_op jit(solution)/shard_map/all_to_all | solution.py:646
  54.3 0.0 copy-start.5
  54.3 0.0 copy-start.6
  54.3 8.2 %shard_map.162 = bf16[64,8,48,128]{3,2,1,0:T(8,128)(2,1)} custom-call(bf16[64,8,48,128]{3,2,1,0:T(8,128)(2,1)} %bitcast.12, bf16[64,64]{1,0:T(8,128)(2,1)S(1)} %copy-done.9), custom_call_target="tpu_custom_call" | custom-call | flops 3221225472 | bytes 12582912 | tf_op jit(solution)/shard_map/pallas_call | solution.py:660
  62.5 2.4 %all-to-all-done.2.arrived = bf16[32,16,256]{2,1,0:T(8,128)(2,1)S(1)} async-done(((bf16[32,16,256]{2,1,0:T(8,128)(2,1)}), bf16[32,16,256]{2,1,0:T(8,128)(2,1)S(1)}, u32[]{:S(2)}, u32[]{:S(2)}) %all-to-all-start.2) | async-done | bytes 262176 | tf_op jit(solution)/shard_map/all_to_all | solution.py:646
  64.9 0.0 copy-done.5
  64.9 1.7 %shard_map.163 = (bf16[256,512]{1,0:T(8,128)(2,1)S(1)}, bf16[32,16,256]{2,1,0:T(8,128)(2,1)}) custom-call(bf16[32,16,256]{2,1,0:T(8,128)(2,1)S(1)} %all-to-all-done.2.arrived, bf16[64,64,128]{2,1,0:T(8,128)(2,1)S(1)} %copy-done, bf16[256,512]{1,0:T(8,128)(2,1)S(1)} %copy-done.6, bf16[512,256]{1,0:T(8,128)(2,1)S(1)} %copy-done.5), custom_call_target="tpu_custom_call" | custom-call | flops 100000000 | bytes 1048576 | tf_op jit(solution)/shard_map/pallas_call | solution.py:719
  66.6 3.4 %all-to-all-start.3 = ((bf16[32,16,256]{2,1,0:T(8,128)(2,1)}), bf16[32,16,256]{2,1,0:T(8,128)(2,1)S(1)}, u32[]{:S(2)}, u32[]{:S(2)}) async-start(bf16[32,16,256]{2,1,0:T(8,128)(2,1)} %get-tuple-element.18), calls=%async_computation.3 | async-start | bytes 524288 | tf_op jit(solution)/shard_map/all_to_all | solution.py:646
  70.0 2.1 %shard_map.165 = f32[64,64,128]{2,1,0:T(8,128)} custom-call(bf16[256,256]{1,0:T(8,128)(2,1)S(1)} %get-tuple-element.20.spec_in, bf16[256,512]{1,0:T(8,128)(2,1)S(1)} %get-tuple-element.21.pairs), custom_call_target="tpu_custom_call" | custom-call | flops 100000000 | bytes 2097152 | tf_op jit(solution)/shard_map/pallas_call | solution.py:727
  72.1 8.5 %all-to-all-done.3.arrived = bf16[32,16,256]{2,1,0:T(8,128)(2,1)S(1)} async-done(((bf16[32,16,256]{2,1,0:T(8,128)(2,1)}), bf16[32,16,256]{2,1,0:T(8,128)(2,1)S(1)}, u32[]{:S(2)}, u32[]{:S(2)}) %all-to-all-start.3) | async-done | bytes 262176 | tf_op jit(solution)/shard_map/all_to_all | solution.py:646
  80.6 5.8 %shard_map.164 = bf16[4,16,8,48,128]{4,3,2,1,0:T(8,128)(2,1)} custom-call(bf16[32,16,256]{2,1,0:T(8,128)(2,1)S(1)} %all-to-all-done.3.arrived, bf16[4,16,8,48,128]{4,3,2,1,0:T(8,128)(2,1)} %bitcast.9, f32[256,128]{1,0:T(8,128)S(1)} %copy-done.3, bf16[768,256]{1,0:T(8,128)(2,1)S(1)} %copy-done.1), custom_call_target="tpu_custom_call" | custom-call | flops 1610612736 | bytes 12582912 | tf_op jit(solution)/shard_map/pallas_call | solution.py:733
  (9 shorter events, 0.0 us)
Async XLA Ops:
  0.6 13.4 %copy-start.9 = (bf16[64,64]{1,0:T(8,128)(2,1)S(1)}, bf16[64,64]{1,0:T(8,128)(2,1)}, u32[]{:S(2)}) copy-start(bf16[64,64]{1,0:T(8,128)(2,1)} %b.1) | copy-start | bytes 24580
  0.6 13.4 %copy-start.12 = (f32[64]{0:T(128)S(1)}, f32[64]{0:T(128)}, u32[]{:S(2)}) copy-start(f32[64]{0:T(128)} %offsets.1) | copy-start | bytes 772
  6.7 17.9 %all-to-all-start = ((bf16[32,16,256]{2,1,0:T(8,128)(2,1)}), bf16[32,16,256]{2,1,0:T(8,128)(2,1)S(1)}, u32[]{:S(2)}, u32[]{:S(2)}) async-start(bf16[32,16,256]{2,1,0:T(8,128)(2,1)} %shard_map.158), calls=%async_computation | async-start | bytes 524288 | tf_op jit(solution)/shard_map/all_to_all | solution.py:646
  14.0 10.6 %copy-start = (bf16[64,64,128]{2,1,0:T(8,128)(2,1)S(1)}, bf16[64,64,128]{2,1,0:T(8,128)(2,1)}, u32[]{:S(2)}) copy-start(bf16[64,64,128]{2,1,0:T(8,128)(2,1)} %weights.3) | copy-start | bytes 3145732
  14.0 10.6 %copy-start.7 = (bf16[512,256]{1,0:T(8,128)(2,1)S(1)}, bf16[512,256]{1,0:T(8,128)(2,1)}, u32[]{:S(2)}) copy-start(bf16[512,256]{1,0:T(8,128)(2,1)} %constant.23.clone.line_back) | copy-start | bytes 786436
  14.1 10.6 %copy-start.8 = (bf16[256,512]{1,0:T(8,128)(2,1)S(1)}, bf16[256,512]{1,0:T(8,128)(2,1)}, u32[]{:S(2)}) copy-start(bf16[256,512]{1,0:T(8,128)(2,1)} %constant.22.clone.line) | copy-start | bytes 786436
  14.1 25.6 %copy-start.1 = (bf16[768,256]{1,0:T(8,128)(2,1)S(1)}, bf16[768,256]{1,0:T(8,128)(2,1)}, u32[]{:S(2)}) copy-start(bf16[768,256]{1,0:T(8,128)(2,1)} %constant.25.clone.ytab_back) | copy-start | bytes 1179652
  14.1 25.6 %copy-start.2 = (bf16[256,768]{1,0:T(8,128)(2,1)S(1)}, bf16[256,768]{1,0:T(8,128)(2,1)}, u32[]{:S(2)}) copy-start(bf16[256,768]{1,0:T(8,128)(2,1)} %constant.21.clone.ytab_far.ytab) | copy-start | bytes 1179652
  14.1 25.6 %copy-start.3 = (f32[256,128]{1,0:T(8,128)S(1)}, f32[256,128]{1,0:T(8,128)}, u32[]{:S(2)}) copy-start(f32[256,128]{1,0:T(8,128)} %constant.24.clone.base_back) | copy-start | bytes 393220
  14.1 25.6 %copy-start.4 = (f32[128,256]{1,0:T(8,128)S(1)}, f32[128,256]{1,0:T(8,128)}, u32[]{:S(2)}) copy-start(f32[128,256]{1,0:T(8,128)} %constant.20.clone.base_far.base) | copy-start | bytes 393220
  14.1 25.6 %copy-start.10 = (f32[1,512]{1,0:T(1,128)S(1)}, f32[1,512]{1,0:T(1,128)}, u32[]{:S(2)}) copy-start(f32[1,512]{1,0:T(1,128)} %constant.27.clone.scale_back) | copy-start | bytes 6148
  14.1 25.6 %copy-start.11 = (f32[1,512]{1,0:T(1,128)S(1)}, f32[1,512]{1,0:T(1,128)}, u32[]{:S(2)}) copy-start(f32[1,512]{1,0:T(1,128)} %constant.26.clone.scale) | copy-start | bytes 6148
  51.7 13.2 %all-to-all-start.2 = ((bf16[32,16,256]{2,1,0:T(8,128)(2,1)}), bf16[32,16,256]{2,1,0:T(8,128)(2,1)S(1)}, u32[]{:S(2)}, u32[]{:S(2)}) async-start(bf16[32,16,256]{2,1,0:T(8,128)(2,1)} %get-tuple-element.15), calls=%async_computation.2 | async-start | bytes 524288 | tf_op jit(solution)/shard_map/all_to_all | solution.py:646
  54.3 10.6 %copy-start.5 = (bf16[512,256]{1,0:T(8,128)(2,1)S(1)}, bf16[512,256]{1,0:T(8,128)(2,1)}, u32[]{:S(2)}) copy-start(bf16[512,256]{1,0:T(8,128)(2,1)} %constant.29.clone.line_back) | copy-start | bytes 786436
  54.3 10.6 %copy-start.6 = (bf16[256,512]{1,0:T(8,128)(2,1)S(1)}, bf16[256,512]{1,0:T(8,128)(2,1)}, u32[]{:S(2)}) copy-start(bf16[256,512]{1,0:T(8,128)(2,1)} %constant.28.clone.line) | copy-start | bytes 786436
  66.6 14.0 %all-to-all-start.3 = ((bf16[32,16,256]{2,1,0:T(8,128)(2,1)}), bf16[32,16,256]{2,1,0:T(8,128)(2,1)S(1)}, u32[]{:S(2)}, u32[]{:S(2)}) async-start(bf16[32,16,256]{2,1,0:T(8,128)(2,1)} %get-tuple-element.18), calls=%async_computation.3 | async-start | bytes 524288 | tf_op jit(solution)/shard_map/all_to_all | solution.py:646

commit v6 on v4

--- a/solution.py
+++ b/solution.py
@@ -162,6 +162,8 @@
 TILE = 8
 SLOTS = 4
 STEPS = GROUP // SLOTS
+PLANE_SLOTS = 8
+PLANE_STEPS = GROUP // PLANE_SLOTS
 MIB = 1024 * 1024
 
 
@@ -310,9 +312,10 @@
 class Move:
     def __init__(self, source, target, sems):
         self.source, self.target, self.sems = source, target, sems
+        self.slots = GROUP // sems.shape[0]
 
     def copy(self, step):
-        run = pl.ds(step * SLOTS, SLOTS)
+        run = pl.ds(step * self.slots, self.slots)
         return pltpu.make_async_copy(self.source.at[:, run], self.target.at[:, run], self.sems.at[step])
 
     def start(self, step):
@@ -342,16 +345,16 @@
         each.start(step)
 
 
-def add_spectra(field, ztab, step, spectra):
+def add_spectra(field, ztab, step, slots, spectra):
     groups = field.shape[0]
     rows_z = field.shape[-1]
-    depth = SLOTS * rows_z
+    depth = slots * rows_z
     table = ztab[pl.ds(pl.multiple_of(step * depth, depth), depth)]
     lanes = [
         jnp.concatenate(
-            [field[g, step * SLOTS + slot].reshape(-1, rows_z) for g in range(groups)], axis=0
+            [field[g, step * slots + slot].reshape(-1, rows_z) for g in range(groups)], axis=0
         )
-        for slot in range(SLOTS)
+        for slot in range(slots)
     ]
     spectra[...] += dot(jnp.concatenate(lanes, axis=1), table)
 
@@ -366,17 +369,16 @@
     incoming.start(0)
     fill_order(per, channels, False, order)
     spectra[...] = jnp.zeros_like(spectra)
-    incoming.start(1)
+    for step in range(1, PLANE_STEPS):
+        incoming.start(step)
+    ytab_copy.start()
     base_copy.wait()
     fill_z(base, ztab)
-    incoming.start(2)
-    ytab_copy.start()
-    incoming.start(3)
-
-    @pl.loop(0, STEPS)
+
+    @pl.loop(0, PLANE_STEPS)
     def _(step):
         incoming.wait(step)
-        add_spectra(buffer, ztab, step, spectra)
+        add_spectra(buffer, ztab, step, PLANE_SLOTS, spectra)
 
     ytab_copy.wait()
     deliver(spectra, ytab, order, None, message, per, channels, slabs)
@@ -420,7 +422,7 @@
                     answer = upstream * doubled_slope(value)
                     result[g, c, x] = answer
             outgoing.copy(step, g).start()
-        add_spectra(result, ztab, step, spectra)
+        add_spectra(result, ztab, step, SLOTS, spectra)
 
     deliver(spectra, ytab, order, scale, message, per, channels, slabs)
     for step in range(STEPS):
@@ -672,7 +674,7 @@
             buffer,
             pltpu.VMEM(base.shape, F32),
             pltpu.VMEM(ytab.shape, BF16),
-            sems,
+            pltpu.SemaphoreType.DMA((PLANE_STEPS,)),
             pltpu.SemaphoreType.DMA((2,)),
         ],
         compiler_params=params(32),

time: 86 us -> 85.9 us (level)
  no operation moved by 1% of the time
where the time goes in v6:
time: 85.9 us; the launch traced here: 85.5 us
  Pallas kernels  44 us (51%)
  blocking collectives  14.1 us (16%)
  starting transfers between devices  13.3 us (15%)
  waiting for transfers between devices  13.1 us (15%)
    pallas_call x2, Pallas kernels, mix_points(): pl.pallas_call(run, grid=(width // step,), in_specs=specs, out_specs=bloc...  16.4 us
    all_to_all x1, blocking collectives, exchange(): lax.all_to_all(array, mesh_axes, split_axis=0, concat_axis=0, tiled=True)  14.1 us
    all_to_all x3, starting transfers between devices, exchange(): lax.all_to_all(array, mesh_axes, split_axis=0, concat_axis=0, tiled=True)  13.3 us
    all_to_all x3, waiting for transfers between devices, exchange(): lax.all_to_all(array, mesh_axes, split_axis=0, concat_axis=0, tiled=True)  13.1 us
    pallas_call x1, Pallas kernels, body(): pl.pallas_call(functools.partial(slope_kernel, per, channels, slabs), in_...  11.9 us
    pallas_call x1, Pallas kernels, body(): pl.pallas_call(functools.partial(field_kernel, per, channels, slabs), in_...  5.6 us
    pallas_call x1, Pallas kernels, body(): pl.pallas_call(functools.partial(plane_kernel, per, channels, slabs), in_...  5.28 us
    pallas_call x1, Pallas kernels, body(): pl.pallas_call(functools.partial(weight_kernel, per, samples), out_shape=...  2.07 us
  transfers between devices with their start and end apart: 3, of which 3 were waited for; matrix products, arithmetic and copies ran while one was open for 0% of the time, Pallas kernels for 22%

profile of v6, /device:TPU:0, one launch (start us, length us, event | category | flops | bytes accessed | tf_op | source)
XLA Modules:
  0.0 85.5 jit_solution(728155077074879291)
XLA Ops:
  0.6 0.0 copy-start.9
  0.6 0.0 copy-start.12
  0.6 5.3 %shard_map.158 = bf16[32,16,256]{2,1,0:T(8,128)(2,1)} custom-call(bf16[4,16,8,48,128]{4,3,2,1,0:T(8,128)(2,1)} %bitcast.7, f32[128,256]{1,0:T(8,128)} %constant.20.clone.base_far.base, bf16[256,768]{1,0:T(8,128)(2,1)} %constant.21.clone.ytab_far.ytab), custom_call_target="tpu_custom_call" | custom-call | flops 1610612736 | bytes 6291456 | tf_op jit(solution)/shard_map/pallas_call | solution.py:665
  5.9 7.3 %all-to-all-start = ((bf16[32,16,256]{2,1,0:T(8,128)(2,1)}), bf16[32,16,256]{2,1,0:T(8,128)(2,1)S(1)}, u32[]{:S(2)}, u32[]{:S(2)}) async-start(bf16[32,16,256]{2,1,0:T(8,128)(2,1)} %shard_map.158), calls=%async_computation | async-start | bytes 524288 | tf_op jit(solution)/shard_map/all_to_all | solution.py:637
  13.2 0.0 copy-done.9
  13.3 0.0 copy-done.12
  13.3 0.0 copy-start
  13.3 0.0 copy-start.7
  13.3 0.0 copy-start.8
  13.3 0.0 copy-start.1
  13.3 0.0 copy-start.2
  13.3 0.0 copy-start.3
  13.3 0.0 copy-start.4
  13.4 0.0 copy-start.10
  13.4 0.0 copy-start.11
  13.4 8.3 %shard_map.159 = bf16[64,8,48,128]{3,2,1,0:T(8,128)(2,1)} custom-call(bf16[64,8,48,128]{3,2,1,0:T(8,128)(2,1)} %bitcast.8, bf16[64,64]{1,0:T(8,128)(2,1)S(1)} %copy-done.9, f32[64]{0:T(128)S(1)} %copy-done.12), custom_call_target="tpu_custom_call" | custom-call | flops 3221225472 | bytes 12582912 | tf_op jit(solution)/shard_map/pallas_call | solution.py:651
  21.7 2.2 %all-to-all-done.arrived = bf16[32,16,256]{2,1,0:T(8,128)(2,1)S(1)} async-done(((bf16[32,16,256]{2,1,0:T(8,128)(2,1)}), bf16[32,16,256]{2,1,0:T(8,128)(2,1)S(1)}, u32[]{:S(2)}, u32[]{:S(2)}) %all-to-all-start) | async-done | bytes 262176 | tf_op jit(solution)/shard_map/all_to_all | solution.py:637
  23.9 0.0 copy-done.7
  23.9 1.0 %shard_map.160 = (bf16[256,256]{1,0:T(8,128)(2,1)S(1)}, bf16[32,16,256]{2,1,0:T(8,128)(2,1)S(1)}) custom-call(bf16[32,16,256]{2,1,0:T(8,128)(2,1)S(1)} %all-to-all-done.arrived, bf16[64,64,128]{2,1,0:T(8,128)(2,1)S(1)} %copy-done, bf16[256,512]{1,0:T(8,128)(2,1)S(1)} %copy-done.8, bf16[512,256]{1,0:T(8,128)(2,1)S(1)} %copy-done.7), custom_call_target="tpu_custom_call" | custom-call | flops 100000000 | bytes 1048576 | tf_op jit(solution)/shard_map/pallas_call | solution.py:686
  24.9 14.1 %all_to_all.20.arrived = bf16[32,16,256]{2,1,0:T(8,128)(2,1)S(1)} all-to-all(bf16[32,16,256]{2,1,0:T(8,128)(2,1)S(1)} %get-tuple-element.13), channel_id=1, replica_groups=mesh['dp'=8,'space'=4] {'dp','space'}, dimensions={0} | all-to-all | bytes 524288 | tf_op jit(solution)/shard_map/all_to_all | solution.py:637
  38.9 0.0 copy-done.2
  39.0 11.9 %shard_map.161 = (bf16[4,16,8,48,128]{4,3,2,1,0:T(8,128)(2,1)}, bf16[32,16,256]{2,1,0:T(8,128)(2,1)}) custom-call(bf16[32,16,256]{2,1,0:T(8,128)(2,1)S(1)} %all_to_all.20.arrived, bf16[4,16,8,48,128]{4,3,2,1,0:T(8,128)(2,1)} %bitcast.10, bf16[4,16,8,48,128]{4,3,2,1,0:T(8,128)(2,1)} %bitcast.11, f32[128,256]{1,0:T(8,128)S(1)} %copy-done.4, ...), custom_call_target="tpu_custom_call" | custom-call | flops 3221225472 | bytes 18874368 | tf_op jit(solution)/shard_map/pallas_call | solution.py:694
  50.9 2.6 %all-to-all-start.2 = ((bf16[32,16,256]{2,1,0:T(8,128)(2,1)}), bf16[32,16,256]{2,1,0:T(8,128)(2,1)S(1)}, u32[]{:S(2)}, u32[]{:S(2)}) async-start(bf16[32,16,256]{2,1,0:T(8,128)(2,1)} %get-tuple-element.15), calls=%async_computation.2 | async-start | bytes 524288 | tf_op jit(solution)/shard_map/all_to_all | solution.py:637
  53.5 0.0 copy-start.5
  53.6 0.0 copy-start.6
  53.6 8.2 %shard_map.162 = bf16[64,8,48,128]{3,2,1,0:T(8,128)(2,1)} custom-call(bf16[64,8,48,128]{3,2,1,0:T(8,128)(2,1)} %bitcast.12, bf16[64,64]{1,0:T(8,128)(2,1)S(1)} %copy-done.9), custom_call_target="tpu_custom_call" | custom-call | flops 3221225472 | bytes 12582912 | tf_op jit(solution)/shard_map/pallas_call | solution.py:651
  61.7 2.4 %all-to-all-done.2.arrived = bf16[32,16,256]{2,1,0:T(8,128)(2,1)S(1)} async-done(((bf16[32,16,256]{2,1,0:T(8,128)(2,1)}), bf16[32,16,256]{2,1,0:T(8,128)(2,1)S(1)}, u32[]{:S(2)}, u32[]{:S(2)}) %all-to-all-start.2) | async-done | bytes 262176 | tf_op jit(solution)/shard_map/all_to_all | solution.py:637
  64.2 1.7 %shard_map.163 = (bf16[256,512]{1,0:T(8,128)(2,1)S(1)}, bf16[32,16,256]{2,1,0:T(8,128)(2,1)}) custom-call(bf16[32,16,256]{2,1,0:T(8,128)(2,1)S(1)} %all-to-all-done.2.arrived, bf16[64,64,128]{2,1,0:T(8,128)(2,1)S(1)} %copy-done, bf16[256,512]{1,0:T(8,128)(2,1)S(1)} %copy-done.6, bf16[512,256]{1,0:T(8,128)(2,1)S(1)} %copy-done.5), custom_call_target="tpu_custom_call" | custom-call | flops 100000000 | bytes 1048576 | tf_op jit(solution)/shard_map/pallas_call | solution.py:710
  65.8 3.4 %all-to-all-start.3 = ((bf16[32,16,256]{2,1,0:T(8,128)(2,1)}), bf16[32,16,256]{2,1,0:T(8,128)(2,1)S(1)}, u32[]{:S(2)}, u32[]{:S(2)}) async-start(bf16[32,16,256]{2,1,0:T(8,128)(2,1)} %get-tuple-element.18), calls=%async_computation.3 | async-start | bytes 524288 | tf_op jit(solution)/shard_map/all_to_all | solution.py:637
  69.3 2.1 %shard_map.165 = f32[64,64,128]{2,1,0:T(8,128)} custom-call(bf16[256,256]{1,0:T(8,128)(2,1)S(1)} %get-tuple-element.20.spec_in, bf16[256,512]{1,0:T(8,128)(2,1)S(1)} %get-tuple-element.21.pairs), custom_call_target="tpu_custom_call" | custom-call | flops 100000000 | bytes 2097152 | tf_op jit(solution)/shard_map/pallas_call | solution.py:718
  71.3 8.5 %all-to-all-done.3.arrived = bf16[32,16,256]{2,1,0:T(8,128)(2,1)S(1)} async-done(((bf16[32,16,256]{2,1,0:T(8,128)(2,1)}), bf16[32,16,256]{2,1,0:T(8,128)(2,1)S(1)}, u32[]{:S(2)}, u32[]{:S(2)}) %all-to-all-start.3) | async-done | bytes 262176 | tf_op jit(solution)/shard_map/all_to_all | solution.py:637
  79.9 5.6 %shard_map.164 = bf16[4,16,8,48,128]{4,3,2,1,0:T(8,128)(2,1)} custom-call(bf16[32,16,256]{2,1,0:T(8,128)(2,1)S(1)} %all-to-all-done.3.arrived, bf16[4,16,8,48,128]{4,3,2,1,0:T(8,128)(2,1)} %bitcast.9, f32[256,128]{1,0:T(8,128)S(1)} %copy-done.3, bf16[768,256]{1,0:T(8,128)(2,1)S(1)} %copy-done.1), custom_call_target="tpu_custom_call" | custom-call | flops 1610612736 | bytes 12582912 | tf_op jit(solution)/shard_map/pallas_call | solution.py:724
  (9 shorter events, 0.0 us)
Async XLA Ops:
  0.6 12.6 %copy-start.9 = (bf16[64,64]{1,0:T(8,128)(2,1)S(1)}, bf16[64,64]{1,0:T(8,128)(2,1)}, u32[]{:S(2)}) copy-start(bf16[64,64]{1,0:T(8,128)(2,1)} %b.1) | copy-start | bytes 24580
  0.6 12.6 %copy-start.12 = (f32[64]{0:T(128)S(1)}, f32[64]{0:T(128)}, u32[]{:S(2)}) copy-start(f32[64]{0:T(128)} %offsets.1) | copy-start | bytes 772
  5.9 17.9 %all-to-all-start = ((bf16[32,16,256]{2,1,0:T(8,128)(2,1)}), bf16[32,16,256]{2,1,0:T(8,128)(2,1)S(1)}, u32[]{:S(2)}, u32[]{:S(2)}) async-start(bf16[32,16,256]{2,1,0:T(8,128)(2,1)} %shard_map.158), calls=%async_computation | async-start | bytes 524288 | tf_op jit(solution)/shard_map/all_to_all | solution.py:637
  13.3 10.6 %copy-start = (bf16[64,64,128]{2,1,0:T(8,128)(2,1)S(1)}, bf16[64,64,128]{2,1,0:T(8,128)(2,1)}, u32[]{:S(2)}) copy-start(bf16[64,64,128]{2,1,0:T(8,128)(2,1)} %weights.3) | copy-start | bytes 3145732
  13.3 10.6 %copy-start.7 = (bf16[512,256]{1,0:T(8,128)(2,1)S(1)}, bf16[512,256]{1,0:T(8,128)(2,1)}, u32[]{:S(2)}) copy-start(bf16[512,256]{1,0:T(8,128)(2,1)} %constant.23.clone.line_back) | copy-start | bytes 786436
  13.3 10.6 %copy-start.8 = (bf16[256,512]{1,0:T(8,128)(2,1)S(1)}, bf16[256,512]{1,0:T(8,128)(2,1)}, u32[]{:S(2)}) copy-start(bf16[256,512]{1,0:T(8,128)(2,1)} %constant.22.clone.line) | copy-start | bytes 786436
  13.3 25.6 %copy-start.1 = (bf16[768,256]{1,0:T(8,128)(2,1)S(1)}, bf16[768,256]{1,0:T(8,128)(2,1)}, u32[]{:S(2)}) copy-start(bf16[768,256]{1,0:T(8,128)(2,1)} %constant.25.clone.ytab_back) | copy-start | bytes 1179652
  13.3 25.6 %copy-start.2 = (bf16[256,768]{1,0:T(8,128)(2,1)S(1)}, bf16[256,768]{1,0:T(8,128)(2,1)}, u32[]{:S(2)}) copy-start(bf16[256,768]{1,0:T(8,128)(2,1)} %constant.21.clone.ytab_far.ytab) | copy-start | bytes 1179652
  13.3 25.6 %copy-start.3 = (f32[256,128]{1,0:T(8,128)S(1)}, f32[256,128]{1,0:T(8,128)}, u32[]{:S(2)}) copy-start(f32[256,128]{1,0:T(8,128)} %constant.24.clone.base_back) | copy-start | bytes 393220
  13.3 25.6 %copy-start.4 = (f32[128,256]{1,0:T(8,128)S(1)}, f32[128,256]{1,0:T(8,128)}, u32[]{:S(2)}) copy-start(f32[128,256]{1,0:T(8,128)} %constant.20.clone.base_far.base) | copy-start | bytes 393220
  13.4 25.6 %copy-start.10 = (f32[1,512]{1,0:T(1,128)S(1)}, f32[1,512]{1,0:T(1,128)}, u32[]{:S(2)}) copy-start(f32[1,512]{1,0:T(1,128)} %constant.27.clone.scale_back) | copy-start | bytes 6148
  13.4 25.6 %copy-start.11 = (f32[1,512]{1,0:T(1,128)S(1)}, f32[1,512]{1,0:T(1,128)}, u32[]{:S(2)}) copy-start(f32[1,512]{1,0:T(1,128)} %constant.26.clone.scale) | copy-start | bytes 6148
  50.9 13.2 %all-to-all-start.2 = ((bf16[32,16,256]{2,1,0:T(8,128)(2,1)}), bf16[32,16,256]{2,1,0:T(8,128)(2,1)S(1)}, u32[]{:S(2)}, u32[]{:S(2)}) async-start(bf16[32,16,256]{2,1,0:T(8,128)(2,1)} %get-tuple-element.15), calls=%async_computation.2 | async-start | bytes 524288 | tf_op jit(solution)/shard_map/all_to_all | solution.py:637
  53.5 10.6 %copy-start.5 = (bf16[512,256]{1,0:T(8,128)(2,1)S(1)}, bf16[512,256]{1,0:T(8,128)(2,1)}, u32[]{:S(2)}) copy-start(bf16[512,256]{1,0:T(8,128)(2,1)} %constant.29.clone.line_back) | copy-start | bytes 786436
  53.6 10.6 %copy-start.6 = (bf16[256,512]{1,0:T(8,128)(2,1)S(1)}, bf16[256,512]{1,0:T(8,128)(2,1)}, u32[]{:S(2)}) copy-start(bf16[256,512]{1,0:T(8,128)(2,1)} %constant.28.clone.line) | copy-start | bytes 786436
  65.8 14.0 %all-to-all-start.3 = ((bf16[32,16,256]{2,1,0:T(8,128)(2,1)}), bf16[32,16,256]{2,1,0:T(8,128)(2,1)S(1)}, u32[]{:S(2)}, u32[]{:S(2)}) async-start(bf16[32,16,256]{2,1,0:T(8,128)(2,1)} %get-tuple-element.18), calls=%async_computation.3 | async-start | bytes 524288 | tf_op jit(solution)/shard_map/all_to_all | solution.py:637

commit v7 on v6

--- a/solution.py
+++ b/solution.py
@@ -441,10 +441,10 @@
     incoming.start(0)
     fill_order(per, channels, True, order)
     incoming.start(1)
+    incoming.start(2)
+    incoming.start(3)
     receive(arrived, order, ytab_back, None, held, per, slabs)
-    incoming.start(2)
     fill_z_back(base_back, ztab_back)
-    incoming.start(3)
 
     @pl.loop(0, STEPS)
     def _(step):

time: 85.9 us -> 85.9 us (level)
  no operation moved by 1% of the time
where the time goes in v7:
time: 85.9 us; the launch traced here: 85.5 us
  Pallas kernels  44 us (51%)
  blocking collectives  14.1 us (16%)
  starting transfers between devices  13.3 us (15%)
  waiting for transfers between devices  13.1 us (15%)
    pallas_call x2, Pallas kernels, mix_points(): pl.pallas_call(run, grid=(width // step,), in_specs=specs, out_specs=bloc...  16.4 us
    all_to_all x1, blocking collectives, exchange(): lax.all_to_all(array, mesh_axes, split_axis=0, concat_axis=0, tiled=True)  14.1 us
    all_to_all x3, starting transfers between devices, exchange(): lax.all_to_all(array, mesh_axes, split_axis=0, concat_axis=0, tiled=True)  13.3 us
    all_to_all x3, waiting for transfers between devices, exchange(): lax.all_to_all(array, mesh_axes, split_axis=0, concat_axis=0, tiled=True)  13.1 us
    pallas_call x1, Pallas kernels, body(): pl.pallas_call(functools.partial(slope_kernel, per, channels, slabs), in_...  11.9 us
    pallas_call x1, Pallas kernels, body(): pl.pallas_call(functools.partial(field_kernel, per, channels, slabs), in_...  5.6 us
    pallas_call x1, Pallas kernels, body(): pl.pallas_call(functools.partial(plane_kernel, per, channels, slabs), in_...  5.28 us
    pallas_call x1, Pallas kernels, body(): pl.pallas_call(functools.partial(weight_kernel, per, samples), out_shape=...  2.07 us
  transfers between devices with their start and end apart: 3, of which 3 were waited for; matrix products, arithmetic and copies ran while one was open for 0% of the time, Pallas kernels for 22%

profile of v7, /device:TPU:0, one launch (start us, length us, event | category | flops | bytes accessed | tf_op | source)
XLA Modules:
  0.0 85.5 jit_solution(728155077074879291)
XLA Ops:
  0.6 0.0 copy-start.9
  0.6 0.0 copy-start.12
  0.6 5.3 %shard_map.158 = bf16[32,16,256]{2,1,0:T(8,128)(2,1)} custom-call(bf16[4,16,8,48,128]{4,3,2,1,0:T(8,128)(2,1)} %bitcast.7, f32[128,256]{1,0:T(8,128)} %constant.20.clone.base_far.base, bf16[256,768]{1,0:T(8,128)(2,1)} %constant.21.clone.ytab_far.ytab), custom_call_target="tpu_custom_call" | custom-call | flops 1610612736 | bytes 6291456 | tf_op jit(solution)/shard_map/pallas_call | solution.py:665
  5.9 7.3 %all-to-all-start = ((bf16[32,16,256]{2,1,0:T(8,128)(2,1)}), bf16[32,16,256]{2,1,0:T(8,128)(2,1)S(1)}, u32[]{:S(2)}, u32[]{:S(2)}) async-start(bf16[32,16,256]{2,1,0:T(8,128)(2,1)} %shard_map.158), calls=%async_computation | async-start | bytes 524288 | tf_op jit(solution)/shard_map/all_to_all | solution.py:637
  13.2 0.0 copy-done.9
  13.3 0.0 copy-done.12
  13.3 0.0 copy-start
  13.3 0.0 copy-start.7
  13.3 0.0 copy-start.8
  13.3 0.0 copy-start.1
  13.3 0.0 copy-start.2
  13.3 0.0 copy-start.3
  13.3 0.0 copy-start.4
  13.4 0.0 copy-start.10
  13.4 0.0 copy-start.11
  13.4 8.3 %shard_map.159 = bf16[64,8,48,128]{3,2,1,0:T(8,128)(2,1)} custom-call(bf16[64,8,48,128]{3,2,1,0:T(8,128)(2,1)} %bitcast.8, bf16[64,64]{1,0:T(8,128)(2,1)S(1)} %copy-done.9, f32[64]{0:T(128)S(1)} %copy-done.12), custom_call_target="tpu_custom_call" | custom-call | flops 3221225472 | bytes 12582912 | tf_op jit(solution)/shard_map/pallas_call | solution.py:651
  21.7 2.2 %all-to-all-done.arrived = bf16[32,16,256]{2,1,0:T(8,128)(2,1)S(1)} async-done(((bf16[32,16,256]{2,1,0:T(8,128)(2,1)}), bf16[32,16,256]{2,1,0:T(8,128)(2,1)S(1)}, u32[]{:S(2)}, u32[]{:S(2)}) %all-to-all-start) | async-done | bytes 262176 | tf_op jit(solution)/shard_map/all_to_all | solution.py:637
  23.9 0.0 copy-done.7
  23.9 1.0 %shard_map.160 = (bf16[256,256]{1,0:T(8,128)(2,1)S(1)}, bf16[32,16,256]{2,1,0:T(8,128)(2,1)S(1)}) custom-call(bf16[32,16,256]{2,1,0:T(8,128)(2,1)S(1)} %all-to-all-done.arrived, bf16[64,64,128]{2,1,0:T(8,128)(2,1)S(1)} %copy-done, bf16[256,512]{1,0:T(8,128)(2,1)S(1)} %copy-done.8, bf16[512,256]{1,0:T(8,128)(2,1)S(1)} %copy-done.7), custom_call_target="tpu_custom_call" | custom-call | flops 100000000 | bytes 1048576 | tf_op jit(solution)/shard_map/pallas_call | solution.py:686
  24.9 14.1 %all_to_all.20.arrived = bf16[32,16,256]{2,1,0:T(8,128)(2,1)S(1)} all-to-all(bf16[32,16,256]{2,1,0:T(8,128)(2,1)S(1)} %get-tuple-element.13), channel_id=1, replica_groups=mesh['dp'=8,'space'=4] {'dp','space'}, dimensions={0} | all-to-all | bytes 524288 | tf_op jit(solution)/shard_map/all_to_all | solution.py:637
  38.9 0.0 copy-done.2
  39.0 11.9 %shard_map.161 = (bf16[4,16,8,48,128]{4,3,2,1,0:T(8,128)(2,1)}, bf16[32,16,256]{2,1,0:T(8,128)(2,1)}) custom-call(bf16[32,16,256]{2,1,0:T(8,128)(2,1)S(1)} %all_to_all.20.arrived, bf16[4,16,8,48,128]{4,3,2,1,0:T(8,128)(2,1)} %bitcast.10, bf16[4,16,8,48,128]{4,3,2,1,0:T(8,128)(2,1)} %bitcast.11, f32[128,256]{1,0:T(8,128)S(1)} %copy-done.4, ...), custom_call_target="tpu_custom_call" | custom-call | flops 3221225472 | bytes 18874368 | tf_op jit(solution)/shard_map/pallas_call | solution.py:694
  50.9 2.6 %all-to-all-start.2 = ((bf16[32,16,256]{2,1,0:T(8,128)(2,1)}), bf16[32,16,256]{2,1,0:T(8,128)(2,1)S(1)}, u32[]{:S(2)}, u32[]{:S(2)}) async-start(bf16[32,16,256]{2,1,0:T(8,128)(2,1)} %get-tuple-element.15), calls=%async_computation.2 | async-start | bytes 524288 | tf_op jit(solution)/shard_map/all_to_all | solution.py:637
  53.5 0.0 copy-start.5
  53.6 0.0 copy-start.6
  53.6 8.2 %shard_map.162 = bf16[64,8,48,128]{3,2,1,0:T(8,128)(2,1)} custom-call(bf16[64,8,48,128]{3,2,1,0:T(8,128)(2,1)} %bitcast.12, bf16[64,64]{1,0:T(8,128)(2,1)S(1)} %copy-done.9), custom_call_target="tpu_custom_call" | custom-call | flops 3221225472 | bytes 12582912 | tf_op jit(solution)/shard_map/pallas_call | solution.py:651
  61.7 2.4 %all-to-all-done.2.arrived = bf16[32,16,256]{2,1,0:T(8,128)(2,1)S(1)} async-done(((bf16[32,16,256]{2,1,0:T(8,128)(2,1)}), bf16[32,16,256]{2,1,0:T(8,128)(2,1)S(1)}, u32[]{:S(2)}, u32[]{:S(2)}) %all-to-all-start.2) | async-done | bytes 262176 | tf_op jit(solution)/shard_map/all_to_all | solution.py:637
  64.2 1.7 %shard_map.163 = (bf16[256,512]{1,0:T(8,128)(2,1)S(1)}, bf16[32,16,256]{2,1,0:T(8,128)(2,1)}) custom-call(bf16[32,16,256]{2,1,0:T(8,128)(2,1)S(1)} %all-to-all-done.2.arrived, bf16[64,64,128]{2,1,0:T(8,128)(2,1)S(1)} %copy-done, bf16[256,512]{1,0:T(8,128)(2,1)S(1)} %copy-done.6, bf16[512,256]{1,0:T(8,128)(2,1)S(1)} %copy-done.5), custom_call_target="tpu_custom_call" | custom-call | flops 100000000 | bytes 1048576 | tf_op jit(solution)/shard_map/pallas_call | solution.py:710
  65.8 3.4 %all-to-all-start.3 = ((bf16[32,16,256]{2,1,0:T(8,128)(2,1)}), bf16[32,16,256]{2,1,0:T(8,128)(2,1)S(1)}, u32[]{:S(2)}, u32[]{:S(2)}) async-start(bf16[32,16,256]{2,1,0:T(8,128)(2,1)} %get-tuple-element.18), calls=%async_computation.3 | async-start | bytes 524288 | tf_op jit(solution)/shard_map/all_to_all | solution.py:637
  69.3 2.1 %shard_map.165 = f32[64,64,128]{2,1,0:T(8,128)} custom-call(bf16[256,256]{1,0:T(8,128)(2,1)S(1)} %get-tuple-element.20.spec_in, bf16[256,512]{1,0:T(8,128)(2,1)S(1)} %get-tuple-element.21.pairs), custom_call_target="tpu_custom_call" | custom-call | flops 100000000 | bytes 2097152 | tf_op jit(solution)/shard_map/pallas_call | solution.py:718
  71.3 8.5 %all-to-all-done.3.arrived = bf16[32,16,256]{2,1,0:T(8,128)(2,1)S(1)} async-done(((bf16[32,16,256]{2,1,0:T(8,128)(2,1)}), bf16[32,16,256]{2,1,0:T(8,128)(2,1)S(1)}, u32[]{:S(2)}, u32[]{:S(2)}) %all-to-all-start.3) | async-done | bytes 262176 | tf_op jit(solution)/shard_map/all_to_all | solution.py:637
  79.9 5.6 %shard_map.164 = bf16[4,16,8,48,128]{4,3,2,1,0:T(8,128)(2,1)} custom-call(bf16[32,16,256]{2,1,0:T(8,128)(2,1)S(1)} %all-to-all-done.3.arrived, bf16[4,16,8,48,128]{4,3,2,1,0:T(8,128)(2,1)} %bitcast.9, f32[256,128]{1,0:T(8,128)S(1)} %copy-done.3, bf16[768,256]{1,0:T(8,128)(2,1)S(1)} %copy-done.1), custom_call_target="tpu_custom_call" | custom-call | flops 1610612736 | bytes 12582912 | tf_op jit(solution)/shard_map/pallas_call | solution.py:724
  (9 shorter events, 0.0 us)
Async XLA Ops:
  0.6 12.6 %copy-start.9 = (bf16[64,64]{1,0:T(8,128)(2,1)S(1)}, bf16[64,64]{1,0:T(8,128)(2,1)}, u32[]{:S(2)}) copy-start(bf16[64,64]{1,0:T(8,128)(2,1)} %b.1) | copy-start | bytes 24580
  0.6 12.6 %copy-start.12 = (f32[64]{0:T(128)S(1)}, f32[64]{0:T(128)}, u32[]{:S(2)}) copy-start(f32[64]{0:T(128)} %offsets.1) | copy-start | bytes 772
  5.9 17.9 %all-to-all-start = ((bf16[32,16,256]{2,1,0:T(8,128)(2,1)}), bf16[32,16,256]{2,1,0:T(8,128)(2,1)S(1)}, u32[]{:S(2)}, u32[]{:S(2)}) async-start(bf16[32,16,256]{2,1,0:T(8,128)(2,1)} %shard_map.158), calls=%async_computation | async-start | bytes 524288 | tf_op jit(solution)/shard_map/all_to_all | solution.py:637
  13.3 10.6 %copy-start = (bf16[64,64,128]{2,1,0:T(8,128)(2,1)S(1)}, bf16[64,64,128]{2,1,0:T(8,128)(2,1)}, u32[]{:S(2)}) copy-start(bf16[64,64,128]{2,1,0:T(8,128)(2,1)} %weights.3) | copy-start | bytes 3145732
  13.3 10.6 %copy-start.7 = (bf16[512,256]{1,0:T(8,128)(2,1)S(1)}, bf16[512,256]{1,0:T(8,128)(2,1)}, u32[]{:S(2)}) copy-start(bf16[512,256]{1,0:T(8,128)(2,1)} %constant.23.clone.line_back) | copy-start | bytes 786436
  13.3 10.6 %copy-start.8 = (bf16[256,512]{1,0:T(8,128)(2,1)S(1)}, bf16[256,512]{1,0:T(8,128)(2,1)}, u32[]{:S(2)}) copy-start(bf16[256,512]{1,0:T(8,128)(2,1)} %constant.22.clone.line) | copy-start | bytes 786436
  13.3 25.6 %copy-start.1 = (bf16[768,256]{1,0:T(8,128)(2,1)S(1)}, bf16[768,256]{1,0:T(8,128)(2,1)}, u32[]{:S(2)}) copy-start(bf16[768,256]{1,0:T(8,128)(2,1)} %constant.25.clone.ytab_back) | copy-start | bytes 1179652
  13.3 25.6 %copy-start.2 = (bf16[256,768]{1,0:T(8,128)(2,1)S(1)}, bf16[256,768]{1,0:T(8,128)(2,1)}, u32[]{:S(2)}) copy-start(bf16[256,768]{1,0:T(8,128)(2,1)} %constant.21.clone.ytab_far.ytab) | copy-start | bytes 1179652
  13.3 25.6 %copy-start.3 = (f32[256,128]{1,0:T(8,128)S(1)}, f32[256,128]{1,0:T(8,128)}, u32[]{:S(2)}) copy-start(f32[256,128]{1,0:T(8,128)} %constant.24.clone.base_back) | copy-start | bytes 393220
  13.3 25.6 %copy-start.4 = (f32[128,256]{1,0:T(8,128)S(1)}, f32[128,256]{1,0:T(8,128)}, u32[]{:S(2)}) copy-start(f32[128,256]{1,0:T(8,128)} %constant.20.clone.base_far.base) | copy-start | bytes 393220
  13.4 25.6 %copy-start.10 = (f32[1,512]{1,0:T(1,128)S(1)}, f32[1,512]{1,0:T(1,128)}, u32[]{:S(2)}) copy-start(f32[1,512]{1,0:T(1,128)} %constant.27.clone.scale_back) | copy-start | bytes 6148
  13.4 25.6 %copy-start.11 = (f32[1,512]{1,0:T(1,128)S(1)}, f32[1,512]{1,0:T(1,128)}, u32[]{:S(2)}) copy-start(f32[1,512]{1,0:T(1,128)} %constant.26.clone.scale) | copy-start | bytes 6148
  50.9 13.2 %all-to-all-start.2 = ((bf16[32,16,256]{2,1,0:T(8,128)(2,1)}), bf16[32,16,256]{2,1,0:T(8,128)(2,1)S(1)}, u32[]{:S(2)}, u32[]{:S(2)}) async-start(bf16[32,16,256]{2,1,0:T(8,128)(2,1)} %get-tuple-element.15), calls=%async_computation.2 | async-start | bytes 524288 | tf_op jit(solution)/shard_map/all_to_all | solution.py:637
  53.5 10.6 %copy-start.5 = (bf16[512,256]{1,0:T(8,128)(2,1)S(1)}, bf16[512,256]{1,0:T(8,128)(2,1)}, u32[]{:S(2)}) copy-start(bf16[512,256]{1,0:T(8,128)(2,1)} %constant.29.clone.line_back) | copy-start | bytes 786436
  53.6 10.6 %copy-start.6 = (bf16[256,512]{1,0:T(8,128)(2,1)S(1)}, bf16[256,512]{1,0:T(8,128)(2,1)}, u32[]{:S(2)}) copy-start(bf16[256,512]{1,0:T(8,128)(2,1)} %constant.28.clone.line) | copy-start | bytes 786436
  65.8 14.0 %all-to-all-start.3 = ((bf16[32,16,256]{2,1,0:T(8,128)(2,1)}), bf16[32,16,256]{2,1,0:T(8,128)(2,1)S(1)}, u32[]{:S(2)}, u32[]{:S(2)}) async-start(bf16[32,16,256]{2,1,0:T(8,128)(2,1)} %get-tuple-element.18), calls=%async_computation.3 | async-start | bytes 524288 | tf_op jit(solution)/shard_map/all_to_all | solution.py:637
